TPU v7x, 256 devices: a whole 4x4x8 slice. The times are simulated.
256 devices in a mesh: seq: 64 (over y, x_hi, z), head: 4 (over x_lo, core).
Axes of the slice: x: 4 (x_hi: 2, x_lo: 2; x = x_hi * 2 + x_lo), y: 4, z: 8, core: 2. Of those that a mesh axis runs over, the one named last changes fastest.
Arguments:
- patches: bfloat16 [8192, 1280], P('seq'), may hold values from -6 to 6
- gain: float32 [1280], replicated, may hold values from 0.25 to 1.75
- w_qkv: bfloat16 [1280, 3, 1280], P(None, None, 'head'), may hold values from -0.15625 to 0.15625
- w_out: bfloat16 [1280, 1280], P('head'), may hold values from -0.3125 to 0.3125
- image_ids: int32 [8192], P('seq'), may hold values from 0 to 63, never falling along the last dimension, each value on 1 to 384 neighbouring positions
- cotangent: bfloat16 [8192, 1280], P('seq', 'head'), may hold values from -6 to 6
Outputs:
- attn_out: bfloat16 [8192, 1280], P('seq', 'head')
- grad_patches: bfloat16 [8192, 1280], P('seq', 'head')
- grad_w_qkv: float32 [1280, 3, 1280], P('seq', None, 'head')
- grad_w_out: float32 [1280, 1280], P('head', 'seq')
- grad_gain: float32 [1280], P('head')
Inputs may be any that keep to these rules, and one draw needn't show every extreme that they name: image_ids never fall along the patches; each image holds 1 to 384 patches, and one holds exactly 384.
All inputs are finite; a program needn't handle non-finite values.
Results may differ from a plain program's by a relative error of at most 0.017.
Values may be sent and summed in bfloat16 or wider, within the bound.
No kernel may reach another device: no remote copies, remote signals or barrier semaphores. Data moves between devices by JAX's collectives and lax.ppermute only.
A program may use at most 64 MiB of HBM per device.

v0:
```python
import jax
import jax.numpy as jnp
from jax import lax
from jax.experimental import pallas as pl
from jax.experimental.pallas import tpu as pltpu
from jax.sharding import Mesh, PartitionSpec as P

D = 1280
HD = 80
T = 128
HL = 4
W = HL * HD
REACH = 3
NB = 2 * REACH + 1
IDROWS = 16
SCALE = HD ** (-0.5)
LOG2E = 1.4426950408889634
SEQ = ("y", "xh", "z")
HEAD = ("xl", "c")
F32 = jnp.float32
BF16 = jnp.bfloat16
GROUPS = ((0, 2, 0, 5), (2, 4, 0, 7), (4, 6, 1, 7), (6, 7, 3, 7))
OWN = REACH


def attention_kernel(*refs):
    blocks = refs[:NB]
    out, kn, vn, es, ds, idk = refs[NB:]
    ids = [b[4 * W : 4 * W + 1, :].astype(F32) for b in blocks]
    for c in range(NB):
        idk[c * T : (c + 1) * T, :] = jnp.transpose(jnp.broadcast_to(ids[c], (2 * T, T)))

    def one_head(h, carry):
        def rows(b, j):
            return blocks[b][pl.ds(pl.multiple_of(j * W + h * HD, 16), HD), :]

        for c in range(NB):
            kn[c * T : (c + 1) * T, :] = jnp.transpose(rows(c, 1))
            vn[c * T : (c + 1) * T, :] = jnp.transpose(rows(c, 2))
        gq = jnp.zeros((HD, T), F32)
        ctx = jnp.zeros((HD, T), F32)
        gk = jnp.zeros((HD, T), F32)
        gv = jnp.zeros((HD, T), F32)
        for qa, qb, ka, kb in GROUPS:
            n = (qb - qa) * T
            qt = jnp.concatenate([rows(b, 0) for b in range(qa, qb)], axis=1)
            dt = jnp.concatenate([rows(b, 3) for b in range(qa, qb)], axis=1)
            idq = jnp.concatenate([ids[b] for b in range(qa, qb)], axis=1)
            esum = jnp.zeros((1, n), F32)
            dsum = jnp.zeros((1, n), F32)
            for c in range(ka, kb):
                kr = slice(c * T, (c + 1) * T)
                s = jnp.dot(kn[kr, :], qt, preferred_element_type=F32)
                dp = jnp.dot(vn[kr, :], dt, preferred_element_type=F32)
                same = idk[kr, :n] == idq
                e = jnp.exp2(jnp.where(same, s * (SCALE * LOG2E), -1e30))
                es[kr, :n] = e
                ds[kr, :n] = dp
                esum = esum + jnp.sum(e, axis=0, keepdims=True)
                dsum = dsum + jnp.sum(e * dp, axis=0, keepdims=True)
            r = 1.0 / jnp.maximum(esum, 1e-37)
            delta = dsum * r
            own = slice(OWN * T, (OWN + 1) * T)
            p = es[own, :n] * r
            dsc = (p * (ds[own, :n] - delta)).astype(BF16)
            lanes = (((1,), (1,)), ((), ()))
            gk = gk + lax.dot_general(qt, dsc, lanes, preferred_element_type=F32)
            gv = gv + lax.dot_general(dt, p.astype(BF16), lanes, preferred_element_type=F32)
            if qa <= OWN < qb:
                o = (OWN - qa) * T
                ro = r[:, o : o + T]
                do = delta[:, o : o + T]
                for c in range(ka, kb):
                    kr = slice(c * T, (c + 1) * T)
                    pc = es[kr, o : o + T] * ro
                    dc = (pc * (ds[kr, o : o + T] - do)).astype(BF16)
                    gq = gq + jnp.dot(rows(c, 1), dc, preferred_element_type=F32)
                    ctx = ctx + jnp.dot(rows(c, 2), pc.astype(BF16), preferred_element_type=F32)
        for j, val in enumerate((gq * SCALE, gk * SCALE, gv, ctx)):
            out[pl.ds(pl.multiple_of(j * W + h * HD, 16), HD), :] = val.astype(BF16)
        return carry

    lax.fori_loop(0, HL, one_head, 0)


def attention(blocks):
    return pl.pallas_call(
        attention_kernel,
        out_shape=jax.ShapeDtypeStruct((4 * W, T), BF16),
        in_specs=[pl.BlockSpec(memory_space=pltpu.VMEM)] * NB,
        out_specs=pl.BlockSpec(memory_space=pltpu.VMEM),
        scratch_shapes=[
            pltpu.VMEM((NB * T, HD), BF16),
            pltpu.VMEM((NB * T, HD), BF16),
            pltpu.VMEM((NB * T, 2 * T), F32),
            pltpu.VMEM((NB * T, 2 * T), F32),
            pltpu.VMEM((NB * T, 2 * T), F32),
        ],
        compiler_params=pltpu.CompilerParams(vmem_limit_bytes=32 * 1024 * 1024),
        name="attention",
    )(*blocks)


def vmem(n):
    return [pl.BlockSpec(memory_space=pltpu.VMEM)] * n


def call(kernel, name, outs, scratch, scalars, *args):
    single = not isinstance(outs, (list, tuple))
    result = pl.pallas_call(
        kernel,
        out_shape=outs,
        in_specs=[pl.BlockSpec(memory_space=pltpu.SMEM)] * len(scalars) + vmem(len(args)),
        out_specs=pl.BlockSpec(memory_space=pltpu.VMEM) if single else vmem(len(outs)),
        scratch_shapes=scratch,
        compiler_params=pltpu.CompilerParams(vmem_limit_bytes=32 * 1024 * 1024),
        name=name,
    )(*scalars, *args)
    return result


def shape(dims, dtype=BF16):
    return jax.ShapeDtypeStruct(dims, dtype)


def project_kernel(head, patches, gain, w, proj, normed, x_own, scale_own, inv_out, xt):
    xt[...] = jnp.transpose(patches[...])
    x = xt[...].astype(F32)
    inv = lax.rsqrt(jnp.sum(x * x, axis=0, keepdims=True) * (1.0 / D) + 1e-06)
    g = jnp.transpose(jnp.broadcast_to(gain[...], (T, D)))
    scale = inv * g
    normed[...] = (x * inv * g).astype(BF16)
    proj[...] = jnp.dot(w[...], normed[...], preferred_element_type=F32).astype(BF16)
    inv_out[...] = jnp.broadcast_to(inv, (8, T))
    for j in range(4):
        @pl.when(head[0] == j)
        def _():
            x_own[...] = xt[j * W : (j + 1) * W, :]
            scale_own[...] = scale[j * W : (j + 1) * W, :]


def payload_kernel(head, here, c0, c1, c2, c3, w_out, proj, normed, ids, own, s0, s1, s2, s3, cot):
    for k, piece in enumerate((c0, c1, c2, c3)):
        cot[pl.ds(pl.multiple_of(jnp.bitwise_xor(head[0], k) * W, W), W), :] = piece[...]
    own[: 3 * W, :] = proj[...]
    own[3 * W : 4 * W, :] = jnp.dot(w_out[...], cot[...], preferred_element_type=F32).astype(BF16)
    own[4 * W :, :] = jnp.broadcast_to((ids[...] + 1).astype(F32), (IDROWS, T)).astype(BF16)
    for by, out in enumerate((s0, s1, s2, s3)):
        at = pl.ds(pl.multiple_of(lax.rem(here[0] + by, 4) * W, W), W)
        out[:W, :] = normed[at, :]
        out[W:, :] = cot[at, :]


def pieces_kernel(grads, own, w, w_out, out):
    total = jnp.sum(grads[: 3 * W, :].astype(F32) * own[: 3 * W, :].astype(F32), axis=0, keepdims=True)
    hi = total.astype(BF16).astype(F32)
    row = lax.broadcasted_iota(jnp.int32, (IDROWS, T), 0)
    tail = jnp.where(row == 0, hi, jnp.where(row == 1, total - hi, 0.0)).astype(BF16)
    g = jnp.transpose(grads[...])
    d_part = jnp.dot(g[:, : 3 * W], w[...], preferred_element_type=F32)
    out_part = jnp.dot(g[:, 3 * W :], w_out[...], preferred_element_type=F32)
    d_part = jnp.transpose(d_part.astype(BF16))
    out_part = jnp.transpose(out_part.astype(BF16))
    for j in range(4):
        out[j, :W, :] = out_part[j * W : (j + 1) * W, :]
        out[j, W : 2 * W, :] = d_part[j * W : (j + 1) * W, :]
        out[j, 2 * W :, :] = tail


def rows_kernel(got, x_own, scale_own, inv, attn_out, grad_patches, gg):
    total = got[0].astype(F32) + got[1].astype(F32) + got[2].astype(F32) + got[3].astype(F32)
    attn_out[...] = total[:W, :].astype(BF16)
    d_own = total[W : 2 * W, :]
    x = x_own[...].astype(F32)
    i = inv[0:1, :]
    row_total = total[2 * W : 2 * W + 1, :] + total[2 * W + 1 : 2 * W + 2, :]
    grad_patches[...] = (scale_own[...] * d_own - x * (i * i * row_total * (1.0 / D))).astype(BF16)
    part = jnp.transpose(d_own * x * i)
    part = jnp.sum(part, axis=0, keepdims=True)
    part = jnp.concatenate([part, jnp.zeros((1, 64), F32)], axis=1)
    row = lax.broadcasted_iota(jnp.int32, (8, T), 0)
    gg[...] = jnp.where(
        row == 0, part[:, :T], jnp.where(row == 1, part[:, T : 2 * T], jnp.where(row == 2, part[:, 2 * T :], 0.0))
    )


def weights_kernel(*refs):
    ss, gs, ggs, out, term = refs[0:4], refs[4:8], refs[8:12], refs[12], refs[13]
    lanes = (((1,), (1,)), ((), ()))
    gg = ggs[0][...] + ggs[1][...] + ggs[2][...] + ggs[3][...]
    hi = gg.astype(BF16).astype(F32)
    tail = hi + pltpu.roll(gg - hi, 4, 0)
    n = jnp.concatenate([s[:W, :] for s in ss], axis=1)
    c = jnp.concatenate([s[W:, :] for s in ss], axis=1)
    g = jnp.concatenate([r[: 3 * W, :] for r in gs], axis=1)
    x = jnp.concatenate([r[3 * W :, :] for r in gs], axis=1)
    term[:, : 3 * W] = lax.dot_general(n, g, lanes, preferred_element_type=F32)
    term[:, 3 * W :] = lax.dot_general(c, x, lanes, preferred_element_type=F32)
    for i in range(16):
        rows = [term[20 * i : 20 * i + 20, T * l : T * (l + 1)] for l in range(10)]
        out[i] = jnp.concatenate(rows + [tail], axis=0).astype(BF16)


def sums_kernel(got, qkv, out, gg):
    total = got[0].astype(F32)
    for i in range(1, 16):
        total = total + got[i].astype(F32)
    full = jnp.concatenate([total[20 * l : 20 * l + 20, :] for l in range(10)], axis=1)
    for j in range(3):
        qkv[j] = full[:, j * W : (j + 1) * W]
    out[...] = full[:, 3 * W :]
    tail = total[200:208, :]
    tail = tail + pltpu.roll(tail, 4, 0)
    gg[...] = jnp.concatenate([tail[0:1, :], tail[1:2, :], tail[2:3, :64]], axis=1)


def along_seq(x, by):
    return lax.ppermute(x, SEQ, [(i, i + by) for i in range(64) if 0 <= i + by < 64])


def along_y(x, by):
    return lax.ppermute(x, "y", [(i, (i + by) % 4) for i in range(4)])


def along_head(x, by):
    return lax.ppermute(x, HEAD, [(i, i ^ by) for i in range(4)])


def body(patches, gain, w_qkv, w_out, image_ids, cotangent):
    here = lax.axis_index("y").astype(jnp.int32).reshape(1)
    head = lax.axis_index(HEAD).astype(jnp.int32).reshape(1)
    cot = cotangent.T
    cots = [along_head(cot, k) if k else cot for k in range(4)]
    w = w_qkv.transpose(1, 2, 0).reshape(3 * W, D)
    proj, normed, x_own, scale_own, inv = call(
        project_kernel,
        "project",
        [shape((3 * W, T)), shape((D, T)), shape((W, T)), shape((W, T), F32), shape((8, T), F32)],
        [pltpu.VMEM((D, T), BF16)],
        [head],
        patches,
        gain.reshape(1, D),
        w,
    )
    own, *slices = call(
        payload_kernel,
        "payload",
        [shape((4 * W + IDROWS, T))] + [shape((2 * W, T))] * 4,
        [pltpu.VMEM((D, T), BF16)],
        [head, here],
        *cots,
        w_out,
        proj,
        normed,
        image_ids.reshape(1, T),
    )
    before, after = [], []
    up = down = own
    for _ in range(REACH):
        up, down = along_seq(up, 1), along_seq(down, -1)
        before.append(up)
        after.append(down)
    slices = [along_y(s, by) if by else s for by, s in enumerate(slices)]
    grads = attention(before[::-1] + [own] + after)
    all_grads = [along_y(grads, by) if by else grads for by in range(4)]
    pieces = call(pieces_kernel, "pieces", shape((4, 2 * W + IDROWS, T)), [], [], grads, own, w, w_out)
    got = lax.all_to_all(pieces, HEAD, 0, 0, tiled=True)
    attn_out, grad_patches, gg = call(
        rows_kernel,
        "rows",
        [shape((W, T)), shape((W, T)), shape((8, T), F32)],
        [],
        [],
        got,
        x_own,
        scale_own,
        inv,
    )
    all_gg = [along_y(gg, by) if by else gg for by in range(4)]
    terms = call(
        weights_kernel,
        "weights",
        shape((16, 208, T)),
        [pltpu.VMEM((W, 4 * W), F32)],
        [],
        *slices,
        *all_grads,
        *all_gg,
    )
    terms = lax.all_to_all(terms, ("xh", "z"), 0, 0, tiled=True)
    grad_w_qkv, grad_w_out, grad_gain = call(
        sums_kernel,
        "sums",
        [shape((3, 20, W), F32), shape((20, W), F32), shape((1, W), F32)],
        [],
        [],
        terms,
    )
    return (attn_out.T, grad_patches.T, grad_w_qkv.transpose(1, 0, 2), grad_w_out.T, grad_gain.reshape(W))


def solution(mesh):
    fine = Mesh(mesh.devices.reshape(4, 2, 8, 2, 2), SEQ + HEAD)
    in_specs = (
        P(SEQ, None),
        P(),
        P(None, None, HEAD),
        P(HEAD, None),
        P(SEQ),
        P(SEQ, HEAD),
    )
    out_specs = (
        P(SEQ, HEAD),
        P(SEQ, HEAD),
        P(SEQ, None, HEAD),
        P(HEAD, SEQ),
        P(HEAD),
    )
    return jax.shard_map(body, mesh=fine, in_specs=in_specs, out_specs=out_specs, check_vma=False)
```

profile of v0, /device:TPU:32, one launch (start us, length us, event | category | flops | bytes accessed | tf_op | source)
XLA Modules:
  0.0 136.5 jit_solution(7650903907759078039)
XLA Ops:
  0.7 1.6 %collective-permute-start.1 = (bf16[320,128]{1,0:T(8,128)(2,1)}, bf16[320,128]{1,0:T(8,128)(2,1)S(1)}, u32[]{:S(2)}, u32[]{:S(2)}) collective-permute-start(bf16[320,128]{1,0:T(8,128)(2,1)} %bitcast.14), channel_id=1, source_target_pairs={{0,2},{1,3},{2,0},{3,1},{4,6},{5,7},{6,4},{7,5},{8,10},{9,11},{10,... | collective-permute-start | bytes 245768 | tf_op jit(solution)/shard_map/ppermute | solution.py:226
  3.3 1.7 %copy-done = bf16[1280,3,320]{0,2,1:T(8,128)(2,1)S(1)} copy-done((bf16[1280,3,320]{0,2,1:T(8,128)(2,1)S(1)}, bf16[1280,3,320]{0,2,1:T(8,128)(2,1)}, u32[]{:S(2)}) %copy-start) | copy-done | bytes 2457624
  5.0 1.0 copy-done.3
  6.0 1.2 project.1
  7.7 4.0 %collective-permute-start.3 = (bf16[1296,128]{1,0:T(8,128)(2,1)S(1)}, bf16[1296,128]{1,0:T(8,128)(2,1)S(1)}, u32[]{:S(2)}, u32[]{:S(2)}) collective-permute-start(bf16[1296,128]{1,0:T(8,128)(2,1)S(1)} %get-tuple-element.23.refs_3_.own), channel_id=1, source_target_pairs={{0,4},{4,8},{8,12},{12,16},{16,20},{20,24},{24,28},{28,32},{32,36}... | collective-permute-start | bytes 995336 | tf_op jit(solution)/shard_map/ppermute | solution.py:218
  11.7 2.0 %collective-permute-start.6 = (bf16[1296,128]{1,0:T(8,128)(2,1)S(1)}, bf16[1296,128]{1,0:T(8,128)(2,1)S(1)}, u32[]{:S(2)}, u32[]{:S(2)}) collective-permute-start(bf16[1296,128]{1,0:T(8,128)(2,1)S(1)} %get-tuple-element.23.refs_3_.own), channel_id=1, source_target_pairs={{4,0},{8,4},{12,8},{16,12},{20,16},{24,20},{28,24},{32,28},{36,32}... | collective-permute-start | bytes 995336 | tf_op jit(solution)/shard_map/ppermute | solution.py:218
  13.7 6.0 %collective-permute-done.3.refs_2_ = bf16[1296,128]{1,0:T(8,128)(2,1)S(1)} collective-permute-done((bf16[1296,128]{1,0:T(8,128)(2,1)S(1)}, bf16[1296,128]{1,0:T(8,128)(2,1)S(1)}, u32[]{:S(2)}, u32[]{:S(2)}) %collective-permute-start.3) | collective-permute-done | bytes 331808 | tf_op jit(solution)/shard_map/ppermute | solution.py:218
  19.7 3.8 %collective-permute-start.4 = (bf16[1296,128]{1,0:T(8,128)(2,1)S(1)}, bf16[1296,128]{1,0:T(8,128)(2,1)S(1)}, u32[]{:S(2)}, u32[]{:S(2)}) collective-permute-start(bf16[1296,128]{1,0:T(8,128)(2,1)S(1)} %collective-permute-done.3.refs_2_), channel_id=1, source_target_pairs={{0,4},{4,8},{8,12},{12,16},{16,20},{20,24},{24,28},{28,32},{32,36}... | collective-permute-start | bytes 995336 | tf_op jit(solution)/shard_map/ppermute | solution.py:218
  23.6 2.0 %collective-permute-start.7 = (bf16[1296,128]{1,0:T(8,128)(2,1)S(1)}, bf16[1296,128]{1,0:T(8,128)(2,1)S(1)}, u32[]{:S(2)}, u32[]{:S(2)}) collective-permute-start(bf16[1296,128]{1,0:T(8,128)(2,1)S(1)} %collective-permute-done.6.refs_4_), channel_id=1, source_target_pairs={{4,0},{8,4},{12,8},{16,12},{20,16},{24,20},{28,24},{32,28},{36,32}... | collective-permute-start | bytes 995336 | tf_op jit(solution)/shard_map/ppermute | solution.py:218
  25.6 5.2 %collective-permute-done.4.refs_1_ = bf16[1296,128]{1,0:T(8,128)(2,1)S(1)} collective-permute-done((bf16[1296,128]{1,0:T(8,128)(2,1)S(1)}, bf16[1296,128]{1,0:T(8,128)(2,1)S(1)}, u32[]{:S(2)}, u32[]{:S(2)}) %collective-permute-start.4) | collective-permute-done | bytes 331808 | tf_op jit(solution)/shard_map/ppermute | solution.py:218
  30.8 3.9 %collective-permute-start.5 = (bf16[1296,128]{1,0:T(8,128)(2,1)S(1)}, bf16[1296,128]{1,0:T(8,128)(2,1)S(1)}, u32[]{:S(2)}, u32[]{:S(2)}) collective-permute-start(bf16[1296,128]{1,0:T(8,128)(2,1)S(1)} %collective-permute-done.4.refs_1_), channel_id=1, source_target_pairs={{0,4},{4,8},{8,12},{12,16},{16,20},{20,24},{24,28},{28,32},{32,36}... | collective-permute-start | bytes 995336 | tf_op jit(solution)/shard_map/ppermute | solution.py:218
  34.7 1.2 collective-permute-done.7.refs_5_
  36.0 1.9 %collective-permute-start.8 = (bf16[1296,128]{1,0:T(8,128)(2,1)S(1)}, bf16[1296,128]{1,0:T(8,128)(2,1)S(1)}, u32[]{:S(2)}, u32[]{:S(2)}) collective-permute-start(bf16[1296,128]{1,0:T(8,128)(2,1)S(1)} %collective-permute-done.7.refs_5_), channel_id=1, source_target_pairs={{4,0},{8,4},{12,8},{16,12},{20,16},{24,20},{28,24},{32,28},{36,32}... | collective-permute-start | bytes 995336 | tf_op jit(solution)/shard_map/ppermute | solution.py:218
  37.9 3.1 %collective-permute-done.5.refs_0_ = bf16[1296,128]{1,0:T(8,128)(2,1)S(1)} collective-permute-done((bf16[1296,128]{1,0:T(8,128)(2,1)S(1)}, bf16[1296,128]{1,0:T(8,128)(2,1)S(1)}, u32[]{:S(2)}, u32[]{:S(2)}) %collective-permute-start.5) | collective-permute-done | bytes 331808 | tf_op jit(solution)/shard_map/ppermute | solution.py:218
  41.0 6.4 %collective-permute-done.8.refs_6_ = bf16[1296,128]{1,0:T(8,128)(2,1)S(1)} collective-permute-done((bf16[1296,128]{1,0:T(8,128)(2,1)S(1)}, bf16[1296,128]{1,0:T(8,128)(2,1)S(1)}, u32[]{:S(2)}, u32[]{:S(2)}) %collective-permute-start.8) | collective-permute-done | bytes 331808 | tf_op jit(solution)/shard_map/ppermute | solution.py:218
  47.4 7.2 %attention.1.grads.refs_4_ = bf16[1280,128]{1,0:T(8,128)(2,1)S(1)} custom-call(bf16[1296,128]{1,0:T(8,128)(2,1)S(1)} %collective-permute-done.5.refs_0_, bf16[1296,128]{1,0:T(8,128)(2,1)S(1)} %collective-permute-done.4.refs_1_, bf16[1296,128]{1,0:T(8,128)(2,1)S(1)} %collective-permute-done.3.refs_2_, bf16[1296,128]{1,0:T(8,128)(2,1)S(1)} %get-tuple-element.23.refs_3_.own, ...), custom_call_target="tpu_custom_call" | custom-call | tf_op jit(solution)/shard_map/attention/pallas_call | solution.py:87
  54.6 1.7 %pieces.1 = bf16[4,656,128]{2,1,0:T(8,128)(2,1)} custom-call(bf16[1280,128]{1,0:T(8,128)(2,1)S(1)} %attention.1.grads.refs_4_, bf16[1296,128]{1,0:T(8,128)(2,1)S(1)} %get-tuple-element.23.refs_3_.own, bf16[960,1280]{1,0:T(8,128)(2,1)S(1)} %bitcast.12, bf16[320,1280]{1,0:T(8,128)(2,1)S(1)} %copy-done.2), custom_call_target="tpu_custom_call" | custom-call | tf_op jit(solution)/shard_map/pieces/pallas_call | solution.py:110
  56.2 3.5 %all-to-all-start = ((bf16[4,656,128]{2,1,0:T(8,128)(2,1)}), bf16[4,656,128]{2,1,0:T(8,128)(2,1)S(1)}, u32[]{:S(2)}, u32[]{:S(2)}) async-start(bf16[4,656,128]{2,1,0:T(8,128)(2,1)} %pieces.1), calls=%async_computation | async-start | bytes 1343488 | tf_op jit(solution)/shard_map/all_to_all | solution.py:267
  59.7 8.1 %collective-permute-start.10 = (bf16[640,128]{1,0:T(8,128)(2,1)S(1)}, bf16[640,128]{1,0:T(8,128)(2,1)S(1)}, u32[]{:S(2)}, u32[]{:S(2)}) collective-permute-start(bf16[640,128]{1,0:T(8,128)(2,1)S(1)} %get-tuple-element.31), channel_id=1, source_target_pairs={{0,128},{64,192},{128,0},{192,64},{1,129},{65,193},{129,1},{193,65... | collective-permute-start | bytes 491528 | tf_op jit(solution)/shard_map/ppermute | solution.py:222
  67.8 1.0 collective-permute-start.12
  68.8 1.6 %collective-permute-start.13 = (bf16[1280,128]{1,0:T(8,128)(2,1)S(1)}, bf16[1280,128]{1,0:T(8,128)(2,1)S(1)}, u32[]{:S(2)}, u32[]{:S(2)}) collective-permute-start(bf16[1280,128]{1,0:T(8,128)(2,1)S(1)} %attention.1.grads.refs_4_), channel_id=1, source_target_pairs={{0,128},{64,192},{128,0},{192,64},{1,129},{65,193},{129,1},{193,65... | collective-permute-start | bytes 983048 | tf_op jit(solution)/shard_map/ppermute | solution.py:222
  70.4 1.1 collective-permute-start.14
  71.5 1.4 %collective-permute-start.11 = (bf16[640,128]{1,0:T(8,128)(2,1)S(1)}, bf16[640,128]{1,0:T(8,128)(2,1)S(1)}, u32[]{:S(2)}, u32[]{:S(2)}) collective-permute-start(bf16[640,128]{1,0:T(8,128)(2,1)S(1)} %get-tuple-element.32), channel_id=1, source_target_pairs={{0,192},{64,0},{128,64},{192,128},{1,193},{65,1},{129,65},{193,129... | collective-permute-start | bytes 491528 | tf_op jit(solution)/shard_map/ppermute | solution.py:222
  72.9 1.9 %collective-permute-start.9 = (bf16[640,128]{1,0:T(8,128)(2,1)S(1)}, bf16[640,128]{1,0:T(8,128)(2,1)S(1)}, u32[]{:S(2)}, u32[]{:S(2)}) collective-permute-start(bf16[640,128]{1,0:T(8,128)(2,1)S(1)} %get-tuple-element.30), channel_id=1, source_target_pairs={{0,64},{64,128},{128,192},{192,0},{1,65},{65,129},{129,193},{193,1... | collective-permute-start | bytes 491528 | tf_op jit(solution)/shard_map/ppermute | solution.py:222
  75.6 15.2 %collective-permute-done.11.refs_3_ = bf16[640,128]{1,0:T(8,128)(2,1)S(1)} collective-permute-done((bf16[640,128]{1,0:T(8,128)(2,1)S(1)}, bf16[640,128]{1,0:T(8,128)(2,1)S(1)}, u32[]{:S(2)}, u32[]{:S(2)}) %collective-permute-start.11) | collective-permute-done | bytes 163872 | tf_op jit(solution)/shard_map/ppermute | solution.py:222
  90.8 0.9 collective-permute-start.15
  91.7 3.2 %collective-permute-start.16 = (f32[8,128]{1,0:T(8,128)S(1)}, f32[8,128]{1,0:T(8,128)S(1)}, u32[]{:S(2)}, u32[]{:S(2)}) collective-permute-start(f32[8,128]{1,0:T(8,128)S(1)} %get-tuple-element.33.refs_8_), channel_id=1, source_target_pairs={{0,128},{64,192},{128,0},{192,64},{1,129},{65,193},{129,1},{193,65... | collective-permute-start | bytes 12296 | tf_op jit(solution)/shard_map/ppermute | solution.py:222
  95.7 1.2 collective-permute-done.16.refs_10_
  96.9 1.7 %collective-permute-done.17.refs_11_ = f32[8,128]{1,0:T(8,128)S(1)} collective-permute-done((f32[8,128]{1,0:T(8,128)S(1)}, f32[8,128]{1,0:T(8,128)S(1)}, u32[]{:S(2)}, u32[]{:S(2)}) %collective-permute-start.17) | collective-permute-done | bytes 4128 | tf_op jit(solution)/shard_map/ppermute | solution.py:222
  98.5 0.9 weights.1
  99.4 35.7 %all_to_all.10.got = bf16[16,208,128]{2,1,0:T(8,128)(2,1)S(1)} all-to-all(bf16[16,208,128]{2,1,0:T(8,128)(2,1)S(1)} %weights.1), channel_id=1, replica_groups=mesh['y'=4,'xh'=2,'z'=8,'xl'=2,'c'=2] {'xh','z'}, dimensions={0} | all-to-all | bytes 1703936 | tf_op jit(solution)/shard_map/all_to_all | solution.py:290
  135.1 0.8 sums.1
  (28 shorter events, 3.7 us)
Async XLA Ops:
  0.6 6.6 %copy-start.5 = (s32[128]{0:T(128)S(1)}, s32[128]{0:T(128)}, u32[]{:S(2)}) copy-start(s32[128]{0:T(128)} %param.10) | copy-start | bytes 1540
  0.6 6.5 %collective-permute-start = (bf16[320,128]{1,0:T(8,128)(2,1)}, bf16[320,128]{1,0:T(8,128)(2,1)S(1)}, u32[]{:S(2)}, u32[]{:S(2)}) collective-permute-start(bf16[320,128]{1,0:T(8,128)(2,1)} %bitcast.13), channel_id=1, source_target_pairs={{0,1},{1,0},{2,3},{3,2},{4,5},{5,4},{6,7},{7,6},{8,9},{9,8},{10,11... | collective-permute-start | bytes 245768 | tf_op jit(solution)/shard_map/ppermute | solution.py:226
  0.7 6.4 %collective-permute-start.1 = (bf16[320,128]{1,0:T(8,128)(2,1)}, bf16[320,128]{1,0:T(8,128)(2,1)S(1)}, u32[]{:S(2)}, u32[]{:S(2)}) collective-permute-start(bf16[320,128]{1,0:T(8,128)(2,1)} %bitcast.14), channel_id=1, source_target_pairs={{0,2},{1,3},{2,0},{3,1},{4,6},{5,7},{6,4},{7,5},{8,10},{9,11},{10,... | collective-permute-start | bytes 245768 | tf_op jit(solution)/shard_map/ppermute | solution.py:226
  2.3 4.9 %collective-permute-start.2 = (bf16[320,128]{1,0:T(8,128)(2,1)}, bf16[320,128]{1,0:T(8,128)(2,1)S(1)}, u32[]{:S(2)}, u32[]{:S(2)}) collective-permute-start(bf16[320,128]{1,0:T(8,128)(2,1)} %bitcast.15), channel_id=1, source_target_pairs={{0,3},{1,2},{2,1},{3,0},{4,7},{5,6},{6,5},{7,4},{8,11},{9,10},{10,... | collective-permute-start | bytes 245768 | tf_op jit(solution)/shard_map/ppermute | solution.py:226
  3.3 1.7 %copy-start = (bf16[1280,3,320]{0,2,1:T(8,128)(2,1)S(1)}, bf16[1280,3,320]{0,2,1:T(8,128)(2,1)}, u32[]{:S(2)}) copy-start(bf16[1280,3,320]{0,2,1:T(8,128)(2,1)} %param.8) | copy-start | bytes 7372804
  5.0 1.0 copy-start.3
  6.0 1.3 copy-start.2
  6.0 1.3 copy-start.4
  7.1 47.4 %copy-start.1 = (bf16[1280,3,320]{0,2,1:T(8,128)(2,1)S(1)}, bf16[1280,3,320]{0,2,1:T(8,128)(2,1)}, u32[]{:S(2)}) copy-start(bf16[1280,3,320]{0,2,1:T(8,128)(2,1)} %param.8) | copy-start | bytes 7372804
  7.7 12.0 %collective-permute-start.3 = (bf16[1296,128]{1,0:T(8,128)(2,1)S(1)}, bf16[1296,128]{1,0:T(8,128)(2,1)S(1)}, u32[]{:S(2)}, u32[]{:S(2)}) collective-permute-start(bf16[1296,128]{1,0:T(8,128)(2,1)S(1)} %get-tuple-element.23.refs_3_.own), channel_id=1, source_target_pairs={{0,4},{4,8},{8,12},{12,16},{16,20},{20,24},{24,28},{28,32},{32,36}... | collective-permute-start | bytes 995336 | tf_op jit(solution)/shard_map/ppermute | solution.py:218
  11.7 11.9 %collective-permute-start.6 = (bf16[1296,128]{1,0:T(8,128)(2,1)S(1)}, bf16[1296,128]{1,0:T(8,128)(2,1)S(1)}, u32[]{:S(2)}, u32[]{:S(2)}) collective-permute-start(bf16[1296,128]{1,0:T(8,128)(2,1)S(1)} %get-tuple-element.23.refs_3_.own), channel_id=1, source_target_pairs={{4,0},{8,4},{12,8},{16,12},{20,16},{24,20},{28,24},{32,28},{36,32}... | collective-permute-start | bytes 995336 | tf_op jit(solution)/shard_map/ppermute | solution.py:218
  19.7 11.1 %collective-permute-start.4 = (bf16[1296,128]{1,0:T(8,128)(2,1)S(1)}, bf16[1296,128]{1,0:T(8,128)(2,1)S(1)}, u32[]{:S(2)}, u32[]{:S(2)}) collective-permute-start(bf16[1296,128]{1,0:T(8,128)(2,1)S(1)} %collective-permute-done.3.refs_2_), channel_id=1, source_target_pairs={{0,4},{4,8},{8,12},{12,16},{16,20},{20,24},{24,28},{28,32},{32,36}... | collective-permute-start | bytes 995336 | tf_op jit(solution)/shard_map/ppermute | solution.py:218
  23.6 12.4 %collective-permute-start.7 = (bf16[1296,128]{1,0:T(8,128)(2,1)S(1)}, bf16[1296,128]{1,0:T(8,128)(2,1)S(1)}, u32[]{:S(2)}, u32[]{:S(2)}) collective-permute-start(bf16[1296,128]{1,0:T(8,128)(2,1)S(1)} %collective-permute-done.6.refs_4_), channel_id=1, source_target_pairs={{4,0},{8,4},{12,8},{16,12},{20,16},{24,20},{28,24},{32,28},{36,32}... | collective-permute-start | bytes 995336 | tf_op jit(solution)/shard_map/ppermute | solution.py:218
  30.8 10.2 %collective-permute-start.5 = (bf16[1296,128]{1,0:T(8,128)(2,1)S(1)}, bf16[1296,128]{1,0:T(8,128)(2,1)S(1)}, u32[]{:S(2)}, u32[]{:S(2)}) collective-permute-start(bf16[1296,128]{1,0:T(8,128)(2,1)S(1)} %collective-permute-done.4.refs_1_), channel_id=1, source_target_pairs={{0,4},{4,8},{8,12},{12,16},{16,20},{20,24},{24,28},{28,32},{32,36}... | collective-permute-start | bytes 995336 | tf_op jit(solution)/shard_map/ppermute | solution.py:218
  36.0 11.4 %collective-permute-start.8 = (bf16[1296,128]{1,0:T(8,128)(2,1)S(1)}, bf16[1296,128]{1,0:T(8,128)(2,1)S(1)}, u32[]{:S(2)}, u32[]{:S(2)}) collective-permute-start(bf16[1296,128]{1,0:T(8,128)(2,1)S(1)} %collective-permute-done.7.refs_5_), channel_id=1, source_target_pairs={{4,0},{8,4},{12,8},{16,12},{20,16},{24,20},{28,24},{32,28},{36,32}... | collective-permute-start | bytes 995336 | tf_op jit(solution)/shard_map/ppermute | solution.py:218
  56.2 18.6 %all-to-all-start = ((bf16[4,656,128]{2,1,0:T(8,128)(2,1)}), bf16[4,656,128]{2,1,0:T(8,128)(2,1)S(1)}, u32[]{:S(2)}, u32[]{:S(2)}) async-start(bf16[4,656,128]{2,1,0:T(8,128)(2,1)} %pieces.1), calls=%async_computation | async-start | bytes 1343488 | tf_op jit(solution)/shard_map/all_to_all | solution.py:267
  59.7 13.1 %collective-permute-start.10 = (bf16[640,128]{1,0:T(8,128)(2,1)S(1)}, bf16[640,128]{1,0:T(8,128)(2,1)S(1)}, u32[]{:S(2)}, u32[]{:S(2)}) collective-permute-start(bf16[640,128]{1,0:T(8,128)(2,1)S(1)} %get-tuple-element.31), channel_id=1, source_target_pairs={{0,128},{64,192},{128,0},{192,64},{1,129},{65,193},{129,1},{193,65... | collective-permute-start | bytes 491528 | tf_op jit(solution)/shard_map/ppermute | solution.py:222
  67.8 27.1 %collective-permute-start.12 = (bf16[1280,128]{1,0:T(8,128)(2,1)S(1)}, bf16[1280,128]{1,0:T(8,128)(2,1)S(1)}, u32[]{:S(2)}, u32[]{:S(2)}) collective-permute-start(bf16[1280,128]{1,0:T(8,128)(2,1)S(1)} %attention.1.grads.refs_4_), channel_id=1, source_target_pairs={{0,64},{64,128},{128,192},{192,0},{1,65},{65,129},{129,193},{193,1... | collective-permute-start | bytes 983048 | tf_op jit(solution)/shard_map/ppermute | solution.py:222
  68.8 26.2 %collective-permute-start.13 = (bf16[1280,128]{1,0:T(8,128)(2,1)S(1)}, bf16[1280,128]{1,0:T(8,128)(2,1)S(1)}, u32[]{:S(2)}, u32[]{:S(2)}) collective-permute-start(bf16[1280,128]{1,0:T(8,128)(2,1)S(1)} %attention.1.grads.refs_4_), channel_id=1, source_target_pairs={{0,128},{64,192},{128,0},{192,64},{1,129},{65,193},{129,1},{193,65... | collective-permute-start | bytes 983048 | tf_op jit(solution)/shard_map/ppermute | solution.py:222
  70.4 24.7 %collective-permute-start.14 = (bf16[1280,128]{1,0:T(8,128)(2,1)S(1)}, bf16[1280,128]{1,0:T(8,128)(2,1)S(1)}, u32[]{:S(2)}, u32[]{:S(2)}) collective-permute-start(bf16[1280,128]{1,0:T(8,128)(2,1)S(1)} %attention.1.grads.refs_4_), channel_id=1, source_target_pairs={{0,192},{64,0},{128,64},{192,128},{1,193},{65,1},{129,65},{193,129... | collective-permute-start | bytes 983048 | tf_op jit(solution)/shard_map/ppermute | solution.py:222
  71.5 19.4 %collective-permute-start.11 = (bf16[640,128]{1,0:T(8,128)(2,1)S(1)}, bf16[640,128]{1,0:T(8,128)(2,1)S(1)}, u32[]{:S(2)}, u32[]{:S(2)}) collective-permute-start(bf16[640,128]{1,0:T(8,128)(2,1)S(1)} %get-tuple-element.32), channel_id=1, source_target_pairs={{0,192},{64,0},{128,64},{192,128},{1,193},{65,1},{129,65},{193,129... | collective-permute-start | bytes 491528 | tf_op jit(solution)/shard_map/ppermute | solution.py:222
  72.9 18.9 %collective-permute-start.9 = (bf16[640,128]{1,0:T(8,128)(2,1)S(1)}, bf16[640,128]{1,0:T(8,128)(2,1)S(1)}, u32[]{:S(2)}, u32[]{:S(2)}) collective-permute-start(bf16[640,128]{1,0:T(8,128)(2,1)S(1)} %get-tuple-element.30), channel_id=1, source_target_pairs={{0,64},{64,128},{128,192},{192,0},{1,65},{65,129},{129,193},{193,1... | collective-permute-start | bytes 491528 | tf_op jit(solution)/shard_map/ppermute | solution.py:222
  90.8 4.8 %collective-permute-start.15 = (f32[8,128]{1,0:T(8,128)S(1)}, f32[8,128]{1,0:T(8,128)S(1)}, u32[]{:S(2)}, u32[]{:S(2)}) collective-permute-start(f32[8,128]{1,0:T(8,128)S(1)} %get-tuple-element.33.refs_8_), channel_id=1, source_target_pairs={{0,64},{64,128},{128,192},{192,0},{1,65},{65,129},{129,193},{193,1... | collective-permute-start | bytes 12296 | tf_op jit(solution)/shard_map/ppermute | solution.py:222
  91.7 5.1 %collective-permute-start.16 = (f32[8,128]{1,0:T(8,128)S(1)}, f32[8,128]{1,0:T(8,128)S(1)}, u32[]{:S(2)}, u32[]{:S(2)}) collective-permute-start(f32[8,128]{1,0:T(8,128)S(1)} %get-tuple-element.33.refs_8_), channel_id=1, source_target_pairs={{0,128},{64,192},{128,0},{192,64},{1,129},{65,193},{129,1},{193,65... | collective-permute-start | bytes 12296 | tf_op jit(solution)/shard_map/ppermute | solution.py:222
  94.9 3.6 %collective-permute-start.17 = (f32[8,128]{1,0:T(8,128)S(1)}, f32[8,128]{1,0:T(8,128)S(1)}, u32[]{:S(2)}, u32[]{:S(2)}) collective-permute-start(f32[8,128]{1,0:T(8,128)S(1)} %get-tuple-element.33.refs_8_), channel_id=1, source_target_pairs={{0,192},{64,0},{128,64},{192,128},{1,193},{65,1},{129,65},{193,129... | collective-permute-start | bytes 12296 | tf_op jit(solution)/shard_map/ppermute | solution.py:222
where the time goes:
time: 137 us
  starting transfers between devices  42.3 us (31%)
  waiting for transfers between devices  40.8 us (30%)
  blocking collectives  35.7 us (26%)
  Pallas kernels  12.9 us (9%)
  local copies, waits for them, and re-layouts  3.38 us (2%)
    all_to_all x1, blocking collectives, body(): terms = lax.all_to_all(terms, ('xh', 'z'), 0, 0, tiled=True)  35.7 us
    ppermute x6, waiting for transfers between devices, along_seq(): lax.ppermute(x, SEQ, [(i, i + by) for i in range(64) if 0 <= i + by < 64])  22 us
    ppermute x9, starting transfers between devices, along_y(): return lax.ppermute(x, 'y', [(i, (i + by) % 4) for i in range(4)])  19.3 us
    ppermute x9, waiting for transfers between devices, along_y(): return lax.ppermute(x, 'y', [(i, (i + by) % 4) for i in range(4)])  18.7 us
    ppermute x6, starting transfers between devices, along_seq(): lax.ppermute(x, SEQ, [(i, i + by) for i in range(64) if 0 <= i + by < 64])  17.6 us
    pallas_call x1, Pallas kernels, attention(): pl.pallas_call(attention_kernel, out_shape=jax.ShapeDtypeStruct((4 * W, T...  7.21 us
    pallas_call x6, Pallas kernels, call(): pl.pallas_call(kernel, out_shape=outs, in_specs=[pl.BlockSpec(memory_spac...  5.69 us
    all_to_all x1, starting transfers between devices, body(): got = lax.all_to_all(pieces, HEAD, 0, 0, tiled=True)  3.48 us
  transfers between devices with their start and end apart: 19, of which 10 were waited for; matrix products, arithmetic and copies ran while one was open for 1% of the time, Pallas kernels for 1%

commit v1 on v0

v1 whole, which is shorter than its diff:
```python
import jax
import jax.numpy as jnp
from jax import lax
from jax.experimental import pallas as pl
from jax.experimental.pallas import tpu as pltpu
from jax.sharding import Mesh, PartitionSpec as P

D = 1280
HD = 80
T = 128
HL = 4
W = HL * HD
IDROWS = 16
R = 4 * HD + IDROWS
WIN = 10
OWN = 3
SCALE = HD ** (-0.5)
LOG2E = 1.4426950408889634
SEQ = ("y", "xh", "z")
HEAD = ("xl", "c")
F32 = jnp.float32
BF16 = jnp.bfloat16
LANES = (((1,), (1,)), ((), ()))
GROUPS = ((0, 2, 0, 5), (2, 4, 0, 7), (4, 6, 1, 9), (6, 8, 3, 10), (8, 10, 5, 10))


def call(kernel, name, outs, scratch, scalars, *args, far=0, far_outs=0, limit=12):
    single = not isinstance(outs, (list, tuple))
    vmem, hbm = pl.BlockSpec(memory_space=pltpu.VMEM), pl.BlockSpec(memory_space=pltpu.HBM)
    specs = [pl.BlockSpec(memory_space=pltpu.SMEM)] * len(scalars)
    specs += [vmem] * (len(args) - far) + [hbm] * far
    return pl.pallas_call(
        kernel,
        out_shape=outs,
        in_specs=specs,
        out_specs=vmem if single else [vmem] * (len(outs) - far_outs) + [hbm] * far_outs,
        scratch_shapes=scratch,
        compiler_params=pltpu.CompilerParams(vmem_limit_bytes=limit * 1024 * 1024),
        cost_estimate=pl.CostEstimate(flops=1000, bytes_accessed=1000, transcendentals=0),
        name=name,
    )(*scalars, *args)


def fetch(sems, *pairs):
    copies = [pltpu.make_async_copy(src, dst, sems.at[i]) for i, (src, dst) in enumerate(pairs)]
    for copy in copies:
        copy.start()
    return copies


def shape(dims, dtype=BF16):
    return jax.ShapeDtypeStruct(dims, dtype)


def times(index, size):
    return pl.ds(pl.multiple_of(index * size, size), size)


def norm_kernel(head, patches_far, gain_far, cot_far, normed, quarter, x_own, scale_own, inv_out, patches, gain, xt, scale, sems):
    copies = fetch(sems, (patches_far, patches), (gain_far, gain), (cot_far, quarter.at[W:]))
    copies[0].wait()
    copies[1].wait()
    xt[...] = jnp.transpose(patches[...])
    x = xt[...].astype(F32)
    inv = lax.rsqrt(jnp.sum(x * x, axis=0, keepdims=True) * (1.0 / D) + 1e-06)
    for l in range(10):
        rows = slice(l * T, (l + 1) * T)
        g = jnp.transpose(jnp.broadcast_to(gain[l : l + 1, :], (T, T)))
        scale[rows, :] = inv * g
        normed[rows, :] = (xt[rows, :].astype(F32) * inv * g).astype(BF16)
    inv_out[...] = jnp.broadcast_to(inv, (8, T))
    at = times(head[0], W)
    x_own[...] = xt[at, :]
    scale_own[...] = scale[at, :]
    quarter[:W, :] = normed[at, :]
    copies[2].wait()


def project_kernel(normed, w, w_out, ids, proj):
    proj[...] = jnp.dot(w[...], normed[...], preferred_element_type=F32).astype(BF16)


def payload_kernel(head, c0, c1, c2, c3, proj, w_out, ids, own, cot):
    for k, piece in enumerate((c0, c1, c2, c3)):
        cot[times(jnp.bitwise_xor(head[0], k), W), :] = piece[...]
    d_ctx = jnp.dot(w_out[...], cot[...], preferred_element_type=F32).astype(BF16)
    id_rows = jnp.broadcast_to((ids[...] + 1).astype(F32), (IDROWS, T)).astype(BF16)
    for m in range(HL):
        rows = [proj[j * W + m * HD : j * W + (m + 1) * HD, :] for j in range(3)]
        rows = rows + [d_ctx[m * HD : (m + 1) * HD, :], id_rows]
        for u in range(2):
            for j, block in enumerate(rows):
                own[4 * u + m, j * HD : j * HD + block.shape[0], :] = block


def attention_kernel(zz, local, halo, grads, o0, o1, o2, o3, win, kn, vn, idk, es, ds, ps, dss, gk, gv, sems):
    u, m = lax.div(zz[0], 4), lax.rem(zz[0], 4)

    @pl.when(u == 0)
    def _():
        win[:3] = halo[...]
        win[3:] = local[:7]

    @pl.when(u == 1)
    def _():
        win[:7] = local[1:]
        win[7:] = halo[...]

    def rows(c, j):
        return win[c, j * HD : (j + 1) * HD, :]

    def side(first, last, j):
        return jnp.concatenate([rows(c, j) for c in range(first, last)], axis=1)

    ids = [win[c, 4 * HD : 4 * HD + 1, :].astype(F32) for c in range(WIN)]
    for c in range(WIN):
        at = slice(c * T, (c + 1) * T)
        idk[at, :] = jnp.transpose(jnp.broadcast_to(ids[c], (2 * T, T)))
        kn[at, :] = jnp.transpose(rows(c, 1))
        vn[at, :] = jnp.transpose(rows(c, 2))
    gk[...] = jnp.zeros(gk.shape, F32)
    gv[...] = jnp.zeros(gv.shape, F32)
    for qa, qb, ka, kb in GROUPS:
        n = (qb - qa) * T
        qt, dt = side(qa, qb, 0), side(qa, qb, 3)
        idq = jnp.concatenate(ids[qa:qb], axis=1)
        esum = jnp.zeros((1, n), F32)
        dsum = jnp.zeros((1, n), F32)
        for c in range(ka, kb):
            kr = slice(c * T, (c + 1) * T)
            s = jnp.dot(kn[kr, :], qt, preferred_element_type=F32)
            dp = jnp.dot(vn[kr, :], dt, preferred_element_type=F32)
            e = jnp.exp2(jnp.where(idk[kr, :] == idq, s * (SCALE * LOG2E), -1e30))
            es[kr, :] = e
            ds[kr, :] = dp
            esum = esum + jnp.sum(e, axis=0, keepdims=True)
            dsum = dsum + jnp.sum(e * dp, axis=0, keepdims=True)
        r = 1.0 / jnp.maximum(esum, 1e-37)
        delta = dsum * r
        qs, qe = max(qa, OWN), min(qb, OWN + 4)
        ks, ke = max(ka, OWN), min(kb, OWN + 4)
        for c in range(ka, kb) if qs < qe else range(ks, ke):
            kr = slice(c * T, (c + 1) * T)
            p = es[kr, :] * r
            ps[kr, :] = p.astype(BF16)
            dss[kr, :] = (p * (ds[kr, :] - delta)).astype(BF16)
        own = slice(ks * T, ke * T)
        to = slice((ks - OWN) * T, (ke - OWN) * T)
        gk[:, to] += lax.dot_general(qt, dss[own, :], LANES, preferred_element_type=F32)
        gv[:, to] += lax.dot_general(dt, ps[own, :], LANES, preferred_element_type=F32)
        if qs < qe:
            cols = slice((qs - qa) * T, (qe - qa) * T)
            kr = slice(ka * T, kb * T)
            gq = jnp.dot(side(ka, kb, 1), dss[kr, cols], preferred_element_type=F32) * SCALE
            ctx = jnp.dot(side(ka, kb, 2), ps[kr, cols], preferred_element_type=F32)
            for i in range(qe - qs):
                lane = slice(i * T, (i + 1) * T)
                grads[qs - OWN + i, :HD, :] = gq[:, lane].astype(BF16)
                grads[qs - OWN + i, 3 * HD :, :] = ctx[:, lane].astype(BF16)
    for i in range(4):
        lane = slice(i * T, (i + 1) * T)
        grads[i, HD : 2 * HD, :] = (gk[:, lane] * SCALE).astype(BF16)
        grads[i, 2 * HD : 3 * HD, :] = gv[:, lane].astype(BF16)
    o0[...] = grads[m]
    outs = enumerate((o1, o2, o3), 1)
    for copy in fetch(sems, *[(grads.at[jnp.bitwise_xor(m, k)], out) for k, out in outs]):
        copy.wait()


def attention(zz, local, halo):
    big = (WIN * T, 2 * T)
    return call(
        attention_kernel,
        "attention",
        [shape((4, 4 * HD, T))] + [shape((4 * HD, T))] * 4,
        [
            pltpu.VMEM((WIN, R, T), BF16),
            pltpu.VMEM((WIN * T, HD), BF16),
            pltpu.VMEM((WIN * T, HD), BF16),
            pltpu.VMEM(big, F32),
            pltpu.VMEM(big, F32),
            pltpu.VMEM(big, F32),
            pltpu.VMEM(big, BF16),
            pltpu.VMEM(big, BF16),
            pltpu.VMEM((HD, 4 * T), F32),
            pltpu.VMEM((HD, 4 * T), F32),
            pltpu.SemaphoreType.DMA((3,)),
        ],
        [zz],
        local,
        halo,
        far_outs=3,
    )


def pieces_kernel(zz, head, b0, b1, b2, b3, proj, w, w_out, p0, p1, p2, p3, grads, parts, sems):
    m = lax.rem(zz[0], 4)
    for k, piece in enumerate((b0, b1, b2, b3)):
        other = jnp.bitwise_xor(m, k)
        for j in range(4):
            grads[times(j * HL + other, HD), :] = piece[j * HD : (j + 1) * HD, :]
    total = jnp.sum(grads[: 3 * W, :].astype(F32) * proj[...].astype(F32), axis=0, keepdims=True)
    hi = total.astype(BF16).astype(F32)
    row = lax.broadcasted_iota(jnp.int32, (IDROWS, T), 0)
    tail = jnp.where(row == 0, hi, jnp.where(row == 1, total - hi, 0.0)).astype(BF16)
    g = jnp.transpose(grads[...])
    d_part = jnp.dot(g[:, : 3 * W], w[...], preferred_element_type=F32)
    out_part = jnp.dot(g[:, 3 * W :], w_out[...], preferred_element_type=F32)
    out_part = jnp.transpose(out_part.astype(BF16))
    d_part = jnp.transpose(d_part.astype(BF16))
    for j in range(4):
        parts[j, :W, :] = out_part[j * W : (j + 1) * W, :]
        parts[j, W : 2 * W, :] = d_part[j * W : (j + 1) * W, :]
        parts[j, 2 * W :, :] = tail
    p0[...] = parts[head[0]]
    outs = enumerate((p1, p2, p3), 1)
    for copy in fetch(sems, *[(parts.at[jnp.bitwise_xor(head[0], k)], out) for k, out in outs]):
        copy.wait()


def rows_kernel(g0, g1, g2, g3, x_own, scale_own, inv, attn_out, grad_patches):
    total = g0[...].astype(F32) + g1[...].astype(F32) + g2[...].astype(F32) + g3[...].astype(F32)
    attn_out[...] = total[:W, :].astype(BF16)
    d_own = total[W : 2 * W, :]
    x = x_own[...].astype(F32)
    i = inv[0:1, :]
    row_total = total[2 * W : 2 * W + 1, :] + total[2 * W + 1 : 2 * W + 2, :]
    grad_patches[...] = (scale_own[...] * d_own - x * (i * i * row_total * (1.0 / D))).astype(BF16)


def assemble_kernel(head, h0, h1, h2, h3, n, c):
    for j, quarter in enumerate((h0, h1, h2, h3)):
        at = times(jnp.bitwise_xor(head[0], j), W)
        for k in range(4):
            lane = slice(k * T, (k + 1) * T)
            n[at, lane] = quarter[2 * k * W : (2 * k + 1) * W, :]
            c[at, lane] = quarter[(2 * k + 1) * W : (2 * k + 2) * W, :]


def weights_kernel(zz, n, c, grads, gain, w, out, g, term):
    m = lax.rem(zz[0], 4)
    for k in range(4):
        g[:, k * T : (k + 1) * T] = grads[jnp.bitwise_xor(m, k)]
    left = lax.dot_general(n[...], g[: 3 * HD, :], LANES, preferred_element_type=F32)
    right = lax.dot_general(c[...], g[3 * HD :, :], LANES, preferred_element_type=F32)
    term[...] = jnp.concatenate([left, right], axis=1)
    turned = lax.dot_general(g[: 3 * HD, :], n[...], LANES, preferred_element_type=F32)
    gg = jnp.zeros((1, D), F32)
    for j in range(3):
        product = turned[j * HD : (j + 1) * HD, :] * w[times(j * HL + m, HD), :].astype(F32)
        gg = gg + jnp.sum(product, axis=0, keepdims=True)
    rows = [gg[:, l * T : (l + 1) * T] / gain[l : l + 1, :] for l in range(10)]
    rows = rows + [jnp.zeros((6, T), F32)]
    tail = jnp.concatenate(rows, axis=0).astype(BF16)
    for d in range(8):
        out[d, :160, :] = term[160 * d : 160 * d + 160, :T].astype(BF16)
        out[d, 160:320, :] = term[160 * d : 160 * d + 160, T : 2 * T].astype(BF16)
        halves = [term[160 * d + 80 * i : 160 * d + 80 * i + 80, 2 * T :] for i in range(2)]
        out[d, 320:400, :] = jnp.concatenate(halves, axis=1).astype(BF16)
        out[d, 400:, :] = tail


def middle_kernel(got, out, total):
    total[...] = sum(got[i].astype(F32) for i in range(8))
    zero = jnp.zeros((4, T), F32)
    for z in range(8):
        third = total[320 + 20 * (z % 4) : 340 + 20 * (z % 4), :]
        if z >= 4:
            third = pltpu.roll(third, 64, 1)
        rows = [total[20 * z : 20 * z + 20, :], total[160 + 20 * z : 180 + 20 * z, :], third]
        out[z] = jnp.concatenate(rows + [zero, total[400:, :]], axis=0).astype(BF16)


def sums_kernel(got, qkv, out, gg):
    tail = jnp.zeros((16, T), F32)
    cols = []
    for m in range(HL):
        total = got[m].astype(F32) + got[4 + m].astype(F32)
        cols.append(jnp.concatenate([total[20 * l : 20 * l + 20, :] for l in range(3)], axis=1))
        tail = tail + total[64:80, :]
    for j in range(3):
        qkv[j] = jnp.concatenate([x[:, j * HD : (j + 1) * HD] for x in cols], axis=1)
    out[...] = jnp.concatenate([x[:, 3 * HD : 4 * HD] for x in cols], axis=1)
    gg[...] = tail


def gain_kernel(head, t0, t1, t2, t3, out):
    total = t0[...] + t1[...] + t2[...] + t3[...]
    flat = jnp.concatenate([total[l : l + 1, :] for l in range(10)], axis=1)
    for j in range(4):
        @pl.when(head[0] == j)
        def _():
            out[...] = flat[:, j * W : (j + 1) * W]


def along_z(x, by):
    return lax.ppermute(x, "z", [(i, i ^ by) for i in range(8)]) if by else x


def along_head(x, by):
    return lax.ppermute(x, HEAD, [(i, i ^ by) for i in range(4)]) if by else x


def to_next_group(x):
    pairs = []
    for i in range(64):
        group = i // 8 + (1 if i % 8 < 4 else -1)
        if 0 <= group < 8:
            pairs.append((i, group * 8 + i % 8))
    return lax.ppermute(x, SEQ, pairs)


def body(patches, gain, w_qkv, w_out, image_ids, cotangent):
    head = lax.axis_index(HEAD).astype(jnp.int32).reshape(1)
    zz = lax.axis_index("z").astype(jnp.int32).reshape(1)
    cot = cotangent.T
    gain = gain.reshape(10, T)
    w = w_qkv.transpose(1, 2, 0).reshape(3 * W, D)
    normed, quarter, x_own, scale_own, inv = call(
        norm_kernel,
        "norm",
        [shape((D, T)), shape((2 * W, T)), shape((W, T)), shape((W, T), F32), shape((8, T), F32)],
        [
            pltpu.VMEM((T, D), BF16),
            pltpu.VMEM((10, T), F32),
            pltpu.VMEM((D, T), BF16),
            pltpu.VMEM((D, T), F32),
            pltpu.SemaphoreType.DMA((3,)),
        ],
        [head],
        patches,
        gain,
        cot,
        far=3,
        limit=60,
    )
    cot, normed = lax.optimization_barrier((cot, normed))
    cots = [along_head(cot, k) for k in range(4)]
    quarter = jnp.concatenate([along_z(quarter, k) for k in range(4)], axis=0)
    ids = image_ids.reshape(1, T)
    proj = call(project_kernel, "project", shape((3 * W, T)), [], [], normed, w, w_out, ids)
    own = call(
        payload_kernel,
        "payload",
        shape((8, R, T)),
        [pltpu.VMEM((D, T), BF16)],
        [head],
        *cots,
        proj,
        w_out,
        ids,
    )
    own, quarter = lax.optimization_barrier((own, quarter))
    local = lax.all_to_all(own, "z", 0, 0, tiled=True)
    near = lax.dynamic_slice_in_dim(local, jnp.where(zz[0] < 4, 5, 0), 3, 0)
    across = along_head(quarter, 2)
    near, across = lax.optimization_barrier((near, across))
    halo = to_next_group(near)
    quarters = [quarter, along_head(quarter, 1), across, along_head(across, 1)]
    n, c = call(
        assemble_kernel, "assemble", [shape((D, 4 * T))] * 2, [], [head], *quarters
    )
    halo, n, c = lax.optimization_barrier((halo, n, c))
    grads, *backs = attention(zz, local, halo)
    terms = call(
        weights_kernel,
        "weights",
        shape((8, 416, T)),
        [pltpu.VMEM((W, 4 * T), BF16), pltpu.VMEM((D, W), F32)],
        [zz],
        n,
        c,
        grads,
        gain,
        w,
    )
    backs, terms = lax.optimization_barrier((backs, terms))
    terms = lax.all_to_all(terms, ("y", "xh"), 0, 0, tiled=True)
    backs = [along_z(b, k) for k, b in enumerate(backs)]
    pieces = call(
        pieces_kernel,
        "pieces",
        [shape((2 * W + IDROWS, T))] * 4,
        [
            pltpu.VMEM((4 * W, T), BF16),
            pltpu.VMEM((4, 2 * W + IDROWS, T), BF16),
            pltpu.SemaphoreType.DMA((3,)),
        ],
        [zz, head],
        *backs,
        proj,
        w,
        w_out,
        far_outs=3,
    )
    terms, pieces = lax.optimization_barrier((terms, pieces))
    got = [along_head(p, k) for k, p in enumerate(pieces)]
    terms = call(middle_kernel, "middle", shape((8, 80, T)), [pltpu.VMEM((416, T), F32)], [], terms)
    terms = lax.all_to_all(terms, "z", 0, 0, tiled=True)
    terms, got = lax.optimization_barrier((terms, got))
    attn_out, grad_patches = call(
        rows_kernel,
        "rows",
        [shape((W, T)), shape((W, T))],
        [],
        [],
        *got,
        x_own,
        scale_own,
        inv,
    )
    grad_w_qkv, grad_w_out, gg = call(
        sums_kernel,
        "sums",
        [shape((3, 20, W), F32), shape((20, W), F32), shape((16, T), F32)],
        [],
        [],
        terms,
    )
    grad_gain = call(
        gain_kernel, "gain", shape((1, W), F32), [], [head], *[along_head(gg, k) for k in range(4)]
    )
    return (attn_out.T, grad_patches.T, grad_w_qkv.transpose(1, 0, 2), grad_w_out.T, grad_gain.reshape(W))


def solution(mesh):
    fine = Mesh(mesh.devices.reshape(4, 2, 8, 2, 2), SEQ + HEAD)
    in_specs = (
        P(SEQ, None),
        P(),
        P(None, None, HEAD),
        P(HEAD, None),
        P(SEQ),
        P(SEQ, HEAD),
    )
    out_specs = (
        P(SEQ, HEAD),
        P(SEQ, HEAD),
        P(SEQ, None, HEAD),
        P(HEAD, SEQ),
        P(HEAD),
    )
    return jax.shard_map(body, mesh=fine, in_specs=in_specs, out_specs=out_specs, check_vma=False)
```

time: 137 us -> 117 us (0.85)
  the two profiles are of different devices: /device:TPU:32 before, /device:TPU:1 now
where the time goes in v1:
time: 117 us
  starting transfers between devices  42.9 us (37%)
  waiting for transfers between devices  42.8 us (37%)
  Pallas kernels  17 us (15%)
  local copies, waits for them, and re-layouts  11.5 us (10%)
  other arithmetic  1.49 us (1%)
    all_to_all x1, waiting for transfers between devices, body(): local = lax.all_to_all(own, 'z', 0, 0, tiled=True)  20 us
    pallas_call x11, Pallas kernels, call(): pl.pallas_call(kernel, out_shape=outs, in_specs=specs, out_specs=vmem if...  17 us
    ppermute x12, starting transfers between devices, along_head(): return lax.ppermute(x, HEAD, [(i, i ^ by) for i in range(4)]) if by else x  12.1 us
    unnamed x52, local copies, waits for them, and re-layouts  11.5 us
    ppermute x6, waiting for transfers between devices, along_z(): return lax.ppermute(x, 'z', [(i, i ^ by) for i in range(8)]) if by else x  9.31 us
    ppermute x6, starting transfers between devices, along_z(): return lax.ppermute(x, 'z', [(i, i ^ by) for i in range(8)]) if by else x  8.17 us
    ppermute x12, waiting for transfers between devices, along_head(): return lax.ppermute(x, HEAD, [(i, i ^ by) for i in range(4)]) if by else x  8.09 us
    all_to_all x1, starting transfers between devices, body(): terms = lax.all_to_all(terms, ('y', 'xh'), 0, 0, tiled=True)  7.75 us
  transfers between devices with their start and end apart: 22, of which 9 were waited for; matrix products, arithmetic and copies ran while one was open for 0% of the time, Pallas kernels for 5%

profile of v1, /device:TPU:1, one launch (start us, length us, event | category | flops | bytes accessed | tf_op | source)
XLA Modules:
  0.0 116.6 jit_solution(6972426178600967523)
XLA Ops:
  0.6 2.2 %norm.1 = (bf16[1280,128]{1,0:T(8,128)(2,1)}, bf16[640,128]{1,0:T(8,128)(2,1)}, bf16[320,128]{1,0:T(8,128)(2,1)}, f32[320,128]{1,0:T(8,128)}, f32[8,128]{1,0:T(8,128)}) custom-call(s32[1]{0:T(128)} %bitcast.1.head, bf16[128,1280]{1,0:T(8,128)(2,1)} %patches_far.1, f32[10,128]{1,0:T(8,128)} %bitcast.20, bf16[320,128]{1,0:T(8,128)(2,1)} %bitcast.15), custom_call_target="tpu_custom_call" | custom-call | flops 1000 | bytes 1000 | tf_op jit(solution)/shard_map/norm/pallas_call | solution.py:32
  2.9 2.7 %collective-permute-start.2 = (bf16[320,128]{1,0:T(8,128)(2,1)}, bf16[320,128]{1,0:T(8,128)(2,1)S(1)}, u32[]{:S(2)}, u32[]{:S(2)}) collective-permute-start(bf16[320,128]{1,0:T(8,128)(2,1)} %bitcast.16), channel_id=1, source_target_pairs={{0,3},{1,2},{2,1},{3,0},{4,7},{5,6},{6,5},{7,4},{8,11},{9,10},{10,... | collective-permute-start | bytes 245768 | tf_op jit(solution)/shard_map/ppermute | solution.py:301
  5.6 4.3 %collective-permute-start.5 = (bf16[640,128]{1,0:T(8,128)(2,1)}, bf16[640,128]{1,0:T(8,128)(2,1)S(1)}, u32[]{:S(2)}, u32[]{:S(2)}) collective-permute-start(bf16[640,128]{1,0:T(8,128)(2,1)} %get-tuple-element.53), channel_id=1, source_target_pairs={{0,12},{4,8},{8,4},{12,0},{16,28},{20,24},{24,20},{28,16},{1,13},{... | collective-permute-start | bytes 491528 | tf_op jit(solution)/shard_map/ppermute | solution.py:297
  10.2 0.9 collective-permute-start.1
  11.4 1.7 %copy-done = bf16[1280,3,320]{0,2,1:T(8,128)(2,1)S(1)} copy-done((bf16[1280,3,320]{0,2,1:T(8,128)(2,1)S(1)}, bf16[1280,3,320]{0,2,1:T(8,128)(2,1)}, u32[]{:S(2)}) %copy-start) | copy-done | bytes 2457624
  13.0 1.1 copy-done.2
  14.2 1.0 copy-done.5
  16.7 1.3 %payload.1 = bf16[8,336,128]{2,1,0:T(8,128)(2,1)} custom-call(s32[1]{0:T(128)} %bitcast.1.head, bf16[320,128]{1,0:T(8,128)(2,1)S(1)} %bitcast.19, bf16[320,128]{1,0:T(8,128)(2,1)S(1)} %collective-permute-done.c1, bf16[320,128]{1,0:T(8,128)(2,1)S(1)} %collective-permute-done.1.c2, bf16[320,128]{1,0:T(8,128)(2,1)S(1)} %collective-permute-done.2.c3, ...), custom_call_target="tpu_custom_call" | custom-call | flops 1000 | bytes 1000 | tf_op jit(solution)/shard_map/payload/pallas_call | solution.py:32
  18.0 5.9 %collective-permute-done.4 = bf16[640,128]{1,0:T(8,128)(2,1)S(1)} collective-permute-done((bf16[640,128]{1,0:T(8,128)(2,1)}, bf16[640,128]{1,0:T(8,128)(2,1)S(1)}, u32[]{:S(2)}, u32[]{:S(2)}) %collective-permute-start.4) | collective-permute-done | bytes 163872 | tf_op jit(solution)/shard_map/ppermute | solution.py:297
  23.9 0.9 pad_maximum_fusion.h0
  24.8 6.9 %all-to-all-start = ((bf16[8,336,128]{2,1,0:T(8,128)(2,1)}), bf16[8,336,128]{2,1,0:T(8,128)(2,1)S(1)}, u32[]{:S(2)}, u32[]{:S(2)}) async-start(bf16[8,336,128]{2,1,0:T(8,128)(2,1)} %payload.1), calls=%async_computation | async-start | bytes 1376256 | tf_op jit(solution)/shard_map/all_to_all | solution.py:354
  32.0 1.3 %collective-permute-start.8 = (bf16[2560,128]{1,0:T(8,128)(2,1)}, bf16[2560,128]{1,0:T(8,128)(2,1)}, u32[]{:S(2)}, u32[]{:S(2)}) collective-permute-start(bf16[2560,128]{1,0:T(8,128)(2,1)} %pad_maximum_fusion.h0), channel_id=1, source_target_pairs={{0,1},{1,0},{2,3},{3,2},{4,5},{5,4},{6,7},{7,6},{8,9},{9,8},{10,11... | collective-permute-start | bytes 1966088 | tf_op jit(solution)/shard_map/ppermute | solution.py:301
  33.3 20.0 %all-to-all-done.local = bf16[8,336,128]{2,1,0:T(8,128)(2,1)S(1)} async-done(((bf16[8,336,128]{2,1,0:T(8,128)(2,1)}), bf16[8,336,128]{2,1,0:T(8,128)(2,1)S(1)}, u32[]{:S(2)}, u32[]{:S(2)}) %all-to-all-start) | async-done | bytes 688160 | tf_op jit(solution)/shard_map/all_to_all | solution.py:354
  53.9 4.5 %collective-permute-start.7 = (bf16[3,336,128]{2,1,0:T(8,128)(2,1)S(1)}, bf16[3,336,128]{2,1,0:T(8,128)(2,1)S(1)}, u32[]{:S(2)}, u32[]{:S(2)}) collective-permute-start(bf16[3,336,128]{2,1,0:T(8,128)(2,1)S(1)} %constant_dynamic-slice_fusion), channel_id=1, source_target_pairs={{0,32},{4,36},{8,40},{12,44},{32,64},{36,68},{40,72},{44,76},{48,1... | collective-permute-start | bytes 774152 | tf_op jit(solution)/shard_map/ppermute | solution.py:310
  58.4 1.9 %assemble.1 = (bf16[1280,512]{1,0:T(8,128)(2,1)S(1)}, bf16[1280,512]{1,0:T(8,128)(2,1)S(1)}) custom-call(s32[1]{0:T(128)} %bitcast.1.head, bf16[2560,128]{1,0:T(8,128)(2,1)} %pad_maximum_fusion.h0, bf16[2560,128]{1,0:T(8,128)(2,1)} %collective-permute-done.8.h1, bf16[2560,128]{1,0:T(8,128)(2,1)} %collective-permute-done.6.h2, ...), custom_call_target="tpu_custom_call" | custom-call | flops 1000 | bytes 1000 | tf_op jit(solution)/shard_map/assemble/pallas_call | solution.py:32
  60.3 3.6 %collective-permute-done.7.halo = bf16[3,336,128]{2,1,0:T(8,128)(2,1)S(1)} collective-permute-done((bf16[3,336,128]{2,1,0:T(8,128)(2,1)S(1)}, bf16[3,336,128]{2,1,0:T(8,128)(2,1)S(1)}, u32[]{:S(2)}, u32[]{:S(2)}) %collective-permute-start.7) | collective-permute-done | bytes 258080 | tf_op jit(solution)/shard_map/ppermute | solution.py:310
  64.0 4.3 %attention.1 = (bf16[4,320,128]{2,1,0:T(8,128)(2,1)S(1)}, bf16[320,128]{1,0:T(8,128)(2,1)S(1)}, bf16[320,128]{1,0:T(8,128)(2,1)S(1)}, bf16[320,128]{1,0:T(8,128)(2,1)S(1)}, bf16[320,128]{1,0:T(8,128)(2,1)S(1)}) custom-call(s32[1]{0:T(128)} %bitcast.zz, bf16[8,336,128]{2,1,0:T(8,128)(2,1)S(1)} %all-to-all-done.local, ...), custom_call_target="tpu_custom_call" | custom-call | flops 1000 | bytes 1000 | tf_op jit(solution)/shard_map/attention/pallas_call | solution.py:32
  70.8 1.3 %weights.1 = bf16[8,416,128]{2,1,0:T(8,128)(2,1)S(1)} custom-call(s32[1]{0:T(128)} %bitcast.zz, bf16[1280,512]{1,0:T(8,128)(2,1)S(1)} %get-tuple-element.65.n, bf16[1280,512]{1,0:T(8,128)(2,1)S(1)} %get-tuple-element.66.c, bf16[4,320,128]{2,1,0:T(8,128)(2,1)S(1)} %get-tuple-element.67.grads, f32[10,128]{1,0:T(8,128)S(1)} %bitcast.21, ...), custom_call_target="tpu_custom_call" | custom-call | flops 1000 | bytes 1000 | tf_op jit(solution)/shard_map/weights/pallas_call | solution.py:32
  72.1 0.9 copy-done.4
  73.0 7.7 %all-to-all-start.1 = ((bf16[8,416,128]{2,1,0:T(8,128)(2,1)}), bf16[8,416,128]{2,1,0:T(8,128)(2,1)}, u32[]{:S(2)}, u32[]{:S(2)}) async-start(bf16[8,416,128]{2,1,0:T(8,128)(2,1)} %copy-done.4), calls=%async_computation.1 | async-start | bytes 1703936 | tf_op jit(solution)/shard_map/all_to_all | solution.py:378
  80.8 3.4 %collective-permute-start.12 = (bf16[320,128]{1,0:T(8,128)(2,1)}, bf16[320,128]{1,0:T(8,128)(2,1)S(1)}, u32[]{:S(2)}, u32[]{:S(2)}) collective-permute-start(bf16[320,128]{1,0:T(8,128)(2,1)} %copy-done.22), channel_id=1, source_target_pairs={{0,12},{4,8},{8,4},{12,0},{16,28},{20,24},{24,20},{28,16},{1,13},{... | collective-permute-start | bytes 245768 | tf_op jit(solution)/shard_map/ppermute | solution.py:297
  84.3 1.0 collective-permute-done.11.b2
  85.2 2.4 %collective-permute-done.12.b3 = bf16[320,128]{1,0:T(8,128)(2,1)S(1)} collective-permute-done((bf16[320,128]{1,0:T(8,128)(2,1)}, bf16[320,128]{1,0:T(8,128)(2,1)S(1)}, u32[]{:S(2)}, u32[]{:S(2)}) %collective-permute-start.12) | collective-permute-done | bytes 81952 | tf_op jit(solution)/shard_map/ppermute | solution.py:297
  88.5 1.5 %pieces.1 = (bf16[656,128]{1,0:T(8,128)(2,1)S(1)}, bf16[656,128]{1,0:T(8,128)(2,1)S(1)}, bf16[656,128]{1,0:T(8,128)(2,1)S(1)}, bf16[656,128]{1,0:T(8,128)(2,1)S(1)}) custom-call(s32[1]{0:T(128)} %bitcast.zz, s32[1]{0:T(128)} %bitcast.1.head, bf16[320,128]{1,0:T(8,128)(2,1)S(1)} %copy-done.12, bf16[320,128]{1,0:T(8,128)(2,1)S(1)} %collective-permute-done.10.b1, ...), custom_call_target="tpu_custom_call" | custom-call | flops 1000 | bytes 1000 | tf_op jit(solution)/shard_map/pieces/pallas_call | solution.py:32
  92.7 1.9 %all-to-all-done.1.got = bf16[8,416,128]{2,1,0:T(8,128)(2,1)} async-done(((bf16[8,416,128]{2,1,0:T(8,128)(2,1)}), bf16[8,416,128]{2,1,0:T(8,128)(2,1)}, u32[]{:S(2)}, u32[]{:S(2)}) %all-to-all-start.1) | async-done | bytes 852000 | tf_op jit(solution)/shard_map/all_to_all | solution.py:378
  94.6 2.1 %middle.1 = bf16[8,80,128]{2,1,0:T(8,128)(2,1)} custom-call(bf16[8,416,128]{2,1,0:T(8,128)(2,1)} %all-to-all-done.1.got), custom_call_target="tpu_custom_call" | custom-call | flops 1000 | bytes 1000 | tf_op jit(solution)/shard_map/middle/pallas_call | solution.py:32
  96.6 3.5 %all-to-all-start.2 = ((bf16[8,80,128]{2,1,0:T(8,128)(2,1)}), bf16[8,80,128]{2,1,0:T(8,128)(2,1)S(1)}, u32[]{:S(2)}, u32[]{:S(2)}) async-start(bf16[8,80,128]{2,1,0:T(8,128)(2,1)} %middle.1), calls=%async_computation.2 | async-start | bytes 327680 | tf_op jit(solution)/shard_map/all_to_all | solution.py:399
  100.1 2.3 %collective-permute-start.13 = (bf16[656,128]{1,0:T(8,128)(2,1)S(1)}, bf16[656,128]{1,0:T(8,128)(2,1)S(1)}, u32[]{:S(2)}, u32[]{:S(2)}) collective-permute-start(bf16[656,128]{1,0:T(8,128)(2,1)S(1)} %copy-done.21), channel_id=1, source_target_pairs={{0,1},{1,0},{2,3},{3,2},{4,5},{5,4},{6,7},{7,6},{8,9},{9,8},{10,11... | collective-permute-start | bytes 503816 | tf_op jit(solution)/shard_map/ppermute | solution.py:301
  102.4 1.7 %collective-permute-start.15 = (bf16[656,128]{1,0:T(8,128)(2,1)S(1)}, bf16[656,128]{1,0:T(8,128)(2,1)S(1)}, u32[]{:S(2)}, u32[]{:S(2)}) collective-permute-start(bf16[656,128]{1,0:T(8,128)(2,1)S(1)} %copy-done.17), channel_id=1, source_target_pairs={{0,3},{1,2},{2,1},{3,0},{4,7},{5,6},{6,5},{7,4},{8,11},{9,10},{10,... | collective-permute-start | bytes 503816 | tf_op jit(solution)/shard_map/ppermute | solution.py:301
  104.2 4.1 %collective-permute-done.14.g2 = bf16[656,128]{1,0:T(8,128)(2,1)S(1)} collective-permute-done((bf16[656,128]{1,0:T(8,128)(2,1)S(1)}, bf16[656,128]{1,0:T(8,128)(2,1)S(1)}, u32[]{:S(2)}, u32[]{:S(2)}) %collective-permute-start.14) | collective-permute-done | bytes 167968 | tf_op jit(solution)/shard_map/ppermute | solution.py:301
  108.3 3.8 %collective-permute-done.15.g3 = bf16[656,128]{1,0:T(8,128)(2,1)S(1)} collective-permute-done((bf16[656,128]{1,0:T(8,128)(2,1)S(1)}, bf16[656,128]{1,0:T(8,128)(2,1)S(1)}, u32[]{:S(2)}, u32[]{:S(2)}) %collective-permute-start.15) | collective-permute-done | bytes 167968 | tf_op jit(solution)/shard_map/ppermute | solution.py:301
  113.0 1.4 %collective-permute-start.17 = (f32[16,128]{1,0:T(8,128)S(1)}, f32[16,128]{1,0:T(8,128)S(1)}, u32[]{:S(2)}, u32[]{:S(2)}) collective-permute-start(f32[16,128]{1,0:T(8,128)S(1)} %get-tuple-element.94.t0), channel_id=1, source_target_pairs={{0,2},{1,3},{2,0},{3,1},{4,6},{5,7},{6,4},{7,5},{8,10},{9,11},{10,... | collective-permute-start | bytes 24584 | tf_op jit(solution)/shard_map/ppermute | solution.py:301
  (78 shorter events, 12.1 us)
Async XLA Ops:
  2.9 8.2 %collective-permute-start.2 = (bf16[320,128]{1,0:T(8,128)(2,1)}, bf16[320,128]{1,0:T(8,128)(2,1)S(1)}, u32[]{:S(2)}, u32[]{:S(2)}) collective-permute-start(bf16[320,128]{1,0:T(8,128)(2,1)} %bitcast.16), channel_id=1, source_target_pairs={{0,3},{1,2},{2,1},{3,0},{4,7},{5,6},{6,5},{7,4},{8,11},{9,10},{10,... | collective-permute-start | bytes 245768 | tf_op jit(solution)/shard_map/ppermute | solution.py:301
  5.6 12.4 %collective-permute-start.5 = (bf16[640,128]{1,0:T(8,128)(2,1)}, bf16[640,128]{1,0:T(8,128)(2,1)S(1)}, u32[]{:S(2)}, u32[]{:S(2)}) collective-permute-start(bf16[640,128]{1,0:T(8,128)(2,1)} %get-tuple-element.53), channel_id=1, source_target_pairs={{0,12},{4,8},{8,4},{12,0},{16,28},{20,24},{24,20},{28,16},{1,13},{... | collective-permute-start | bytes 491528 | tf_op jit(solution)/shard_map/ppermute | solution.py:297
  9.9 14.0 %collective-permute-start.4 = (bf16[640,128]{1,0:T(8,128)(2,1)}, bf16[640,128]{1,0:T(8,128)(2,1)S(1)}, u32[]{:S(2)}, u32[]{:S(2)}) collective-permute-start(bf16[640,128]{1,0:T(8,128)(2,1)} %get-tuple-element.53), channel_id=1, source_target_pairs={{0,8},{4,12},{8,0},{12,4},{16,24},{20,28},{24,16},{28,20},{1,9},{5... | collective-permute-start | bytes 491528 | tf_op jit(solution)/shard_map/ppermute | solution.py:297
  9.9 14.0 %collective-permute-start.3 = (bf16[640,128]{1,0:T(8,128)(2,1)}, bf16[640,128]{1,0:T(8,128)(2,1)S(1)}, u32[]{:S(2)}, u32[]{:S(2)}) collective-permute-start(bf16[640,128]{1,0:T(8,128)(2,1)} %get-tuple-element.53), channel_id=1, source_target_pairs={{0,4},{4,0},{8,12},{12,8},{16,20},{20,16},{24,28},{28,24},{1,5},{5... | collective-permute-start | bytes 491528 | tf_op jit(solution)/shard_map/ppermute | solution.py:297
  10.2 6.4 %collective-permute-start.1 = (bf16[320,128]{1,0:T(8,128)(2,1)}, bf16[320,128]{1,0:T(8,128)(2,1)S(1)}, u32[]{:S(2)}, u32[]{:S(2)}) collective-permute-start(bf16[320,128]{1,0:T(8,128)(2,1)} %bitcast.17), channel_id=1, source_target_pairs={{0,2},{1,3},{2,0},{3,1},{4,6},{5,7},{6,4},{7,5},{8,10},{9,11},{10,... | collective-permute-start | bytes 245768 | tf_op jit(solution)/shard_map/ppermute | solution.py:301
  11.1 5.5 %collective-permute-start = (bf16[320,128]{1,0:T(8,128)(2,1)}, bf16[320,128]{1,0:T(8,128)(2,1)S(1)}, u32[]{:S(2)}, u32[]{:S(2)}) collective-permute-start(bf16[320,128]{1,0:T(8,128)(2,1)} %bitcast.18), channel_id=1, source_target_pairs={{0,1},{1,0},{2,3},{3,2},{4,5},{5,4},{6,7},{7,6},{8,9},{9,8},{10,11... | collective-permute-start | bytes 245768 | tf_op jit(solution)/shard_map/ppermute | solution.py:301
  16.6 7.3 %copy-start.25 = (bf16[640,128]{1,0:T(8,128)(2,1)S(1)}, bf16[640,128]{1,0:T(8,128)(2,1)}, u32[]{:S(2)}) copy-start(bf16[640,128]{1,0:T(8,128)(2,1)} %get-tuple-element.53) | copy-start | bytes 491524
  24.8 28.4 %all-to-all-start = ((bf16[8,336,128]{2,1,0:T(8,128)(2,1)}), bf16[8,336,128]{2,1,0:T(8,128)(2,1)S(1)}, u32[]{:S(2)}, u32[]{:S(2)}) async-start(bf16[8,336,128]{2,1,0:T(8,128)(2,1)} %payload.1), calls=%async_computation | async-start | bytes 1376256 | tf_op jit(solution)/shard_map/all_to_all | solution.py:354
  31.8 21.5 %collective-permute-start.6 = (bf16[2560,128]{1,0:T(8,128)(2,1)}, bf16[2560,128]{1,0:T(8,128)(2,1)}, u32[]{:S(2)}, u32[]{:S(2)}) collective-permute-start(bf16[2560,128]{1,0:T(8,128)(2,1)} %pad_maximum_fusion.h0), channel_id=1, source_target_pairs={{0,2},{1,3},{2,0},{3,1},{4,6},{5,7},{6,4},{7,5},{8,10},{9,11},{10,... | collective-permute-start | bytes 1966088 | tf_op jit(solution)/shard_map/ppermute | solution.py:301
  32.0 26.4 %collective-permute-start.8 = (bf16[2560,128]{1,0:T(8,128)(2,1)}, bf16[2560,128]{1,0:T(8,128)(2,1)}, u32[]{:S(2)}, u32[]{:S(2)}) collective-permute-start(bf16[2560,128]{1,0:T(8,128)(2,1)} %pad_maximum_fusion.h0), channel_id=1, source_target_pairs={{0,1},{1,0},{2,3},{3,2},{4,5},{5,4},{6,7},{7,6},{8,9},{9,8},{10,11... | collective-permute-start | bytes 1966088 | tf_op jit(solution)/shard_map/ppermute | solution.py:301
  53.3 17.5 %copy-start.1 = (bf16[1280,3,320]{0,2,1:T(8,128)(2,1)S(1)}, bf16[1280,3,320]{0,2,1:T(8,128)(2,1)}, u32[]{:S(2)}) copy-start(bf16[1280,3,320]{0,2,1:T(8,128)(2,1)} %param.8) | copy-start | bytes 7372804
  53.3 17.5 %copy-start.13 = (f32[1280]{0:T(1024)S(1)}, f32[1280]{0:T(1024)}, u32[]{:S(2)}) copy-start(f32[1280]{0:T(1024)} %param.7) | copy-start | bytes 15364
  53.3 5.1 %collective-permute-start.9 = (bf16[2560,128]{1,0:T(8,128)(2,1)}, bf16[2560,128]{1,0:T(8,128)(2,1)S(1)}, u32[]{:S(2)}, u32[]{:S(2)}) collective-permute-start(bf16[2560,128]{1,0:T(8,128)(2,1)} %collective-permute-done.6.h2), channel_id=1, source_target_pairs={{0,1},{1,0},{2,3},{3,2},{4,5},{5,4},{6,7},{7,6},{8,9},{9,8},{10,11... | collective-permute-start | bytes 1966088 | tf_op jit(solution)/shard_map/ppermute | solution.py:301
  53.9 10.1 %collective-permute-start.7 = (bf16[3,336,128]{2,1,0:T(8,128)(2,1)S(1)}, bf16[3,336,128]{2,1,0:T(8,128)(2,1)S(1)}, u32[]{:S(2)}, u32[]{:S(2)}) collective-permute-start(bf16[3,336,128]{2,1,0:T(8,128)(2,1)S(1)} %constant_dynamic-slice_fusion), channel_id=1, source_target_pairs={{0,32},{4,36},{8,40},{12,44},{32,64},{36,68},{40,72},{44,76},{48,1... | collective-permute-start | bytes 774152 | tf_op jit(solution)/shard_map/ppermute | solution.py:310
  73.0 14.7 %copy-start.3 = (bf16[320,1280]{1,0:T(8,128)(2,1)S(1)}, bf16[320,1280]{1,0:T(8,128)(2,1)}, u32[]{:S(2)}) copy-start(bf16[320,1280]{1,0:T(8,128)(2,1)} %w_out.5) | copy-start | bytes 2457604
  73.0 21.6 %all-to-all-start.1 = ((bf16[8,416,128]{2,1,0:T(8,128)(2,1)}), bf16[8,416,128]{2,1,0:T(8,128)(2,1)}, u32[]{:S(2)}, u32[]{:S(2)}) async-start(bf16[8,416,128]{2,1,0:T(8,128)(2,1)} %copy-done.4), calls=%async_computation.1 | async-start | bytes 1703936 | tf_op jit(solution)/shard_map/all_to_all | solution.py:378
  80.7 3.6 %collective-permute-start.10 = (bf16[320,128]{1,0:T(8,128)(2,1)}, bf16[320,128]{1,0:T(8,128)(2,1)S(1)}, u32[]{:S(2)}, u32[]{:S(2)}) collective-permute-start(bf16[320,128]{1,0:T(8,128)(2,1)} %copy-done.24), channel_id=1, source_target_pairs={{0,4},{4,0},{8,12},{12,8},{16,20},{20,16},{24,28},{28,24},{1,5},{5... | collective-permute-start | bytes 245768 | tf_op jit(solution)/shard_map/ppermute | solution.py:297
  80.7 4.5 %collective-permute-start.11 = (bf16[320,128]{1,0:T(8,128)(2,1)}, bf16[320,128]{1,0:T(8,128)(2,1)S(1)}, u32[]{:S(2)}, u32[]{:S(2)}) collective-permute-start(bf16[320,128]{1,0:T(8,128)(2,1)} %copy-done.23), channel_id=1, source_target_pairs={{0,8},{4,12},{8,0},{12,4},{16,24},{20,28},{24,16},{28,20},{1,9},{5... | collective-permute-start | bytes 245768 | tf_op jit(solution)/shard_map/ppermute | solution.py:297
  80.8 6.8 %collective-permute-start.12 = (bf16[320,128]{1,0:T(8,128)(2,1)}, bf16[320,128]{1,0:T(8,128)(2,1)S(1)}, u32[]{:S(2)}, u32[]{:S(2)}) collective-permute-start(bf16[320,128]{1,0:T(8,128)(2,1)} %copy-done.22), channel_id=1, source_target_pairs={{0,12},{4,8},{8,4},{12,0},{16,28},{20,24},{24,20},{28,16},{1,13},{... | collective-permute-start | bytes 245768 | tf_op jit(solution)/shard_map/ppermute | solution.py:297
  92.7 22.3 %copy-start.9 = (f32[320,128]{1,0:T(8,128)S(1)}, f32[320,128]{1,0:T(8,128)}, u32[]{:S(2)}) copy-start(f32[320,128]{1,0:T(8,128)} %get-tuple-element.87.scale_own) | copy-start | bytes 491524
  92.7 22.3 %copy-start.10 = (bf16[320,128]{1,0:T(8,128)(2,1)S(1)}, bf16[320,128]{1,0:T(8,128)(2,1)}, u32[]{:S(2)}) copy-start(bf16[320,128]{1,0:T(8,128)(2,1)} %get-tuple-element.86.x_own) | copy-start | bytes 245764
  92.7 22.3 %copy-start.14 = (f32[8,128]{1,0:T(8,128)S(1)}, f32[8,128]{1,0:T(8,128)}, u32[]{:S(2)}) copy-start(f32[8,128]{1,0:T(8,128)} %get-tuple-element.88.inv) | copy-start | bytes 12292
  94.6 7.8 %copy-start.19 = (bf16[656,128]{1,0:T(8,128)(2,1)S(1)}, bf16[656,128]{1,0:T(8,128)(2,1)}, u32[]{:S(2)}) copy-start(bf16[656,128]{1,0:T(8,128)(2,1)} %copy-done.18) | copy-start | bytes 503812
  94.6 7.8 %copy-start.17 = (bf16[656,128]{1,0:T(8,128)(2,1)S(1)}, bf16[656,128]{1,0:T(8,128)(2,1)}, u32[]{:S(2)}) copy-start(bf16[656,128]{1,0:T(8,128)(2,1)} %copy-done.16) | copy-start | bytes 503812
  94.6 20.4 %copy-start.8 = (bf16[656,128]{1,0:T(8,128)(2,1)S(1)}, bf16[656,128]{1,0:T(8,128)(2,1)}, u32[]{:S(2)}) copy-start(bf16[656,128]{1,0:T(8,128)(2,1)} %copy-done.7) | copy-start | bytes 503812
  96.6 15.4 %all-to-all-start.2 = ((bf16[8,80,128]{2,1,0:T(8,128)(2,1)}), bf16[8,80,128]{2,1,0:T(8,128)(2,1)S(1)}, u32[]{:S(2)}, u32[]{:S(2)}) async-start(bf16[8,80,128]{2,1,0:T(8,128)(2,1)} %middle.1), calls=%async_computation.2 | async-start | bytes 327680 | tf_op jit(solution)/shard_map/all_to_all | solution.py:399
  100.1 4.0 %collective-permute-start.13 = (bf16[656,128]{1,0:T(8,128)(2,1)S(1)}, bf16[656,128]{1,0:T(8,128)(2,1)S(1)}, u32[]{:S(2)}, u32[]{:S(2)}) collective-permute-start(bf16[656,128]{1,0:T(8,128)(2,1)S(1)} %copy-done.21), channel_id=1, source_target_pairs={{0,1},{1,0},{2,3},{3,2},{4,5},{5,4},{6,7},{7,6},{8,9},{9,8},{10,11... | collective-permute-start | bytes 503816 | tf_op jit(solution)/shard_map/ppermute | solution.py:301
  102.4 5.9 %collective-permute-start.14 = (bf16[656,128]{1,0:T(8,128)(2,1)S(1)}, bf16[656,128]{1,0:T(8,128)(2,1)S(1)}, u32[]{:S(2)}, u32[]{:S(2)}) collective-permute-start(bf16[656,128]{1,0:T(8,128)(2,1)S(1)} %copy-done.19), channel_id=1, source_target_pairs={{0,2},{1,3},{2,0},{3,1},{4,6},{5,7},{6,4},{7,5},{8,10},{9,11},{10,... | collective-permute-start | bytes 503816 | tf_op jit(solution)/shard_map/ppermute | solution.py:301
  102.4 9.6 %collective-permute-start.15 = (bf16[656,128]{1,0:T(8,128)(2,1)S(1)}, bf16[656,128]{1,0:T(8,128)(2,1)S(1)}, u32[]{:S(2)}, u32[]{:S(2)}) collective-permute-start(bf16[656,128]{1,0:T(8,128)(2,1)S(1)} %copy-done.17), channel_id=1, source_target_pairs={{0,3},{1,2},{2,1},{3,0},{4,7},{5,6},{6,5},{7,4},{8,11},{9,10},{10,... | collective-permute-start | bytes 503816 | tf_op jit(solution)/shard_map/ppermute | solution.py:301
  112.8 3.1 %collective-permute-start.18 = (f32[16,128]{1,0:T(8,128)S(1)}, f32[16,128]{1,0:T(8,128)S(1)}, u32[]{:S(2)}, u32[]{:S(2)}) collective-permute-start(f32[16,128]{1,0:T(8,128)S(1)} %get-tuple-element.94.t0), channel_id=1, source_target_pairs={{0,3},{1,2},{2,1},{3,0},{4,7},{5,6},{6,5},{7,4},{8,11},{9,10},{10,... | collective-permute-start | bytes 24584 | tf_op jit(solution)/shard_map/ppermute | solution.py:301
  113.0 3.0 %collective-permute-start.17 = (f32[16,128]{1,0:T(8,128)S(1)}, f32[16,128]{1,0:T(8,128)S(1)}, u32[]{:S(2)}, u32[]{:S(2)}) collective-permute-start(f32[16,128]{1,0:T(8,128)S(1)} %get-tuple-element.94.t0), channel_id=1, source_target_pairs={{0,2},{1,3},{2,0},{3,1},{4,6},{5,7},{6,4},{7,5},{8,10},{9,11},{10,... | collective-permute-start | bytes 24584 | tf_op jit(solution)/shard_map/ppermute | solution.py:301
  114.4 1.5 %collective-permute-start.16 = (f32[16,128]{1,0:T(8,128)S(1)}, f32[16,128]{1,0:T(8,128)S(1)}, u32[]{:S(2)}, u32[]{:S(2)}) collective-permute-start(f32[16,128]{1,0:T(8,128)S(1)} %get-tuple-element.94.t0), channel_id=1, source_target_pairs={{0,1},{1,0},{2,3},{3,2},{4,5},{5,4},{6,7},{7,6},{8,9},{9,8},{10,11... | collective-permute-start | bytes 24584 | tf_op jit(solution)/shard_map/ppermute | solution.py:301
  (16 other events, 17.9 us)

commit v2 on v1

--- a/solution.py
+++ b/solution.py
@@ -93,7 +93,7 @@
                 own[4 * u + m, j * HD : j * HD + block.shape[0], :] = block
 
 
-def attention_kernel(zz, local, halo, grads, o0, o1, o2, o3, win, kn, vn, idk, es, ds, ps, dss, gk, gv, sems):
+def attention_kernel(zz, local, halo, out, grads, win, kn, vn, idk, es, ds, ps, dss, gk, gv):
     u, m = lax.div(zz[0], 4), lax.rem(zz[0], 4)
 
     @pl.when(u == 0)
@@ -161,10 +161,8 @@
         lane = slice(i * T, (i + 1) * T)
         grads[i, HD : 2 * HD, :] = (gk[:, lane] * SCALE).astype(BF16)
         grads[i, 2 * HD : 3 * HD, :] = gv[:, lane].astype(BF16)
-    o0[...] = grads[m]
-    outs = enumerate((o1, o2, o3), 1)
-    for copy in fetch(sems, *[(grads.at[jnp.bitwise_xor(m, k)], out) for k, out in outs]):
-        copy.wait()
+    for k in range(4):
+        out[k] = grads[jnp.bitwise_xor(m, k)]
 
 
 def attention(zz, local, halo):
@@ -172,8 +170,9 @@
     return call(
         attention_kernel,
         "attention",
-        [shape((4, 4 * HD, T))] + [shape((4 * HD, T))] * 4,
+        shape((4, 4 * HD, T)),
         [
+            pltpu.VMEM((4, 4 * HD, T), BF16),
             pltpu.VMEM((WIN, R, T), BF16),
             pltpu.VMEM((WIN * T, HD), BF16),
             pltpu.VMEM((WIN * T, HD), BF16),
@@ -184,16 +183,14 @@
             pltpu.VMEM(big, BF16),
             pltpu.VMEM((HD, 4 * T), F32),
             pltpu.VMEM((HD, 4 * T), F32),
-            pltpu.SemaphoreType.DMA((3,)),
         ],
         [zz],
         local,
         halo,
-        far_outs=3,
-    )
-
-
-def pieces_kernel(zz, head, b0, b1, b2, b3, proj, w, w_out, p0, p1, p2, p3, grads, parts, sems):
+    )
+
+
+def pieces_kernel(zz, head, b0, b1, b2, b3, proj, w, w_out, out, grads, parts):
     m = lax.rem(zz[0], 4)
     for k, piece in enumerate((b0, b1, b2, b3)):
         other = jnp.bitwise_xor(m, k)
@@ -212,10 +209,8 @@
         parts[j, :W, :] = out_part[j * W : (j + 1) * W, :]
         parts[j, W : 2 * W, :] = d_part[j * W : (j + 1) * W, :]
         parts[j, 2 * W :, :] = tail
-    p0[...] = parts[head[0]]
-    outs = enumerate((p1, p2, p3), 1)
-    for copy in fetch(sems, *[(parts.at[jnp.bitwise_xor(head[0], k)], out) for k, out in outs]):
-        copy.wait()
+    for k in range(4):
+        out[k] = parts[jnp.bitwise_xor(head[0], k)]
 
 
 def rows_kernel(g0, g1, g2, g3, x_own, scale_own, inv, attn_out, grad_patches):
@@ -237,10 +232,10 @@
             c[at, lane] = quarter[(2 * k + 1) * W : (2 * k + 2) * W, :]
 
 
-def weights_kernel(zz, n, c, grads, gain, w, out, g, term):
+def weights_kernel(zz, n, c, grads, w, out, g, term):
     m = lax.rem(zz[0], 4)
     for k in range(4):
-        g[:, k * T : (k + 1) * T] = grads[jnp.bitwise_xor(m, k)]
+        g[:, k * T : (k + 1) * T] = grads[k]
     left = lax.dot_general(n[...], g[: 3 * HD, :], LANES, preferred_element_type=F32)
     right = lax.dot_general(c[...], g[3 * HD :, :], LANES, preferred_element_type=F32)
     term[...] = jnp.concatenate([left, right], axis=1)
@@ -249,7 +244,7 @@
     for j in range(3):
         product = turned[j * HD : (j + 1) * HD, :] * w[times(j * HL + m, HD), :].astype(F32)
         gg = gg + jnp.sum(product, axis=0, keepdims=True)
-    rows = [gg[:, l * T : (l + 1) * T] / gain[l : l + 1, :] for l in range(10)]
+    rows = [gg[:, l * T : (l + 1) * T] for l in range(10)]
     rows = rows + [jnp.zeros((6, T), F32)]
     tail = jnp.concatenate(rows, axis=0).astype(BF16)
     for d in range(8):
@@ -268,14 +263,14 @@
         if z >= 4:
             third = pltpu.roll(third, 64, 1)
         rows = [total[20 * z : 20 * z + 20, :], total[160 + 20 * z : 180 + 20 * z, :], third]
-        out[z] = jnp.concatenate(rows + [zero, total[400:, :]], axis=0).astype(BF16)
+        out[7 - z] = jnp.concatenate(rows + [zero, total[400:, :]], axis=0).astype(BF16)
 
 
 def sums_kernel(got, qkv, out, gg):
     tail = jnp.zeros((16, T), F32)
     cols = []
     for m in range(HL):
-        total = got[m].astype(F32) + got[4 + m].astype(F32)
+        total = got[7 - m].astype(F32) + got[3 - m].astype(F32)
         cols.append(jnp.concatenate([total[20 * l : 20 * l + 20, :] for l in range(3)], axis=1))
         tail = tail + total[64:80, :]
     for j in range(3):
@@ -284,13 +279,13 @@
     gg[...] = tail
 
 
-def gain_kernel(head, t0, t1, t2, t3, out):
-    total = t0[...] + t1[...] + t2[...] + t3[...]
+def gain_kernel(head, t0, t1, t2, t3, gain, out):
+    total = (t0[...] + t1[...] + t2[...] + t3[...])[:10, :] / gain[...]
     flat = jnp.concatenate([total[l : l + 1, :] for l in range(10)], axis=1)
     for j in range(4):
         @pl.when(head[0] == j)
         def _():
-            out[...] = flat[:, j * W : (j + 1) * W]
+            out[...] = flat[0, j * W : (j + 1) * W]
 
 
 def along_z(x, by):
@@ -336,7 +331,10 @@
     )
     cot, normed = lax.optimization_barrier((cot, normed))
     cots = [along_head(cot, k) for k in range(4)]
-    quarter = jnp.concatenate([along_z(quarter, k) for k in range(4)], axis=0)
+    quarter = [quarter, along_z(quarter, 1), None, along_z(quarter, 3)]
+    quarter[3], cots = lax.optimization_barrier((quarter[3], cots))
+    quarter[2] = along_z(quarter[3], 1)
+    quarter = jnp.concatenate(quarter, axis=0)
     ids = image_ids.reshape(1, T)
     proj = call(project_kernel, "project", shape((3 * W, T)), [], [], normed, w, w_out, ids)
     own = call(
@@ -361,7 +359,8 @@
         assemble_kernel, "assemble", [shape((D, 4 * T))] * 2, [], [head], *quarters
     )
     halo, n, c = lax.optimization_barrier((halo, n, c))
-    grads, *backs = attention(zz, local, halo)
+    grads = attention(zz, local, halo)
+    backs = [grads[k] for k in range(4)]
     terms = call(
         weights_kernel,
         "weights",
@@ -371,7 +370,6 @@
         n,
         c,
         grads,
-        gain,
         w,
     )
     backs, terms = lax.optimization_barrier((backs, terms))
@@ -380,24 +378,20 @@
     pieces = call(
         pieces_kernel,
         "pieces",
-        [shape((2 * W + IDROWS, T))] * 4,
-        [
-            pltpu.VMEM((4 * W, T), BF16),
-            pltpu.VMEM((4, 2 * W + IDROWS, T), BF16),
-            pltpu.SemaphoreType.DMA((3,)),
-        ],
+        shape((4, 2 * W + IDROWS, T)),
+        [pltpu.VMEM((4 * W, T), BF16), pltpu.VMEM((4, 2 * W + IDROWS, T), BF16)],
         [zz, head],
         *backs,
         proj,
         w,
         w_out,
-        far_outs=3,
     )
     terms, pieces = lax.optimization_barrier((terms, pieces))
-    got = [along_head(p, k) for k, p in enumerate(pieces)]
+    got = [along_head(pieces[k], k) for k in range(4)]
     terms = call(middle_kernel, "middle", shape((8, 80, T)), [pltpu.VMEM((416, T), F32)], [], terms)
-    terms = lax.all_to_all(terms, "z", 0, 0, tiled=True)
-    terms, got = lax.optimization_barrier((terms, got))
+    terms = lax.all_to_all(
+        terms, "z", 0, 0, tiled=True, axis_index_groups=[list(range(7, -1, -1))]
+    )
     attn_out, grad_patches = call(
         rows_kernel,
         "rows",
@@ -418,9 +412,9 @@
         terms,
     )
     grad_gain = call(
-        gain_kernel, "gain", shape((1, W), F32), [], [head], *[along_head(gg, k) for k in range(4)]
-    )
-    return (attn_out.T, grad_patches.T, grad_w_qkv.transpose(1, 0, 2), grad_w_out.T, grad_gain.reshape(W))
+        gain_kernel, "gain", shape((W,), F32), [], [head], *[along_head(gg, k) for k in range(4)], gain
+    )
+    return (attn_out.T, grad_patches.T, grad_w_qkv.transpose(1, 0, 2), grad_w_out.T, grad_gain)
 
 
 def solution(mesh):

time: 117 us -> 110 us (0.940)
  waiting for transfers between devices: 42.8 us -> 30.2 us
  starting transfers between devices: 42.9 us -> 50 us
  Pallas kernels: 17 us -> 15.1 us
  other arithmetic: 1.49 us -> 0.05 us
  local copies, waits for them, and re-layouts: 11.5 us -> 12.9 us
    ppermute x12, starting transfers between devices: 12.1 us -> 18.7 us  [along_head(): return lax.ppermute(x, HEAD, [(i, i ^ by) for i in range(4)]) if by else x]
    ppermute x6, waiting for transfers between devices: 9.31 us -> 3.37 us  [along_z(): return lax.ppermute(x, 'z', [(i, i ^ by) for i in range(8)]) if by else x]
    all_to_all x1, waiting for transfers between devices: 20 us -> 15.6 us  [body(): local = lax.all_to_all(own, 'z', 0, 0, tiled=True)]
    ppermute x12, waiting for transfers between devices: 8.09 us -> 5.32 us  [along_head(): return lax.ppermute(x, HEAD, [(i, i ^ by) for i in range(4)]) if by else x]
    ppermute x1, waiting for transfers between devices: 3.63 us -> 0.99 us  [to_next_group(): return lax.ppermute(x, SEQ, pairs)]
    all_to_all x1, waiting for transfers between devices: 1.86 us -> 4.31 us  [body(): terms = lax.all_to_all(terms, ('y', 'xh'), 0, 0, tiled=True)]
    pallas_call x11, Pallas kernels: 17 us -> 15.1 us  [call(): pl.pallas_call(kernel, out_shape=outs, in_specs=specs, out_specs=vmem if...]
    unnamed x52 -> x44, local copies, waits for them, and re-layouts: 11.5 us -> 12.2 us
  transfers between devices with their start and end apart: 22 -> 22, of which waited for: 9 -> 10; matrix products, arithmetic and copies ran while one was open for 0% -> 0% of each run, Pallas kernels for 5% -> 5%
where the time goes in v2:
time: 110 us; the launch traced here: 109 us
  starting transfers between devices  50 us (45%)
  waiting for transfers between devices  30.2 us (27%)
  Pallas kernels  15.1 us (14%)
  local copies, waits for them, and re-layouts  12.9 us (12%)
    ppermute x12, starting transfers between devices, along_head(): return lax.ppermute(x, HEAD, [(i, i ^ by) for i in range(4)]) if by else x  18.7 us
    all_to_all x1, waiting for transfers between devices, body(): local = lax.all_to_all(own, 'z', 0, 0, tiled=True)  15.6 us
    pallas_call x11, Pallas kernels, call(): pl.pallas_call(kernel, out_shape=outs, in_specs=specs, out_specs=vmem if...  15.1 us
    unnamed x44, local copies, waits for them, and re-layouts  12.2 us
    ppermute x6, starting transfers between devices, along_z(): return lax.ppermute(x, 'z', [(i, i ^ by) for i in range(8)]) if by else x  8.81 us
    all_to_all x1, starting transfers between devices, body(): terms = lax.all_to_all(terms, ('y', 'xh'), 0, 0, tiled=True)  7.73 us
    all_to_all x1, starting transfers between devices, body(): local = lax.all_to_all(own, 'z', 0, 0, tiled=True)  6.07 us
    ppermute x12, waiting for transfers between devices, along_head(): return lax.ppermute(x, HEAD, [(i, i ^ by) for i in range(4)]) if by else x  5.32 us
  transfers between devices with their start and end apart: 22, of which 10 were waited for; matrix products, arithmetic and copies ran while one was open for 0% of the time, Pallas kernels for 5%

profile of v2, /device:TPU:1, one launch (start us, length us, event | category | flops | bytes accessed | tf_op | source)
XLA Modules:
  0.0 109.2 jit_solution(17105537566871749886)
XLA Ops:
  0.6 2.2 %norm.1 = (bf16[1280,128]{1,0:T(8,128)(2,1)}, bf16[640,128]{1,0:T(8,128)(2,1)}, bf16[320,128]{1,0:T(8,128)(2,1)}, f32[320,128]{1,0:T(8,128)}, f32[8,128]{1,0:T(8,128)}) custom-call(s32[1]{0:T(128)} %bitcast.1.head, bf16[128,1280]{1,0:T(8,128)(2,1)} %patches_far.1, f32[10,128]{1,0:T(8,128)} %bitcast.36, bf16[320,128]{1,0:T(8,128)(2,1)} %bitcast.31), custom_call_target="tpu_custom_call" | custom-call | flops 1000 | bytes 1000 | tf_op jit(solution)/shard_map/norm/pallas_call | solution.py:32
  2.9 5.3 %collective-permute-start = (bf16[640,128]{1,0:T(8,128)(2,1)}, bf16[640,128]{1,0:T(8,128)(2,1)S(1)}, u32[]{:S(2)}, u32[]{:S(2)}) collective-permute-start(bf16[640,128]{1,0:T(8,128)(2,1)} %get-tuple-element.38), channel_id=1, source_target_pairs={{0,12},{4,8},{8,4},{12,0},{16,28},{20,24},{24,20},{28,16},{1,13},{... | collective-permute-start | bytes 491528 | tf_op jit(solution)/shard_map/ppermute | solution.py:292
  8.1 2.1 %collective-permute-start.3 = (bf16[320,128]{1,0:T(8,128)(2,1)}, bf16[320,128]{1,0:T(8,128)(2,1)S(1)}, u32[]{:S(2)}, u32[]{:S(2)}) collective-permute-start(bf16[320,128]{1,0:T(8,128)(2,1)} %bitcast.32), channel_id=1, source_target_pairs={{0,3},{1,2},{2,1},{3,0},{4,7},{5,6},{6,5},{7,4},{8,11},{9,10},{10,... | collective-permute-start | bytes 245768 | tf_op jit(solution)/shard_map/ppermute | solution.py:296
  10.6 3.1 %collective-permute-done.3.c3 = bf16[320,128]{1,0:T(8,128)(2,1)S(1)} collective-permute-done((bf16[320,128]{1,0:T(8,128)(2,1)}, bf16[320,128]{1,0:T(8,128)(2,1)S(1)}, u32[]{:S(2)}, u32[]{:S(2)}) %collective-permute-start.3) | collective-permute-done | bytes 81952 | tf_op jit(solution)/shard_map/ppermute | solution.py:296
  13.7 1.7 %collective-permute-done.2.c2 = bf16[320,128]{1,0:T(8,128)(2,1)S(1)} collective-permute-done((bf16[320,128]{1,0:T(8,128)(2,1)}, bf16[320,128]{1,0:T(8,128)(2,1)S(1)}, u32[]{:S(2)}, u32[]{:S(2)}) %collective-permute-start.2) | collective-permute-done | bytes 81952 | tf_op jit(solution)/shard_map/ppermute | solution.py:296
  15.4 1.7 %copy-done = bf16[1280,3,320]{0,2,1:T(8,128)(2,1)S(1)} copy-done((bf16[1280,3,320]{0,2,1:T(8,128)(2,1)S(1)}, bf16[1280,3,320]{0,2,1:T(8,128)(2,1)}, u32[]{:S(2)}) %copy-start) | copy-done | bytes 2457624
  17.1 1.1 %copy-done.2 = bf16[320,1280]{1,0:T(8,128)(2,1)S(1)} copy-done((bf16[320,1280]{1,0:T(8,128)(2,1)S(1)}, bf16[320,1280]{1,0:T(8,128)(2,1)}, u32[]{:S(2)}) %copy-start.2) | copy-done | bytes 819224
  18.2 1.0 copy-done.13
  20.7 1.3 %payload.1 = bf16[8,336,128]{2,1,0:T(8,128)(2,1)} custom-call(s32[1]{0:T(128)} %bitcast.1.head, bf16[320,128]{1,0:T(8,128)(2,1)S(1)} %bitcast.35, bf16[320,128]{1,0:T(8,128)(2,1)S(1)} %collective-permute-done.1.c1, bf16[320,128]{1,0:T(8,128)(2,1)S(1)} %collective-permute-done.2.c2, bf16[320,128]{1,0:T(8,128)(2,1)S(1)} %collective-permute-done.3.c3, ...), custom_call_target="tpu_custom_call" | custom-call | flops 1000 | bytes 1000 | tf_op jit(solution)/shard_map/payload/pallas_call | solution.py:32
  22.1 6.1 %all-to-all-start = ((bf16[8,336,128]{2,1,0:T(8,128)(2,1)}), bf16[8,336,128]{2,1,0:T(8,128)(2,1)S(1)}, u32[]{:S(2)}, u32[]{:S(2)}) async-start(bf16[8,336,128]{2,1,0:T(8,128)(2,1)} %payload.1), calls=%async_computation | async-start | bytes 1376256 | tf_op jit(solution)/shard_map/all_to_all | solution.py:352
  28.2 1.1 %collective-permute-start.6 = (bf16[2560,128]{1,0:T(8,128)(2,1)S(1)}, bf16[2560,128]{1,0:T(8,128)(2,1)S(1)}, u32[]{:S(2)}, u32[]{:S(2)}) collective-permute-start(bf16[2560,128]{1,0:T(8,128)(2,1)S(1)} %pad_maximum_fusion.h0), channel_id=1, source_target_pairs={{0,2},{1,3},{2,0},{3,1},{4,6},{5,7},{6,4},{7,5},{8,10},{9,11},{10,... | collective-permute-start | bytes 1966088 | tf_op jit(solution)/shard_map/ppermute | solution.py:296
  29.3 2.5 %collective-permute-start.8 = (bf16[2560,128]{1,0:T(8,128)(2,1)S(1)}, bf16[2560,128]{1,0:T(8,128)(2,1)S(1)}, u32[]{:S(2)}, u32[]{:S(2)}) collective-permute-start(bf16[2560,128]{1,0:T(8,128)(2,1)S(1)} %pad_maximum_fusion.h0), channel_id=1, source_target_pairs={{0,1},{1,0},{2,3},{3,2},{4,5},{5,4},{6,7},{7,6},{8,9},{9,8},{10,11... | collective-permute-start | bytes 1966088 | tf_op jit(solution)/shard_map/ppermute | solution.py:296
  31.8 15.6 %all-to-all-done.local = bf16[8,336,128]{2,1,0:T(8,128)(2,1)S(1)} async-done(((bf16[8,336,128]{2,1,0:T(8,128)(2,1)}), bf16[8,336,128]{2,1,0:T(8,128)(2,1)S(1)}, u32[]{:S(2)}, u32[]{:S(2)}) %all-to-all-start) | async-done | bytes 688160 | tf_op jit(solution)/shard_map/all_to_all | solution.py:352
  47.4 2.8 %collective-permute-start.9 = (bf16[2560,128]{1,0:T(8,128)(2,1)S(1)}, bf16[2560,128]{1,0:T(8,128)(2,1)S(1)}, u32[]{:S(2)}, u32[]{:S(2)}) collective-permute-start(bf16[2560,128]{1,0:T(8,128)(2,1)S(1)} %collective-permute-done.6.h2), channel_id=1, source_target_pairs={{0,1},{1,0},{2,3},{3,2},{4,5},{5,4},{6,7},{7,6},{8,9},{9,8},{10,11... | collective-permute-start | bytes 1966088 | tf_op jit(solution)/shard_map/ppermute | solution.py:296
  51.1 4.6 %collective-permute-start.7 = (bf16[3,336,128]{2,1,0:T(8,128)(2,1)S(1)}, bf16[3,336,128]{2,1,0:T(8,128)(2,1)S(1)}, u32[]{:S(2)}, u32[]{:S(2)}) collective-permute-start(bf16[3,336,128]{2,1,0:T(8,128)(2,1)S(1)} %constant_dynamic-slice_fusion), channel_id=1, source_target_pairs={{0,32},{4,36},{8,40},{12,44},{32,64},{36,68},{40,72},{44,76},{48,1... | collective-permute-start | bytes 774152 | tf_op jit(solution)/shard_map/ppermute | solution.py:305
  56.6 1.1 copy-done.8
  57.7 1.1 copy-done.10
  58.8 1.1 copy-done.12
  60.3 1.0 collective-permute-done.7.halo
  61.3 3.9 %attention.1.grads = bf16[4,320,128]{2,1,0:T(8,128)(2,1)S(1)} custom-call(s32[1]{0:T(128)} %bitcast.zz, bf16[8,336,128]{2,1,0:T(8,128)(2,1)S(1)} %all-to-all-done.local, bf16[3,336,128]{2,1,0:T(8,128)(2,1)S(1)} %collective-permute-done.7.halo), custom_call_target="tpu_custom_call" | custom-call | flops 1000 | bytes 1000 | tf_op jit(solution)/shard_map/attention/pallas_call | solution.py:32
  66.0 1.3 %weights.1 = bf16[8,416,128]{2,1,0:T(8,128)(2,1)S(1)} custom-call(s32[1]{0:T(128)} %bitcast.zz, bf16[1280,512]{1,0:T(8,128)(2,1)S(1)} %get-tuple-element.54.n, bf16[1280,512]{1,0:T(8,128)(2,1)S(1)} %get-tuple-element.55.c, bf16[4,320,128]{2,1,0:T(8,128)(2,1)S(1)} %attention.1.grads, bf16[960,1280]{1,0:T(8,128)(2,1)S(1)} %bitcast.29), custom_call_target="tpu_custom_call" | custom-call | flops 1000 | bytes 1000 | tf_op jit(solution)/shard_map/weights/pallas_call | solution.py:32
  68.2 7.7 %all-to-all-start.1 = ((bf16[8,416,128]{2,1,0:T(8,128)(2,1)}), bf16[8,416,128]{2,1,0:T(8,128)(2,1)}, u32[]{:S(2)}, u32[]{:S(2)}) async-start(bf16[8,416,128]{2,1,0:T(8,128)(2,1)} %copy-done.4), calls=%async_computation.1 | async-start | bytes 1703936 | tf_op jit(solution)/shard_map/all_to_all | solution.py:376
  76.2 3.3 %collective-permute-start.12 = (bf16[320,128]{1,0:T(8,128)(2,1)}, bf16[320,128]{1,0:T(8,128)(2,1)S(1)}, u32[]{:S(2)}, u32[]{:S(2)}) collective-permute-start(bf16[320,128]{1,0:T(8,128)(2,1)} %get-tuple-element.60), channel_id=1, source_target_pairs={{0,12},{4,8},{8,4},{12,0},{16,28},{20,24},{24,20},{28,16},{1,13},{... | collective-permute-start | bytes 245768 | tf_op jit(solution)/shard_map/ppermute | solution.py:292
  79.5 1.1 %collective-permute-done.11.b2 = bf16[320,128]{1,0:T(8,128)(2,1)S(1)} collective-permute-done((bf16[320,128]{1,0:T(8,128)(2,1)}, bf16[320,128]{1,0:T(8,128)(2,1)S(1)}, u32[]{:S(2)}, u32[]{:S(2)}) %collective-permute-start.11) | collective-permute-done | bytes 81952 | tf_op jit(solution)/shard_map/ppermute | solution.py:292
  80.6 2.2 %collective-permute-done.12.b3 = bf16[320,128]{1,0:T(8,128)(2,1)S(1)} collective-permute-done((bf16[320,128]{1,0:T(8,128)(2,1)}, bf16[320,128]{1,0:T(8,128)(2,1)S(1)}, u32[]{:S(2)}, u32[]{:S(2)}) %collective-permute-start.12) | collective-permute-done | bytes 81952 | tf_op jit(solution)/shard_map/ppermute | solution.py:292
  85.5 4.3 %all-to-all-done.1.got = bf16[8,416,128]{2,1,0:T(8,128)(2,1)} async-done(((bf16[8,416,128]{2,1,0:T(8,128)(2,1)}), bf16[8,416,128]{2,1,0:T(8,128)(2,1)}, u32[]{:S(2)}, u32[]{:S(2)}) %all-to-all-start.1) | async-done | bytes 852000 | tf_op jit(solution)/shard_map/all_to_all | solution.py:376
  89.8 2.0 %middle.1 = bf16[8,80,128]{2,1,0:T(8,128)(2,1)} custom-call(bf16[8,416,128]{2,1,0:T(8,128)(2,1)} %all-to-all-done.1.got), custom_call_target="tpu_custom_call" | custom-call | flops 1000 | bytes 1000 | tf_op jit(solution)/shard_map/middle/pallas_call | solution.py:32
  91.8 4.1 %all-to-all-start.2 = ((bf16[8,80,128]{2,1,0:T(8,128)(2,1)}), bf16[8,80,128]{2,1,0:T(8,128)(2,1)S(1)}, u32[]{:S(2)}, u32[]{:S(2)}) async-start(bf16[8,80,128]{2,1,0:T(8,128)(2,1)} %middle.1), calls=%async_computation.2 | async-start | bytes 327680 | tf_op jit(solution)/shard_map/all_to_all | solution.py:392
  96.0 3.1 %collective-permute-start.15 = (bf16[656,128]{1,0:T(8,128)(2,1)S(1)}, bf16[656,128]{1,0:T(8,128)(2,1)S(1)}, u32[]{:S(2)}, u32[]{:S(2)}) collective-permute-start(bf16[656,128]{1,0:T(8,128)(2,1)S(1)} %get-tuple-element.71), channel_id=1, source_target_pairs={{0,3},{1,2},{2,1},{3,0},{4,7},{5,6},{6,5},{7,4},{8,11},{9,10},{10,... | collective-permute-start | bytes 503816 | tf_op jit(solution)/shard_map/ppermute | solution.py:296
  99.1 1.1 %collective-permute-start.14 = (bf16[656,128]{1,0:T(8,128)(2,1)S(1)}, bf16[656,128]{1,0:T(8,128)(2,1)S(1)}, u32[]{:S(2)}, u32[]{:S(2)}) collective-permute-start(bf16[656,128]{1,0:T(8,128)(2,1)S(1)} %get-tuple-element.72), channel_id=1, source_target_pairs={{0,2},{1,3},{2,0},{3,1},{4,6},{5,7},{6,4},{7,5},{8,10},{9,11},{10,... | collective-permute-start | bytes 503816 | tf_op jit(solution)/shard_map/ppermute | solution.py:296
  101.7 4.3 %collective-permute-start.18 = (f32[16,128]{1,0:T(8,128)S(1)}, f32[16,128]{1,0:T(8,128)S(1)}, u32[]{:S(2)}, u32[]{:S(2)}) collective-permute-start(f32[16,128]{1,0:T(8,128)S(1)} %get-tuple-element.70.t0), channel_id=1, source_target_pairs={{0,3},{1,2},{2,1},{3,0},{4,7},{5,6},{6,5},{7,4},{8,11},{9,10},{10,... | collective-permute-start | bytes 24584 | tf_op jit(solution)/shard_map/ppermute | solution.py:296
  106.0 1.2 %collective-permute-start.17 = (f32[16,128]{1,0:T(8,128)S(1)}, f32[16,128]{1,0:T(8,128)S(1)}, u32[]{:S(2)}, u32[]{:S(2)}) collective-permute-start(f32[16,128]{1,0:T(8,128)S(1)} %get-tuple-element.70.t0), channel_id=1, source_target_pairs={{0,2},{1,3},{2,0},{3,1},{4,6},{5,7},{6,4},{7,5},{8,10},{9,11},{10,... | collective-permute-start | bytes 24584 | tf_op jit(solution)/shard_map/ppermute | solution.py:296
  (71 shorter events, 12.2 us)
Async XLA Ops:
  2.9 12.5 %collective-permute-start = (bf16[640,128]{1,0:T(8,128)(2,1)}, bf16[640,128]{1,0:T(8,128)(2,1)S(1)}, u32[]{:S(2)}, u32[]{:S(2)}) collective-permute-start(bf16[640,128]{1,0:T(8,128)(2,1)} %get-tuple-element.38), channel_id=1, source_target_pairs={{0,12},{4,8},{8,4},{12,0},{16,28},{20,24},{24,20},{28,16},{1,13},{... | collective-permute-start | bytes 491528 | tf_op jit(solution)/shard_map/ppermute | solution.py:292
  8.1 5.6 %collective-permute-start.3 = (bf16[320,128]{1,0:T(8,128)(2,1)}, bf16[320,128]{1,0:T(8,128)(2,1)S(1)}, u32[]{:S(2)}, u32[]{:S(2)}) collective-permute-start(bf16[320,128]{1,0:T(8,128)(2,1)} %bitcast.32), channel_id=1, source_target_pairs={{0,3},{1,2},{2,1},{3,0},{4,7},{5,6},{6,5},{7,4},{8,11},{9,10},{10,... | collective-permute-start | bytes 245768 | tf_op jit(solution)/shard_map/ppermute | solution.py:296
  10.2 5.2 %collective-permute-start.2 = (bf16[320,128]{1,0:T(8,128)(2,1)}, bf16[320,128]{1,0:T(8,128)(2,1)S(1)}, u32[]{:S(2)}, u32[]{:S(2)}) collective-permute-start(bf16[320,128]{1,0:T(8,128)(2,1)} %bitcast.33), channel_id=1, source_target_pairs={{0,2},{1,3},{2,0},{3,1},{4,6},{5,7},{6,4},{7,5},{8,10},{9,11},{10,... | collective-permute-start | bytes 245768 | tf_op jit(solution)/shard_map/ppermute | solution.py:296
  10.4 4.9 %collective-permute-start.1 = (bf16[320,128]{1,0:T(8,128)(2,1)}, bf16[320,128]{1,0:T(8,128)(2,1)S(1)}, u32[]{:S(2)}, u32[]{:S(2)}) collective-permute-start(bf16[320,128]{1,0:T(8,128)(2,1)} %bitcast.34), channel_id=1, source_target_pairs={{0,1},{1,0},{2,3},{3,2},{4,5},{5,4},{6,7},{7,6},{8,9},{9,8},{10,11... | collective-permute-start | bytes 245768 | tf_op jit(solution)/shard_map/ppermute | solution.py:296
  10.6 11.4 %collective-permute-start.4 = (bf16[640,128]{1,0:T(8,128)(2,1)}, bf16[640,128]{1,0:T(8,128)(2,1)S(1)}, u32[]{:S(2)}, u32[]{:S(2)}) collective-permute-start(bf16[640,128]{1,0:T(8,128)(2,1)} %get-tuple-element.38), channel_id=1, source_target_pairs={{0,4},{4,0},{8,12},{12,8},{16,20},{20,16},{24,28},{28,24},{1,5},{5... | collective-permute-start | bytes 491528 | tf_op jit(solution)/shard_map/ppermute | solution.py:292
  15.4 6.7 %collective-permute-start.5 = (bf16[640,128]{1,0:T(8,128)(2,1)S(1)}, bf16[640,128]{1,0:T(8,128)(2,1)S(1)}, u32[]{:S(2)}, u32[]{:S(2)}) collective-permute-start(bf16[640,128]{1,0:T(8,128)(2,1)S(1)} %collective-permute-done), channel_id=1, source_target_pairs={{0,4},{4,0},{8,12},{12,8},{16,20},{20,16},{24,28},{28,24},{1,5},{5... | collective-permute-start | bytes 491528 | tf_op jit(solution)/shard_map/ppermute | solution.py:292
  15.4 1.7 %copy-start = (bf16[1280,3,320]{0,2,1:T(8,128)(2,1)S(1)}, bf16[1280,3,320]{0,2,1:T(8,128)(2,1)}, u32[]{:S(2)}) copy-start(bf16[1280,3,320]{0,2,1:T(8,128)(2,1)} %param.8) | copy-start | bytes 7372804
  20.7 1.3 %copy-start.21 = (bf16[640,128]{1,0:T(8,128)(2,1)S(1)}, bf16[640,128]{1,0:T(8,128)(2,1)}, u32[]{:S(2)}) copy-start(bf16[640,128]{1,0:T(8,128)(2,1)} %get-tuple-element.38) | copy-start | bytes 491524
  22.1 33.7 %copy-start.7 = (bf16[2560,128]{1,0:T(8,128)(2,1)}, bf16[2560,128]{1,0:T(8,128)(2,1)S(1)}, u32[]{:S(2)}) copy-start(bf16[2560,128]{1,0:T(8,128)(2,1)S(1)} %pad_maximum_fusion.h0) | copy-start | bytes 1966084
  22.1 25.3 %all-to-all-start = ((bf16[8,336,128]{2,1,0:T(8,128)(2,1)}), bf16[8,336,128]{2,1,0:T(8,128)(2,1)S(1)}, u32[]{:S(2)}, u32[]{:S(2)}) async-start(bf16[8,336,128]{2,1,0:T(8,128)(2,1)} %payload.1), calls=%async_computation | async-start | bytes 1376256 | tf_op jit(solution)/shard_map/all_to_all | solution.py:352
  28.2 19.3 %collective-permute-start.6 = (bf16[2560,128]{1,0:T(8,128)(2,1)S(1)}, bf16[2560,128]{1,0:T(8,128)(2,1)S(1)}, u32[]{:S(2)}, u32[]{:S(2)}) collective-permute-start(bf16[2560,128]{1,0:T(8,128)(2,1)S(1)} %pad_maximum_fusion.h0), channel_id=1, source_target_pairs={{0,2},{1,3},{2,0},{3,1},{4,6},{5,7},{6,4},{7,5},{8,10},{9,11},{10,... | collective-permute-start | bytes 1966088 | tf_op jit(solution)/shard_map/ppermute | solution.py:296
  29.3 26.4 %collective-permute-start.8 = (bf16[2560,128]{1,0:T(8,128)(2,1)S(1)}, bf16[2560,128]{1,0:T(8,128)(2,1)S(1)}, u32[]{:S(2)}, u32[]{:S(2)}) collective-permute-start(bf16[2560,128]{1,0:T(8,128)(2,1)S(1)} %pad_maximum_fusion.h0), channel_id=1, source_target_pairs={{0,1},{1,0},{2,3},{3,2},{4,5},{5,4},{6,7},{7,6},{8,9},{9,8},{10,11... | collective-permute-start | bytes 1966088 | tf_op jit(solution)/shard_map/ppermute | solution.py:296
  47.4 9.2 %collective-permute-start.9 = (bf16[2560,128]{1,0:T(8,128)(2,1)S(1)}, bf16[2560,128]{1,0:T(8,128)(2,1)S(1)}, u32[]{:S(2)}, u32[]{:S(2)}) collective-permute-start(bf16[2560,128]{1,0:T(8,128)(2,1)S(1)} %collective-permute-done.6.h2), channel_id=1, source_target_pairs={{0,1},{1,0},{2,3},{3,2},{4,5},{5,4},{6,7},{7,6},{8,9},{9,8},{10,11... | collective-permute-start | bytes 1966088 | tf_op jit(solution)/shard_map/ppermute | solution.py:296
  51.1 10.2 %collective-permute-start.7 = (bf16[3,336,128]{2,1,0:T(8,128)(2,1)S(1)}, bf16[3,336,128]{2,1,0:T(8,128)(2,1)S(1)}, u32[]{:S(2)}, u32[]{:S(2)}) collective-permute-start(bf16[3,336,128]{2,1,0:T(8,128)(2,1)S(1)} %constant_dynamic-slice_fusion), channel_id=1, source_target_pairs={{0,32},{4,36},{8,40},{12,44},{32,64},{36,68},{40,72},{44,76},{48,1... | collective-permute-start | bytes 774152 | tf_op jit(solution)/shard_map/ppermute | solution.py:305
  59.9 6.1 %copy-start.1 = (bf16[1280,3,320]{0,2,1:T(8,128)(2,1)S(1)}, bf16[1280,3,320]{0,2,1:T(8,128)(2,1)}, u32[]{:S(2)}) copy-start(bf16[1280,3,320]{0,2,1:T(8,128)(2,1)} %param.8) | copy-start | bytes 7372804
  68.2 14.6 %copy-start.3 = (bf16[320,1280]{1,0:T(8,128)(2,1)S(1)}, bf16[320,1280]{1,0:T(8,128)(2,1)}, u32[]{:S(2)}) copy-start(bf16[320,1280]{1,0:T(8,128)(2,1)} %w_out.5) | copy-start | bytes 2457604
  68.2 21.6 %all-to-all-start.1 = ((bf16[8,416,128]{2,1,0:T(8,128)(2,1)}), bf16[8,416,128]{2,1,0:T(8,128)(2,1)}, u32[]{:S(2)}, u32[]{:S(2)}) async-start(bf16[8,416,128]{2,1,0:T(8,128)(2,1)} %copy-done.4), calls=%async_computation.1 | async-start | bytes 1703936 | tf_op jit(solution)/shard_map/all_to_all | solution.py:376
  75.9 3.6 %collective-permute-start.10 = (bf16[320,128]{1,0:T(8,128)(2,1)}, bf16[320,128]{1,0:T(8,128)(2,1)S(1)}, u32[]{:S(2)}, u32[]{:S(2)}) collective-permute-start(bf16[320,128]{1,0:T(8,128)(2,1)} %get-tuple-element.58), channel_id=1, source_target_pairs={{0,4},{4,0},{8,12},{12,8},{16,20},{20,16},{24,28},{28,24},{1,5},{5... | collective-permute-start | bytes 245768 | tf_op jit(solution)/shard_map/ppermute | solution.py:292
  76.2 4.5 %collective-permute-start.11 = (bf16[320,128]{1,0:T(8,128)(2,1)}, bf16[320,128]{1,0:T(8,128)(2,1)S(1)}, u32[]{:S(2)}, u32[]{:S(2)}) collective-permute-start(bf16[320,128]{1,0:T(8,128)(2,1)} %get-tuple-element.59), channel_id=1, source_target_pairs={{0,8},{4,12},{8,0},{12,4},{16,24},{20,28},{24,16},{28,20},{1,9},{5... | collective-permute-start | bytes 245768 | tf_op jit(solution)/shard_map/ppermute | solution.py:292
  76.2 6.7 %collective-permute-start.12 = (bf16[320,128]{1,0:T(8,128)(2,1)}, bf16[320,128]{1,0:T(8,128)(2,1)S(1)}, u32[]{:S(2)}, u32[]{:S(2)}) collective-permute-start(bf16[320,128]{1,0:T(8,128)(2,1)} %get-tuple-element.60), channel_id=1, source_target_pairs={{0,12},{4,8},{8,4},{12,0},{16,28},{20,24},{24,20},{28,16},{1,13},{... | collective-permute-start | bytes 245768 | tf_op jit(solution)/shard_map/ppermute | solution.py:292
  85.5 22.2 %copy-start.16 = (f32[320,128]{1,0:T(8,128)S(1)}, f32[320,128]{1,0:T(8,128)}, u32[]{:S(2)}) copy-start(f32[320,128]{1,0:T(8,128)} %get-tuple-element.63.scale_own) | copy-start | bytes 491524
  85.5 22.2 %copy-start.17 = (bf16[320,128]{1,0:T(8,128)(2,1)S(1)}, bf16[320,128]{1,0:T(8,128)(2,1)}, u32[]{:S(2)}) copy-start(bf16[320,128]{1,0:T(8,128)(2,1)} %get-tuple-element.62.x_own) | copy-start | bytes 245764
  85.5 22.2 %copy-start.19 = (f32[8,128]{1,0:T(8,128)S(1)}, f32[8,128]{1,0:T(8,128)}, u32[]{:S(2)}) copy-start(f32[8,128]{1,0:T(8,128)} %get-tuple-element.64.inv) | copy-start | bytes 12292
  89.8 6.1 %copy-start.6 = (bf16[4,656,128]{2,1,0:T(8,128)(2,1)S(1)}, bf16[4,656,128]{2,1,0:T(8,128)(2,1)}, u32[]{:S(2)}) copy-start(bf16[4,656,128]{2,1,0:T(8,128)(2,1)} %copy-done.5) | copy-start | bytes 2015236
  91.8 16.7 %copy-start.18 = (f32[1280]{0:T(1024)S(1)}, f32[1280]{0:T(1024)}, u32[]{:S(2)}) copy-start(f32[1280]{0:T(1024)} %param.7) | copy-start | bytes 15364
  91.8 9.1 %all-to-all-start.2 = ((bf16[8,80,128]{2,1,0:T(8,128)(2,1)}), bf16[8,80,128]{2,1,0:T(8,128)(2,1)S(1)}, u32[]{:S(2)}, u32[]{:S(2)}) async-start(bf16[8,80,128]{2,1,0:T(8,128)(2,1)} %middle.1), calls=%async_computation.2 | async-start | bytes 327680 | tf_op jit(solution)/shard_map/all_to_all | solution.py:392
  96.0 11.2 %collective-permute-start.15 = (bf16[656,128]{1,0:T(8,128)(2,1)S(1)}, bf16[656,128]{1,0:T(8,128)(2,1)S(1)}, u32[]{:S(2)}, u32[]{:S(2)}) collective-permute-start(bf16[656,128]{1,0:T(8,128)(2,1)S(1)} %get-tuple-element.71), channel_id=1, source_target_pairs={{0,3},{1,2},{2,1},{3,0},{4,7},{5,6},{6,5},{7,4},{8,11},{9,10},{10,... | collective-permute-start | bytes 503816 | tf_op jit(solution)/shard_map/ppermute | solution.py:296
  99.1 8.5 %collective-permute-start.14 = (bf16[656,128]{1,0:T(8,128)(2,1)S(1)}, bf16[656,128]{1,0:T(8,128)(2,1)S(1)}, u32[]{:S(2)}, u32[]{:S(2)}) collective-permute-start(bf16[656,128]{1,0:T(8,128)(2,1)S(1)} %get-tuple-element.72), channel_id=1, source_target_pairs={{0,2},{1,3},{2,0},{3,1},{4,6},{5,7},{6,4},{7,5},{8,10},{9,11},{10,... | collective-permute-start | bytes 503816 | tf_op jit(solution)/shard_map/ppermute | solution.py:296
  100.2 7.4 %collective-permute-start.13 = (bf16[656,128]{1,0:T(8,128)(2,1)S(1)}, bf16[656,128]{1,0:T(8,128)(2,1)S(1)}, u32[]{:S(2)}, u32[]{:S(2)}) collective-permute-start(bf16[656,128]{1,0:T(8,128)(2,1)S(1)} %get-tuple-element.73), channel_id=1, source_target_pairs={{0,1},{1,0},{2,3},{3,2},{4,5},{5,4},{6,7},{7,6},{8,9},{9,8},{10,11... | collective-permute-start | bytes 503816 | tf_op jit(solution)/shard_map/ppermute | solution.py:296
  101.7 6.7 %collective-permute-start.18 = (f32[16,128]{1,0:T(8,128)S(1)}, f32[16,128]{1,0:T(8,128)S(1)}, u32[]{:S(2)}, u32[]{:S(2)}) collective-permute-start(f32[16,128]{1,0:T(8,128)S(1)} %get-tuple-element.70.t0), channel_id=1, source_target_pairs={{0,3},{1,2},{2,1},{3,0},{4,7},{5,6},{6,5},{7,4},{8,11},{9,10},{10,... | collective-permute-start | bytes 24584 | tf_op jit(solution)/shard_map/ppermute | solution.py:296
  106.0 2.5 %collective-permute-start.17 = (f32[16,128]{1,0:T(8,128)S(1)}, f32[16,128]{1,0:T(8,128)S(1)}, u32[]{:S(2)}, u32[]{:S(2)}) collective-permute-start(f32[16,128]{1,0:T(8,128)S(1)} %get-tuple-element.70.t0), channel_id=1, source_target_pairs={{0,2},{1,3},{2,0},{3,1},{4,6},{5,7},{6,4},{7,5},{8,10},{9,11},{10,... | collective-permute-start | bytes 24584 | tf_op jit(solution)/shard_map/ppermute | solution.py:296
  107.2 1.3 %collective-permute-start.16 = (f32[16,128]{1,0:T(8,128)S(1)}, f32[16,128]{1,0:T(8,128)S(1)}, u32[]{:S(2)}, u32[]{:S(2)}) collective-permute-start(f32[16,128]{1,0:T(8,128)S(1)} %get-tuple-element.70.t0), channel_id=1, source_target_pairs={{0,1},{1,0},{2,3},{3,2},{4,5},{5,4},{6,7},{7,6},{8,9},{9,8},{10,11... | collective-permute-start | bytes 24584 | tf_op jit(solution)/shard_map/ppermute | solution.py:296
  (12 other events, 11.3 us)

commit v3 on v2

--- a/solution.py
+++ b/solution.py
@@ -80,7 +80,7 @@
     proj[...] = jnp.dot(w[...], normed[...], preferred_element_type=F32).astype(BF16)
 
 
-def payload_kernel(head, c0, c1, c2, c3, proj, w_out, ids, own, cot):
+def payload_kernel(head, zz, c0, c1, c2, c3, proj, w_out, ids, e0, e1, e2, e3, own, cot):
     for k, piece in enumerate((c0, c1, c2, c3)):
         cot[times(jnp.bitwise_xor(head[0], k), W), :] = piece[...]
     d_ctx = jnp.dot(w_out[...], cot[...], preferred_element_type=F32).astype(BF16)
@@ -88,31 +88,42 @@
     for m in range(HL):
         rows = [proj[j * W + m * HD : j * W + (m + 1) * HD, :] for j in range(3)]
         rows = rows + [d_ctx[m * HD : (m + 1) * HD, :], id_rows]
-        for u in range(2):
-            for j, block in enumerate(rows):
-                own[4 * u + m, j * HD : j * HD + block.shape[0], :] = block
-
-
-def attention_kernel(zz, local, halo, out, grads, win, kn, vn, idk, es, ds, ps, dss, gk, gv):
+        for j, block in enumerate(rows):
+            own[m, j * HD : j * HD + block.shape[0], :] = block
+    m = lax.rem(zz[0], 4)
+    for k, out in enumerate((e0, e1, e2, e3)):
+        out[...] = own[jnp.bitwise_xor(m, k)]
+
+
+def near_kernel(zz, r4, r5, r6, r7, out, far):
+    for i, block in enumerate((r4, r5, r6, r7)):
+        far[i] = block[...]
+    first = jnp.where(zz[0] < 4, 5, 0)
+    for i in range(3):
+        out[i] = far[jnp.bitwise_xor(zz[0], first + i) - 4]
+
+
+def attention_kernel(zz, r0, r1, r2, r3, r4, r5, r6, r7, halo, out, grads, win, kn, vn, idk, es, ds, ps, dss, gk, gv):
     u, m = lax.div(zz[0], 4), lax.rem(zz[0], 4)
+
+    for k, block in enumerate((r0, r1, r2, r3, r4, r5, r6, r7)):
+        win[jnp.bitwise_xor(zz[0], k) + jnp.where(u == 0, 4, 0)] = block[...]
 
     @pl.when(u == 0)
     def _():
-        win[:3] = halo[...]
-        win[3:] = local[:7]
+        win[1:4] = halo[...]
 
     @pl.when(u == 1)
     def _():
-        win[:7] = local[1:]
-        win[7:] = halo[...]
+        win[8:11] = halo[...]
 
     def rows(c, j):
-        return win[c, j * HD : (j + 1) * HD, :]
+        return win[1 + c, j * HD : (j + 1) * HD, :]
 
     def side(first, last, j):
         return jnp.concatenate([rows(c, j) for c in range(first, last)], axis=1)
 
-    ids = [win[c, 4 * HD : 4 * HD + 1, :].astype(F32) for c in range(WIN)]
+    ids = [win[1 + c, 4 * HD : 4 * HD + 1, :].astype(F32) for c in range(WIN)]
     for c in range(WIN):
         at = slice(c * T, (c + 1) * T)
         idk[at, :] = jnp.transpose(jnp.broadcast_to(ids[c], (2 * T, T)))
@@ -165,7 +176,7 @@
         out[k] = grads[jnp.bitwise_xor(m, k)]
 
 
-def attention(zz, local, halo):
+def attention(zz, locals_, halo):
     big = (WIN * T, 2 * T)
     return call(
         attention_kernel,
@@ -173,7 +184,7 @@
         shape((4, 4 * HD, T)),
         [
             pltpu.VMEM((4, 4 * HD, T), BF16),
-            pltpu.VMEM((WIN, R, T), BF16),
+            pltpu.VMEM((WIN + 2, R, T), BF16),
             pltpu.VMEM((WIN * T, HD), BF16),
             pltpu.VMEM((WIN * T, HD), BF16),
             pltpu.VMEM(big, F32),
@@ -185,7 +196,7 @@
             pltpu.VMEM((HD, 4 * T), F32),
         ],
         [zz],
-        local,
+        *locals_,
         halo,
     )
 
@@ -223,13 +234,14 @@
     grad_patches[...] = (scale_own[...] * d_own - x * (i * i * row_total * (1.0 / D))).astype(BF16)
 
 
-def assemble_kernel(head, h0, h1, h2, h3, n, c):
-    for j, quarter in enumerate((h0, h1, h2, h3)):
+def assemble_kernel(head, *refs):
+    n, c = refs[8:]
+    for j in range(4):
         at = times(jnp.bitwise_xor(head[0], j), W)
-        for k in range(4):
+        for k, (part, row) in enumerate(((0, 0), (0, 1), (4, 0), (0, 2))):
             lane = slice(k * T, (k + 1) * T)
-            n[at, lane] = quarter[2 * k * W : (2 * k + 1) * W, :]
-            c[at, lane] = quarter[(2 * k + 1) * W : (2 * k + 2) * W, :]
+            n[at, lane] = refs[part + j][2 * row * W : (2 * row + 1) * W, :]
+            c[at, lane] = refs[part + j][(2 * row + 1) * W : (2 * row + 2) * W, :]
 
 
 def weights_kernel(zz, n, c, grads, w, out, g, term):
@@ -332,34 +344,41 @@
     cot, normed = lax.optimization_barrier((cot, normed))
     cots = [along_head(cot, k) for k in range(4)]
     quarter = [quarter, along_z(quarter, 1), None, along_z(quarter, 3)]
-    quarter[3], cots = lax.optimization_barrier((quarter[3], cots))
-    quarter[2] = along_z(quarter[3], 1)
-    quarter = jnp.concatenate(quarter, axis=0)
     ids = image_ids.reshape(1, T)
     proj = call(project_kernel, "project", shape((3 * W, T)), [], [], normed, w, w_out, ids)
     own = call(
         payload_kernel,
         "payload",
-        shape((8, R, T)),
-        [pltpu.VMEM((D, T), BF16)],
-        [head],
+        [shape((R, T))] * 4,
+        [pltpu.VMEM((4, R, T), BF16), pltpu.VMEM((D, T), BF16)],
+        [head, zz],
         *cots,
         proj,
         w_out,
         ids,
     )
-    own, quarter = lax.optimization_barrier((own, quarter))
-    local = lax.all_to_all(own, "z", 0, 0, tiled=True)
-    near = lax.dynamic_slice_in_dim(local, jnp.where(zz[0] < 4, 5, 0), 3, 0)
-    across = along_head(quarter, 2)
-    near, across = lax.optimization_barrier((near, across))
+    own, quarter[1], quarter[3] = lax.optimization_barrier((own, quarter[1], quarter[3]))
+    local = {k: along_z(own[k % 4], k) for k in (4, 5, 6, 7, 0, 1, 2, 3)}
+    first = jnp.concatenate([quarter[0], quarter[1], quarter[3]], axis=0)
+    last = along_z(quarter[3], 1)
+    near = call(
+        near_kernel,
+        "near",
+        shape((3, R, T)),
+        [pltpu.VMEM((4, R, T), BF16)],
+        [zz],
+        *[local[k] for k in (4, 5, 6, 7)],
+    )
+    across = along_head(first, 2)
+    near, local[2], local[3] = lax.optimization_barrier((near, local[2], local[3]))
     halo = to_next_group(near)
-    quarters = [quarter, along_head(quarter, 1), across, along_head(across, 1)]
+    quarters = [first, along_head(first, 1), across, along_head(across, 1)]
+    across = along_head(last, 2)
+    quarters += [last, along_head(last, 1), across, along_head(across, 1)]
     n, c = call(
         assemble_kernel, "assemble", [shape((D, 4 * T))] * 2, [], [head], *quarters
     )
-    halo, n, c = lax.optimization_barrier((halo, n, c))
-    grads = attention(zz, local, halo)
+    grads = attention(zz, [local[k] for k in range(8)], halo)
     backs = [grads[k] for k in range(4)]
     terms = call(
         weights_kernel,

time: 110 us -> 106 us (0.964)
  starting transfers between devices: 50 us -> 57 us
  waiting for transfers between devices: 30.2 us -> 23.7 us
  local copies, waits for them, and re-layouts: 12.9 us -> 9.5 us
    all_to_all x1 -> x0, waiting for transfers between devices: 15.6 us -> none  [body(): local = lax.all_to_all(own, 'z', 0, 0, tiled=True)]
    ppermute x6 -> x13, starting transfers between devices: 8.81 us -> 23.5 us  [along_z(): return lax.ppermute(x, 'z', [(i, i ^ by) for i in range(8)]) if by else x]
    ppermute x6 -> x13, waiting for transfers between devices: 3.37 us -> 15.1 us  [along_z(): return lax.ppermute(x, 'z', [(i, i ^ by) for i in range(8)]) if by else x]
    all_to_all x1 -> x0, starting transfers between devices: 6.07 us -> none  [body(): local = lax.all_to_all(own, 'z', 0, 0, tiled=True)]
    unnamed x44 -> x34, local copies, waits for them, and re-layouts: 12.2 us -> 8.72 us
    ppermute x12 -> x15, waiting for transfers between devices: 5.32 us -> 2.56 us  [along_head(): return lax.ppermute(x, HEAD, [(i, i ^ by) for i in range(4)]) if by else x]
    all_to_all x1, starting transfers between devices: 7.73 us -> 6.06 us  [body(): terms = lax.all_to_all(terms, ('y', 'xh'), 0, 0, tiled=True)]
    all_to_all x1, starting transfers between devices: 4.08 us -> 5.46 us  [body(): lax.all_to_all(terms, 'z', 0, 0, tiled=True, axis_index_groups=[list(rang...]
  transfers between devices with their start and end apart: 22 -> 31, of which waited for: 10 -> 12; matrix products, arithmetic and copies ran while one was open for 0% -> 1% of each run, Pallas kernels for 5% -> 7%
where the time goes in v3:
time: 106 us; the launch traced here: 105 us
  starting transfers between devices  57 us (54%)
  waiting for transfers between devices  23.7 us (22%)
  Pallas kernels  14.4 us (14%)
  local copies, waits for them, and re-layouts  9.5 us (9%)
    ppermute x13, starting transfers between devices, along_z(): return lax.ppermute(x, 'z', [(i, i ^ by) for i in range(8)]) if by else x  23.5 us
    ppermute x15, starting transfers between devices, along_head(): return lax.ppermute(x, HEAD, [(i, i ^ by) for i in range(4)]) if by else x  17.6 us
    ppermute x13, waiting for transfers between devices, along_z(): return lax.ppermute(x, 'z', [(i, i ^ by) for i in range(8)]) if by else x  15.1 us
    pallas_call x12, Pallas kernels, call(): pl.pallas_call(kernel, out_shape=outs, in_specs=specs, out_specs=vmem if...  14.4 us
    unnamed x34, local copies, waits for them, and re-layouts  8.72 us
    all_to_all x1, starting transfers between devices, body(): terms = lax.all_to_all(terms, ('y', 'xh'), 0, 0, tiled=True)  6.06 us
    all_to_all x1, starting transfers between devices, body(): lax.all_to_all(terms, 'z', 0, 0, tiled=True, axis_index_groups=[list(rang...  5.46 us
    all_to_all x1, waiting for transfers between devices, body(): terms = lax.all_to_all(terms, ('y', 'xh'), 0, 0, tiled=True)  4.52 us
  transfers between devices with their start and end apart: 31, of which 12 were waited for; matrix products, arithmetic and copies ran while one was open for 1% of the time, Pallas kernels for 7%

profile of v3, /device:TPU:1, one launch (start us, length us, event | category | flops | bytes accessed | tf_op | source)
XLA Modules:
  0.0 105.5 jit_solution(7714893084670334280)
XLA Ops:
  0.6 2.2 %norm.1 = (bf16[1280,128]{1,0:T(8,128)(2,1)}, bf16[640,128]{1,0:T(8,128)(2,1)}, bf16[320,128]{1,0:T(8,128)(2,1)}, f32[320,128]{1,0:T(8,128)}, f32[8,128]{1,0:T(8,128)}) custom-call(s32[1]{0:T(128)} %bitcast.1.head, bf16[128,1280]{1,0:T(8,128)(2,1)} %patches_far.1, f32[10,128]{1,0:T(8,128)} %bitcast.36, bf16[320,128]{1,0:T(8,128)(2,1)} %bitcast.31), custom_call_target="tpu_custom_call" | custom-call | flops 1000 | bytes 1000 | tf_op jit(solution)/shard_map/norm/pallas_call | solution.py:32
  2.9 2.6 %collective-permute-start.3 = (bf16[640,128]{1,0:T(8,128)(2,1)}, bf16[640,128]{1,0:T(8,128)(2,1)S(1)}, u32[]{:S(2)}, u32[]{:S(2)}) collective-permute-start(bf16[640,128]{1,0:T(8,128)(2,1)} %get-tuple-element.46), channel_id=1, source_target_pairs={{0,4},{4,0},{8,12},{12,8},{16,20},{20,16},{24,28},{28,24},{1,5},{5... | collective-permute-start | bytes 491528 | tf_op jit(solution)/shard_map/ppermute | solution.py:304
  5.4 2.8 %collective-permute-start.4 = (bf16[640,128]{1,0:T(8,128)(2,1)}, bf16[640,128]{1,0:T(8,128)(2,1)S(1)}, u32[]{:S(2)}, u32[]{:S(2)}) collective-permute-start(bf16[640,128]{1,0:T(8,128)(2,1)} %get-tuple-element.46), channel_id=1, source_target_pairs={{0,12},{4,8},{8,4},{12,0},{16,28},{20,24},{24,20},{28,16},{1,13},{... | collective-permute-start | bytes 491528 | tf_op jit(solution)/shard_map/ppermute | solution.py:304
  10.8 1.7 %copy-done = bf16[1280,3,320]{0,2,1:T(8,128)(2,1)S(1)} copy-done((bf16[1280,3,320]{0,2,1:T(8,128)(2,1)S(1)}, bf16[1280,3,320]{0,2,1:T(8,128)(2,1)}, u32[]{:S(2)}) %copy-start) | copy-done | bytes 2457624
  17.1 1.3 %collective-permute-start.14 = (bf16[1920,128]{1,0:T(8,128)(2,1)S(1)}, bf16[1920,128]{1,0:T(8,128)(2,1)S(1)}, u32[]{:S(2)}, u32[]{:S(2)}) collective-permute-start(bf16[1920,128]{1,0:T(8,128)(2,1)S(1)} %constant_dynamic-update-slice_fusion.refs_0_), channel_id=1, source_target_pairs={{0,2},{1,3},{2,0},{3,1},{4,6},{5,7},{6,4},{7,5},{8,10},{9,11},{10,... | collective-permute-start | bytes 1474568 | tf_op jit(solution)/shard_map/ppermute | solution.py:308
  18.4 5.1 %collective-permute-start.6 = (bf16[336,128]{1,0:T(8,128)(2,1)S(1)}, bf16[336,128]{1,0:T(8,128)(2,1)S(1)}, u32[]{:S(2)}, u32[]{:S(2)}) collective-permute-start(bf16[336,128]{1,0:T(8,128)(2,1)S(1)} %get-tuple-element.47.r0), channel_id=1, source_target_pairs={{0,16},{4,20},{8,24},{12,28},{16,0},{20,4},{24,8},{28,12},{1,17},{... | collective-permute-start | bytes 258056 | tf_op jit(solution)/shard_map/ppermute | solution.py:304
  23.5 4.0 %collective-permute-start.8 = (bf16[336,128]{1,0:T(8,128)(2,1)S(1)}, bf16[336,128]{1,0:T(8,128)(2,1)S(1)}, u32[]{:S(2)}, u32[]{:S(2)}) collective-permute-start(bf16[336,128]{1,0:T(8,128)(2,1)S(1)} %get-tuple-element.49), channel_id=1, source_target_pairs={{0,24},{4,28},{8,16},{12,20},{16,8},{20,12},{24,0},{28,4},{1,25},{... | collective-permute-start | bytes 258056 | tf_op jit(solution)/shard_map/ppermute | solution.py:304
  27.5 1.6 %collective-permute-start.10 = (bf16[336,128]{1,0:T(8,128)(2,1)S(1)}, bf16[336,128]{1,0:T(8,128)(2,1)S(1)}, u32[]{:S(2)}, u32[]{:S(2)}) collective-permute-start(bf16[336,128]{1,0:T(8,128)(2,1)S(1)} %get-tuple-element.49), channel_id=1, source_target_pairs={{0,8},{4,12},{8,0},{12,4},{16,24},{20,28},{24,16},{28,20},{1,9},{5... | collective-permute-start | bytes 258056 | tf_op jit(solution)/shard_map/ppermute | solution.py:304
  29.1 3.5 %collective-permute-done.7.r5 = bf16[336,128]{1,0:T(8,128)(2,1)S(1)} collective-permute-done((bf16[336,128]{1,0:T(8,128)(2,1)S(1)}, bf16[336,128]{1,0:T(8,128)(2,1)S(1)}, u32[]{:S(2)}, u32[]{:S(2)}) %collective-permute-start.7) | collective-permute-done | bytes 86048 | tf_op jit(solution)/shard_map/ppermute | solution.py:304
  32.7 1.5 %collective-permute-start.11 = (bf16[336,128]{1,0:T(8,128)(2,1)S(1)}, bf16[336,128]{1,0:T(8,128)(2,1)S(1)}, u32[]{:S(2)}, u32[]{:S(2)}) collective-permute-start(bf16[336,128]{1,0:T(8,128)(2,1)S(1)} %get-tuple-element.50), channel_id=1, source_target_pairs={{0,12},{4,8},{8,4},{12,0},{16,28},{20,24},{24,20},{28,16},{1,13},{... | collective-permute-start | bytes 258056 | tf_op jit(solution)/shard_map/ppermute | solution.py:304
  34.1 1.8 %collective-permute-done.8.r6 = bf16[336,128]{1,0:T(8,128)(2,1)S(1)} collective-permute-done((bf16[336,128]{1,0:T(8,128)(2,1)S(1)}, bf16[336,128]{1,0:T(8,128)(2,1)S(1)}, u32[]{:S(2)}, u32[]{:S(2)}) %collective-permute-start.8) | collective-permute-done | bytes 86048 | tf_op jit(solution)/shard_map/ppermute | solution.py:304
  38.0 2.3 %collective-permute-done.11.r3 = bf16[336,128]{1,0:T(8,128)(2,1)S(1)} collective-permute-done((bf16[336,128]{1,0:T(8,128)(2,1)S(1)}, bf16[336,128]{1,0:T(8,128)(2,1)S(1)}, u32[]{:S(2)}, u32[]{:S(2)}) %collective-permute-start.11) | collective-permute-done | bytes 86048 | tf_op jit(solution)/shard_map/ppermute | solution.py:304
  40.3 4.4 %collective-permute-start.12 = (bf16[3,336,128]{2,1,0:T(8,128)(2,1)S(1)}, bf16[3,336,128]{2,1,0:T(8,128)(2,1)S(1)}, u32[]{:S(2)}, u32[]{:S(2)}) collective-permute-start(bf16[3,336,128]{2,1,0:T(8,128)(2,1)S(1)} %near.1), channel_id=1, source_target_pairs={{0,32},{4,36},{8,40},{12,44},{32,64},{36,68},{40,72},{44,76},{48,1... | collective-permute-start | bytes 774152 | tf_op jit(solution)/shard_map/ppermute | solution.py:317
  44.7 1.6 %collective-permute-start.13 = (bf16[1920,128]{1,0:T(8,128)(2,1)S(1)}, bf16[1920,128]{1,0:T(8,128)(2,1)S(1)}, u32[]{:S(2)}, u32[]{:S(2)}) collective-permute-start(bf16[1920,128]{1,0:T(8,128)(2,1)S(1)} %constant_dynamic-update-slice_fusion.refs_0_), channel_id=1, source_target_pairs={{0,1},{1,0},{2,3},{3,2},{4,5},{5,4},{6,7},{7,6},{8,9},{9,8},{10,11... | collective-permute-start | bytes 1474568 | tf_op jit(solution)/shard_map/ppermute | solution.py:308
  46.4 1.2 %collective-permute-start.5 = (bf16[336,128]{1,0:T(8,128)(2,1)S(1)}, bf16[336,128]{1,0:T(8,128)(2,1)S(1)}, u32[]{:S(2)}, u32[]{:S(2)}) collective-permute-start(bf16[336,128]{1,0:T(8,128)(2,1)S(1)} %get-tuple-element.48), channel_id=1, source_target_pairs={{0,4},{4,0},{8,12},{12,8},{16,20},{20,16},{24,28},{28,24},{1,5},{5... | collective-permute-start | bytes 258056 | tf_op jit(solution)/shard_map/ppermute | solution.py:304
  47.7 2.2 %collective-permute-done.5.r1 = bf16[336,128]{1,0:T(8,128)(2,1)S(1)} collective-permute-done((bf16[336,128]{1,0:T(8,128)(2,1)S(1)}, bf16[336,128]{1,0:T(8,128)(2,1)S(1)}, u32[]{:S(2)}, u32[]{:S(2)}) %collective-permute-start.5) | collective-permute-done | bytes 86048 | tf_op jit(solution)/shard_map/ppermute | solution.py:304
  49.8 1.7 %collective-permute-start.17 = (bf16[640,128]{1,0:T(8,128)(2,1)S(1)}, bf16[640,128]{1,0:T(8,128)(2,1)S(1)}, u32[]{:S(2)}, u32[]{:S(2)}) collective-permute-start(bf16[640,128]{1,0:T(8,128)(2,1)S(1)} %collective-permute-done.16.refs_4_), channel_id=1, source_target_pairs={{0,1},{1,0},{2,3},{3,2},{4,5},{5,4},{6,7},{7,6},{8,9},{9,8},{10,11... | collective-permute-start | bytes 491528 | tf_op jit(solution)/shard_map/ppermute | solution.py:308
  51.5 1.6 %collective-permute-done.18.refs_6_ = bf16[640,128]{1,0:T(8,128)(2,1)S(1)} collective-permute-done((bf16[640,128]{1,0:T(8,128)(2,1)S(1)}, bf16[640,128]{1,0:T(8,128)(2,1)S(1)}, u32[]{:S(2)}, u32[]{:S(2)}) %collective-permute-start.18) | collective-permute-done | bytes 163872 | tf_op jit(solution)/shard_map/ppermute | solution.py:308
  53.2 2.1 %collective-permute-start.19 = (bf16[640,128]{1,0:T(8,128)(2,1)S(1)}, bf16[640,128]{1,0:T(8,128)(2,1)S(1)}, u32[]{:S(2)}, u32[]{:S(2)}) collective-permute-start(bf16[640,128]{1,0:T(8,128)(2,1)S(1)} %collective-permute-done.18.refs_6_), channel_id=1, source_target_pairs={{0,1},{1,0},{2,3},{3,2},{4,5},{5,4},{6,7},{7,6},{8,9},{9,8},{10,11... | collective-permute-start | bytes 491528 | tf_op jit(solution)/shard_map/ppermute | solution.py:308
  55.3 4.1 %attention.1.grads = bf16[4,320,128]{2,1,0:T(8,128)(2,1)S(1)} custom-call(s32[1]{0:T(128)} %bitcast.zz, bf16[336,128]{1,0:T(8,128)(2,1)S(1)} %get-tuple-element.47.r0, bf16[336,128]{1,0:T(8,128)(2,1)S(1)} %collective-permute-done.5.r1, bf16[336,128]{1,0:T(8,128)(2,1)S(1)} %collective-permute-done.10.r2, bf16[336,128]{1,0:T(8,128)(2,1)S(1)} %collective-permute-done.11.r3, ...), custom_call_target="tpu_custom_call" | custom-call | flops 1000 | bytes 1000 | tf_op jit(solution)/shard_map/attention/pallas_call | solution.py:32
  64.0 6.1 %all-to-all-start = ((bf16[8,416,128]{2,1,0:T(8,128)(2,1)}), bf16[8,416,128]{2,1,0:T(8,128)(2,1)}, u32[]{:S(2)}, u32[]{:S(2)}) async-start(bf16[8,416,128]{2,1,0:T(8,128)(2,1)} %copy-done.4), calls=%async_computation | async-start | bytes 1703936 | tf_op jit(solution)/shard_map/all_to_all | solution.py:395
  70.1 1.8 %collective-permute-start.21 = (bf16[320,128]{1,0:T(8,128)(2,1)}, bf16[320,128]{1,0:T(8,128)(2,1)S(1)}, u32[]{:S(2)}, u32[]{:S(2)}) collective-permute-start(bf16[320,128]{1,0:T(8,128)(2,1)} %get-tuple-element.61), channel_id=1, source_target_pairs={{0,8},{4,12},{8,0},{12,4},{16,24},{20,28},{24,16},{28,20},{1,9},{5... | collective-permute-start | bytes 245768 | tf_op jit(solution)/shard_map/ppermute | solution.py:304
  72.0 1.6 %collective-permute-start.22 = (bf16[320,128]{1,0:T(8,128)(2,1)}, bf16[320,128]{1,0:T(8,128)(2,1)S(1)}, u32[]{:S(2)}, u32[]{:S(2)}) collective-permute-start(bf16[320,128]{1,0:T(8,128)(2,1)} %get-tuple-element.62), channel_id=1, source_target_pairs={{0,12},{4,8},{8,4},{12,0},{16,28},{20,24},{24,20},{28,16},{1,13},{... | collective-permute-start | bytes 245768 | tf_op jit(solution)/shard_map/ppermute | solution.py:304
  74.6 3.3 %collective-permute-done.22.b3 = bf16[320,128]{1,0:T(8,128)(2,1)S(1)} collective-permute-done((bf16[320,128]{1,0:T(8,128)(2,1)}, bf16[320,128]{1,0:T(8,128)(2,1)S(1)}, u32[]{:S(2)}, u32[]{:S(2)}) %collective-permute-start.22) | collective-permute-done | bytes 81952 | tf_op jit(solution)/shard_map/ppermute | solution.py:304
  80.6 4.5 %all-to-all-done.got = bf16[8,416,128]{2,1,0:T(8,128)(2,1)} async-done(((bf16[8,416,128]{2,1,0:T(8,128)(2,1)}), bf16[8,416,128]{2,1,0:T(8,128)(2,1)}, u32[]{:S(2)}, u32[]{:S(2)}) %all-to-all-start) | async-done | bytes 852000 | tf_op jit(solution)/shard_map/all_to_all | solution.py:395
  85.1 2.0 %middle.1 = bf16[8,80,128]{2,1,0:T(8,128)(2,1)} custom-call(bf16[8,416,128]{2,1,0:T(8,128)(2,1)} %all-to-all-done.got), custom_call_target="tpu_custom_call" | custom-call | flops 1000 | bytes 1000 | tf_op jit(solution)/shard_map/middle/pallas_call | solution.py:32
  87.1 5.5 %all-to-all-start.1 = ((bf16[8,80,128]{2,1,0:T(8,128)(2,1)}), bf16[8,80,128]{2,1,0:T(8,128)(2,1)S(1)}, u32[]{:S(2)}, u32[]{:S(2)}) async-start(bf16[8,80,128]{2,1,0:T(8,128)(2,1)} %middle.1), calls=%async_computation.1 | async-start | bytes 327680 | tf_op jit(solution)/shard_map/all_to_all | solution.py:411
  92.6 1.7 %collective-permute-start.23 = (bf16[656,128]{1,0:T(8,128)(2,1)S(1)}, bf16[656,128]{1,0:T(8,128)(2,1)S(1)}, u32[]{:S(2)}, u32[]{:S(2)}) collective-permute-start(bf16[656,128]{1,0:T(8,128)(2,1)S(1)} %get-tuple-element.75), channel_id=1, source_target_pairs={{0,1},{1,0},{2,3},{3,2},{4,5},{5,4},{6,7},{7,6},{8,9},{9,8},{10,11... | collective-permute-start | bytes 503816 | tf_op jit(solution)/shard_map/ppermute | solution.py:308
  94.5 1.6 %collective-permute-start.25 = (bf16[656,128]{1,0:T(8,128)(2,1)S(1)}, bf16[656,128]{1,0:T(8,128)(2,1)S(1)}, u32[]{:S(2)}, u32[]{:S(2)}) collective-permute-start(bf16[656,128]{1,0:T(8,128)(2,1)S(1)} %get-tuple-element.73), channel_id=1, source_target_pairs={{0,3},{1,2},{2,1},{3,0},{4,7},{5,6},{6,5},{7,4},{8,11},{9,10},{10,... | collective-permute-start | bytes 503816 | tf_op jit(solution)/shard_map/ppermute | solution.py:308
  96.1 1.6 %all-to-all-done.1.got = bf16[8,80,128]{2,1,0:T(8,128)(2,1)S(1)} async-done(((bf16[8,80,128]{2,1,0:T(8,128)(2,1)}), bf16[8,80,128]{2,1,0:T(8,128)(2,1)S(1)}, u32[]{:S(2)}, u32[]{:S(2)}) %all-to-all-start.1) | async-done | bytes 163872 | tf_op jit(solution)/shard_map/all_to_all | solution.py:411
  98.5 3.0 %collective-permute-start.26 = (f32[16,128]{1,0:T(8,128)S(1)}, f32[16,128]{1,0:T(8,128)S(1)}, u32[]{:S(2)}, u32[]{:S(2)}) collective-permute-start(f32[16,128]{1,0:T(8,128)S(1)} %get-tuple-element.72.t0), channel_id=1, source_target_pairs={{0,1},{1,0},{2,3},{3,2},{4,5},{5,4},{6,7},{7,6},{8,9},{9,8},{10,11... | collective-permute-start | bytes 24584 | tf_op jit(solution)/shard_map/ppermute | solution.py:308
  101.7 1.5 %collective-permute-start.28 = (f32[16,128]{1,0:T(8,128)S(1)}, f32[16,128]{1,0:T(8,128)S(1)}, u32[]{:S(2)}, u32[]{:S(2)}) collective-permute-start(f32[16,128]{1,0:T(8,128)S(1)} %get-tuple-element.72.t0), channel_id=1, source_target_pairs={{0,3},{1,2},{2,1},{3,0},{4,7},{5,6},{6,5},{7,4},{8,11},{9,10},{10,... | collective-permute-start | bytes 24584 | tf_op jit(solution)/shard_map/ppermute | solution.py:308
  (79 shorter events, 20.9 us)
Async XLA Ops:
  2.9 14.1 %collective-permute-start.3 = (bf16[640,128]{1,0:T(8,128)(2,1)}, bf16[640,128]{1,0:T(8,128)(2,1)S(1)}, u32[]{:S(2)}, u32[]{:S(2)}) collective-permute-start(bf16[640,128]{1,0:T(8,128)(2,1)} %get-tuple-element.46), channel_id=1, source_target_pairs={{0,4},{4,0},{8,12},{12,8},{16,20},{20,16},{24,28},{28,24},{1,5},{5... | collective-permute-start | bytes 491528 | tf_op jit(solution)/shard_map/ppermute | solution.py:304
  5.4 11.6 %collective-permute-start.4 = (bf16[640,128]{1,0:T(8,128)(2,1)}, bf16[640,128]{1,0:T(8,128)(2,1)S(1)}, u32[]{:S(2)}, u32[]{:S(2)}) collective-permute-start(bf16[640,128]{1,0:T(8,128)(2,1)} %get-tuple-element.46), channel_id=1, source_target_pairs={{0,12},{4,8},{8,4},{12,0},{16,28},{20,24},{24,20},{28,16},{1,13},{... | collective-permute-start | bytes 491528 | tf_op jit(solution)/shard_map/ppermute | solution.py:304
  8.2 8.0 %collective-permute-start = (bf16[320,128]{1,0:T(8,128)(2,1)}, bf16[320,128]{1,0:T(8,128)(2,1)S(1)}, u32[]{:S(2)}, u32[]{:S(2)}) collective-permute-start(bf16[320,128]{1,0:T(8,128)(2,1)} %bitcast.32), channel_id=1, source_target_pairs={{0,1},{1,0},{2,3},{3,2},{4,5},{5,4},{6,7},{7,6},{8,9},{9,8},{10,11... | collective-permute-start | bytes 245768 | tf_op jit(solution)/shard_map/ppermute | solution.py:308
  9.2 7.0 %collective-permute-start.1 = (bf16[320,128]{1,0:T(8,128)(2,1)}, bf16[320,128]{1,0:T(8,128)(2,1)S(1)}, u32[]{:S(2)}, u32[]{:S(2)}) collective-permute-start(bf16[320,128]{1,0:T(8,128)(2,1)} %bitcast.33), channel_id=1, source_target_pairs={{0,2},{1,3},{2,0},{3,1},{4,6},{5,7},{6,4},{7,5},{8,10},{9,11},{10,... | collective-permute-start | bytes 245768 | tf_op jit(solution)/shard_map/ppermute | solution.py:308
  10.4 5.8 %collective-permute-start.2 = (bf16[320,128]{1,0:T(8,128)(2,1)}, bf16[320,128]{1,0:T(8,128)(2,1)S(1)}, u32[]{:S(2)}, u32[]{:S(2)}) collective-permute-start(bf16[320,128]{1,0:T(8,128)(2,1)} %bitcast.34), channel_id=1, source_target_pairs={{0,3},{1,2},{2,1},{3,0},{4,7},{5,6},{6,5},{7,4},{8,11},{9,10},{10,... | collective-permute-start | bytes 245768 | tf_op jit(solution)/shard_map/ppermute | solution.py:308
  17.1 29.2 %collective-permute-start.14 = (bf16[1920,128]{1,0:T(8,128)(2,1)S(1)}, bf16[1920,128]{1,0:T(8,128)(2,1)S(1)}, u32[]{:S(2)}, u32[]{:S(2)}) collective-permute-start(bf16[1920,128]{1,0:T(8,128)(2,1)S(1)} %constant_dynamic-update-slice_fusion.refs_0_), channel_id=1, source_target_pairs={{0,2},{1,3},{2,0},{3,1},{4,6},{5,7},{6,4},{7,5},{8,10},{9,11},{10,... | collective-permute-start | bytes 1474568 | tf_op jit(solution)/shard_map/ppermute | solution.py:308
  18.4 9.2 %collective-permute-start.6 = (bf16[336,128]{1,0:T(8,128)(2,1)S(1)}, bf16[336,128]{1,0:T(8,128)(2,1)S(1)}, u32[]{:S(2)}, u32[]{:S(2)}) collective-permute-start(bf16[336,128]{1,0:T(8,128)(2,1)S(1)} %get-tuple-element.47.r0), channel_id=1, source_target_pairs={{0,16},{4,20},{8,24},{12,28},{16,0},{20,4},{24,8},{28,12},{1,17},{... | collective-permute-start | bytes 258056 | tf_op jit(solution)/shard_map/ppermute | solution.py:304
  23.5 9.2 %collective-permute-start.7 = (bf16[336,128]{1,0:T(8,128)(2,1)S(1)}, bf16[336,128]{1,0:T(8,128)(2,1)S(1)}, u32[]{:S(2)}, u32[]{:S(2)}) collective-permute-start(bf16[336,128]{1,0:T(8,128)(2,1)S(1)} %get-tuple-element.48), channel_id=1, source_target_pairs={{0,20},{4,16},{8,28},{12,24},{16,4},{20,0},{24,12},{28,8},{1,21},{... | collective-permute-start | bytes 258056 | tf_op jit(solution)/shard_map/ppermute | solution.py:304
  23.5 12.5 %collective-permute-start.8 = (bf16[336,128]{1,0:T(8,128)(2,1)S(1)}, bf16[336,128]{1,0:T(8,128)(2,1)S(1)}, u32[]{:S(2)}, u32[]{:S(2)}) collective-permute-start(bf16[336,128]{1,0:T(8,128)(2,1)S(1)} %get-tuple-element.49), channel_id=1, source_target_pairs={{0,24},{4,28},{8,16},{12,20},{16,8},{20,12},{24,0},{28,4},{1,25},{... | collective-permute-start | bytes 258056 | tf_op jit(solution)/shard_map/ppermute | solution.py:304
  27.5 10.4 %collective-permute-start.9 = (bf16[336,128]{1,0:T(8,128)(2,1)S(1)}, bf16[336,128]{1,0:T(8,128)(2,1)S(1)}, u32[]{:S(2)}, u32[]{:S(2)}) collective-permute-start(bf16[336,128]{1,0:T(8,128)(2,1)S(1)} %get-tuple-element.50), channel_id=1, source_target_pairs={{0,28},{4,24},{8,20},{12,16},{16,12},{20,8},{24,4},{28,0},{1,29},{... | collective-permute-start | bytes 258056 | tf_op jit(solution)/shard_map/ppermute | solution.py:304
  27.5 10.5 %collective-permute-start.10 = (bf16[336,128]{1,0:T(8,128)(2,1)S(1)}, bf16[336,128]{1,0:T(8,128)(2,1)S(1)}, u32[]{:S(2)}, u32[]{:S(2)}) collective-permute-start(bf16[336,128]{1,0:T(8,128)(2,1)S(1)} %get-tuple-element.49), channel_id=1, source_target_pairs={{0,8},{4,12},{8,0},{12,4},{16,24},{20,28},{24,16},{28,20},{1,9},{5... | collective-permute-start | bytes 258056 | tf_op jit(solution)/shard_map/ppermute | solution.py:304
  32.7 7.7 %collective-permute-start.11 = (bf16[336,128]{1,0:T(8,128)(2,1)S(1)}, bf16[336,128]{1,0:T(8,128)(2,1)S(1)}, u32[]{:S(2)}, u32[]{:S(2)}) collective-permute-start(bf16[336,128]{1,0:T(8,128)(2,1)S(1)} %get-tuple-element.50), channel_id=1, source_target_pairs={{0,12},{4,8},{8,4},{12,0},{16,28},{20,24},{24,20},{28,16},{1,13},{... | collective-permute-start | bytes 258056 | tf_op jit(solution)/shard_map/ppermute | solution.py:304
  36.0 10.4 %collective-permute-start.16 = (bf16[640,128]{1,0:T(8,128)(2,1)S(1)}, bf16[640,128]{1,0:T(8,128)(2,1)S(1)}, u32[]{:S(2)}, u32[]{:S(2)}) collective-permute-start(bf16[640,128]{1,0:T(8,128)(2,1)S(1)} %collective-permute-done.4), channel_id=1, source_target_pairs={{0,4},{4,0},{8,12},{12,8},{16,20},{20,16},{24,28},{28,24},{1,5},{5... | collective-permute-start | bytes 491528 | tf_op jit(solution)/shard_map/ppermute | solution.py:304
  40.3 15.0 %collective-permute-start.12 = (bf16[3,336,128]{2,1,0:T(8,128)(2,1)S(1)}, bf16[3,336,128]{2,1,0:T(8,128)(2,1)S(1)}, u32[]{:S(2)}, u32[]{:S(2)}) collective-permute-start(bf16[3,336,128]{2,1,0:T(8,128)(2,1)S(1)} %near.1), channel_id=1, source_target_pairs={{0,32},{4,36},{8,40},{12,44},{32,64},{36,68},{40,72},{44,76},{48,1... | collective-permute-start | bytes 774152 | tf_op jit(solution)/shard_map/ppermute | solution.py:317
  44.7 15.5 %collective-permute-start.13 = (bf16[1920,128]{1,0:T(8,128)(2,1)S(1)}, bf16[1920,128]{1,0:T(8,128)(2,1)S(1)}, u32[]{:S(2)}, u32[]{:S(2)}) collective-permute-start(bf16[1920,128]{1,0:T(8,128)(2,1)S(1)} %constant_dynamic-update-slice_fusion.refs_0_), channel_id=1, source_target_pairs={{0,1},{1,0},{2,3},{3,2},{4,5},{5,4},{6,7},{7,6},{8,9},{9,8},{10,11... | collective-permute-start | bytes 1474568 | tf_op jit(solution)/shard_map/ppermute | solution.py:308
  46.3 13.9 %collective-permute-start.15 = (bf16[1920,128]{1,0:T(8,128)(2,1)S(1)}, bf16[1920,128]{1,0:T(8,128)(2,1)S(1)}, u32[]{:S(2)}, u32[]{:S(2)}) collective-permute-start(bf16[1920,128]{1,0:T(8,128)(2,1)S(1)} %collective-permute-done.14.refs_2_), channel_id=1, source_target_pairs={{0,1},{1,0},{2,3},{3,2},{4,5},{5,4},{6,7},{7,6},{8,9},{9,8},{10,11... | collective-permute-start | bytes 1474568 | tf_op jit(solution)/shard_map/ppermute | solution.py:308
  46.4 6.8 %collective-permute-start.18 = (bf16[640,128]{1,0:T(8,128)(2,1)S(1)}, bf16[640,128]{1,0:T(8,128)(2,1)S(1)}, u32[]{:S(2)}, u32[]{:S(2)}) collective-permute-start(bf16[640,128]{1,0:T(8,128)(2,1)S(1)} %collective-permute-done.16.refs_4_), channel_id=1, source_target_pairs={{0,2},{1,3},{2,0},{3,1},{4,6},{5,7},{6,4},{7,5},{8,10},{9,11},{10,... | collective-permute-start | bytes 491528 | tf_op jit(solution)/shard_map/ppermute | solution.py:308
  46.4 3.4 %collective-permute-start.5 = (bf16[336,128]{1,0:T(8,128)(2,1)S(1)}, bf16[336,128]{1,0:T(8,128)(2,1)S(1)}, u32[]{:S(2)}, u32[]{:S(2)}) collective-permute-start(bf16[336,128]{1,0:T(8,128)(2,1)S(1)} %get-tuple-element.48), channel_id=1, source_target_pairs={{0,4},{4,0},{8,12},{12,8},{16,20},{20,16},{24,28},{28,24},{1,5},{5... | collective-permute-start | bytes 258056 | tf_op jit(solution)/shard_map/ppermute | solution.py:304
  49.8 10.3 %collective-permute-start.17 = (bf16[640,128]{1,0:T(8,128)(2,1)S(1)}, bf16[640,128]{1,0:T(8,128)(2,1)S(1)}, u32[]{:S(2)}, u32[]{:S(2)}) collective-permute-start(bf16[640,128]{1,0:T(8,128)(2,1)S(1)} %collective-permute-done.16.refs_4_), channel_id=1, source_target_pairs={{0,1},{1,0},{2,3},{3,2},{4,5},{5,4},{6,7},{7,6},{8,9},{9,8},{10,11... | collective-permute-start | bytes 491528 | tf_op jit(solution)/shard_map/ppermute | solution.py:308
  53.2 7.0 %collective-permute-start.19 = (bf16[640,128]{1,0:T(8,128)(2,1)S(1)}, bf16[640,128]{1,0:T(8,128)(2,1)S(1)}, u32[]{:S(2)}, u32[]{:S(2)}) collective-permute-start(bf16[640,128]{1,0:T(8,128)(2,1)S(1)} %collective-permute-done.18.refs_6_), channel_id=1, source_target_pairs={{0,1},{1,0},{2,3},{3,2},{4,5},{5,4},{6,7},{7,6},{8,9},{9,8},{10,11... | collective-permute-start | bytes 491528 | tf_op jit(solution)/shard_map/ppermute | solution.py:308
  64.0 21.1 %all-to-all-start = ((bf16[8,416,128]{2,1,0:T(8,128)(2,1)}), bf16[8,416,128]{2,1,0:T(8,128)(2,1)}, u32[]{:S(2)}, u32[]{:S(2)}) async-start(bf16[8,416,128]{2,1,0:T(8,128)(2,1)} %copy-done.4), calls=%async_computation | async-start | bytes 1703936 | tf_op jit(solution)/shard_map/all_to_all | solution.py:395
  70.0 4.1 %collective-permute-start.20 = (bf16[320,128]{1,0:T(8,128)(2,1)}, bf16[320,128]{1,0:T(8,128)(2,1)S(1)}, u32[]{:S(2)}, u32[]{:S(2)}) collective-permute-start(bf16[320,128]{1,0:T(8,128)(2,1)} %get-tuple-element.60), channel_id=1, source_target_pairs={{0,4},{4,0},{8,12},{12,8},{16,20},{20,16},{24,28},{28,24},{1,5},{5... | collective-permute-start | bytes 245768 | tf_op jit(solution)/shard_map/ppermute | solution.py:304
  70.1 4.5 %collective-permute-start.21 = (bf16[320,128]{1,0:T(8,128)(2,1)}, bf16[320,128]{1,0:T(8,128)(2,1)S(1)}, u32[]{:S(2)}, u32[]{:S(2)}) collective-permute-start(bf16[320,128]{1,0:T(8,128)(2,1)} %get-tuple-element.61), channel_id=1, source_target_pairs={{0,8},{4,12},{8,0},{12,4},{16,24},{20,28},{24,16},{28,20},{1,9},{5... | collective-permute-start | bytes 245768 | tf_op jit(solution)/shard_map/ppermute | solution.py:304
  72.0 6.0 %collective-permute-start.22 = (bf16[320,128]{1,0:T(8,128)(2,1)}, bf16[320,128]{1,0:T(8,128)(2,1)S(1)}, u32[]{:S(2)}, u32[]{:S(2)}) collective-permute-start(bf16[320,128]{1,0:T(8,128)(2,1)} %get-tuple-element.62), channel_id=1, source_target_pairs={{0,12},{4,8},{8,4},{12,0},{16,28},{20,24},{24,20},{28,16},{1,13},{... | collective-permute-start | bytes 245768 | tf_op jit(solution)/shard_map/ppermute | solution.py:304
  80.6 23.5 %copy-start.13 = (f32[8,128]{1,0:T(8,128)S(1)}, f32[8,128]{1,0:T(8,128)}, u32[]{:S(2)}) copy-start(f32[8,128]{1,0:T(8,128)} %get-tuple-element.66.inv) | copy-start | bytes 12292
  87.1 10.6 %all-to-all-start.1 = ((bf16[8,80,128]{2,1,0:T(8,128)(2,1)}), bf16[8,80,128]{2,1,0:T(8,128)(2,1)S(1)}, u32[]{:S(2)}, u32[]{:S(2)}) async-start(bf16[8,80,128]{2,1,0:T(8,128)(2,1)} %middle.1), calls=%async_computation.1 | async-start | bytes 327680 | tf_op jit(solution)/shard_map/all_to_all | solution.py:411
  92.6 9.0 %collective-permute-start.23 = (bf16[656,128]{1,0:T(8,128)(2,1)S(1)}, bf16[656,128]{1,0:T(8,128)(2,1)S(1)}, u32[]{:S(2)}, u32[]{:S(2)}) collective-permute-start(bf16[656,128]{1,0:T(8,128)(2,1)S(1)} %get-tuple-element.75), channel_id=1, source_target_pairs={{0,1},{1,0},{2,3},{3,2},{4,5},{5,4},{6,7},{7,6},{8,9},{9,8},{10,11... | collective-permute-start | bytes 503816 | tf_op jit(solution)/shard_map/ppermute | solution.py:308
  94.4 8.8 %collective-permute-start.24 = (bf16[656,128]{1,0:T(8,128)(2,1)S(1)}, bf16[656,128]{1,0:T(8,128)(2,1)S(1)}, u32[]{:S(2)}, u32[]{:S(2)}) collective-permute-start(bf16[656,128]{1,0:T(8,128)(2,1)S(1)} %get-tuple-element.74), channel_id=1, source_target_pairs={{0,2},{1,3},{2,0},{3,1},{4,6},{5,7},{6,4},{7,5},{8,10},{9,11},{10,... | collective-permute-start | bytes 503816 | tf_op jit(solution)/shard_map/ppermute | solution.py:308
  94.5 9.5 %collective-permute-start.25 = (bf16[656,128]{1,0:T(8,128)(2,1)S(1)}, bf16[656,128]{1,0:T(8,128)(2,1)S(1)}, u32[]{:S(2)}, u32[]{:S(2)}) collective-permute-start(bf16[656,128]{1,0:T(8,128)(2,1)S(1)} %get-tuple-element.73), channel_id=1, source_target_pairs={{0,3},{1,2},{2,1},{3,0},{4,7},{5,6},{6,5},{7,4},{8,11},{9,10},{10,... | collective-permute-start | bytes 503816 | tf_op jit(solution)/shard_map/ppermute | solution.py:308
  98.5 6.3 %collective-permute-start.26 = (f32[16,128]{1,0:T(8,128)S(1)}, f32[16,128]{1,0:T(8,128)S(1)}, u32[]{:S(2)}, u32[]{:S(2)}) collective-permute-start(f32[16,128]{1,0:T(8,128)S(1)} %get-tuple-element.72.t0), channel_id=1, source_target_pairs={{0,1},{1,0},{2,3},{3,2},{4,5},{5,4},{6,7},{7,6},{8,9},{9,8},{10,11... | collective-permute-start | bytes 24584 | tf_op jit(solution)/shard_map/ppermute | solution.py:308
  101.5 3.3 %collective-permute-start.27 = (f32[16,128]{1,0:T(8,128)S(1)}, f32[16,128]{1,0:T(8,128)S(1)}, u32[]{:S(2)}, u32[]{:S(2)}) collective-permute-start(f32[16,128]{1,0:T(8,128)S(1)} %get-tuple-element.72.t0), channel_id=1, source_target_pairs={{0,2},{1,3},{2,0},{3,1},{4,6},{5,7},{6,4},{7,5},{8,10},{9,11},{10,... | collective-permute-start | bytes 24584 | tf_op jit(solution)/shard_map/ppermute | solution.py:308
  101.7 3.1 %collective-permute-start.28 = (f32[16,128]{1,0:T(8,128)S(1)}, f32[16,128]{1,0:T(8,128)S(1)}, u32[]{:S(2)}, u32[]{:S(2)}) collective-permute-start(f32[16,128]{1,0:T(8,128)S(1)} %get-tuple-element.72.t0), channel_id=1, source_target_pairs={{0,3},{1,2},{2,1},{3,0},{4,7},{5,6},{6,5},{7,4},{8,11},{9,10},{10,... | collective-permute-start | bytes 24584 | tf_op jit(solution)/shard_map/ppermute | solution.py:308
  (15 other events, 84.3 us)

commit v4 on v3

--- a/solution.py
+++ b/solution.py
@@ -76,7 +76,7 @@
     copies[2].wait()
 
 
-def project_kernel(normed, w, w_out, ids, proj):
+def project_kernel(normed, w, proj):
     proj[...] = jnp.dot(w[...], normed[...], preferred_element_type=F32).astype(BF16)
 
 
@@ -278,17 +278,18 @@
         out[7 - z] = jnp.concatenate(rows + [zero, total[400:, :]], axis=0).astype(BF16)
 
 
-def sums_kernel(got, qkv, out, gg):
-    tail = jnp.zeros((16, T), F32)
+def tails_kernel(got, gg):
+    gg[...] = sum(got[i, 64:80, :].astype(F32) for i in range(8))
+
+
+def sums_kernel(got, qkv, out):
     cols = []
     for m in range(HL):
         total = got[7 - m].astype(F32) + got[3 - m].astype(F32)
         cols.append(jnp.concatenate([total[20 * l : 20 * l + 20, :] for l in range(3)], axis=1))
-        tail = tail + total[64:80, :]
     for j in range(3):
         qkv[j] = jnp.concatenate([x[:, j * HD : (j + 1) * HD] for x in cols], axis=1)
     out[...] = jnp.concatenate([x[:, 3 * HD : 4 * HD] for x in cols], axis=1)
-    gg[...] = tail
 
 
 def gain_kernel(head, t0, t1, t2, t3, gain, out):
@@ -345,7 +346,7 @@
     cots = [along_head(cot, k) for k in range(4)]
     quarter = [quarter, along_z(quarter, 1), None, along_z(quarter, 3)]
     ids = image_ids.reshape(1, T)
-    proj = call(project_kernel, "project", shape((3 * W, T)), [], [], normed, w, w_out, ids)
+    proj = call(project_kernel, "project", shape((3 * W, T)), [], [], normed, w, limit=60)
     own = call(
         payload_kernel,
         "payload",
@@ -422,10 +423,11 @@
         scale_own,
         inv,
     )
-    grad_w_qkv, grad_w_out, gg = call(
+    gg = call(tails_kernel, "tails", shape((16, T), F32), [], [], terms)
+    grad_w_qkv, grad_w_out = call(
         sums_kernel,
         "sums",
-        [shape((3, 20, W), F32), shape((20, W), F32), shape((16, T), F32)],
+        [shape((3, 20, W), F32), shape((20, W), F32)],
         [],
         [],
         terms,

time: 106 us -> 106 us (level)
  local copies, waits for them, and re-layouts: 9.5 us -> 5.9 us
  Pallas kernels: 14.4 us -> 16.7 us
    unnamed x34 -> x32, local copies, waits for them, and re-layouts: 8.72 us -> 5.1 us
    pallas_call x12 -> x13, Pallas kernels: 14.4 us -> 16.7 us  [call(): pl.pallas_call(kernel, out_shape=outs, in_specs=specs, out_specs=vmem if...]
    ppermute x15, waiting for transfers between devices: 2.56 us -> 4.76 us  [along_head(): return lax.ppermute(x, HEAD, [(i, i ^ by) for i in range(4)]) if by else x]
    all_to_all x1, waiting for transfers between devices: 4.52 us -> 3.35 us  [body(): terms = lax.all_to_all(terms, ('y', 'xh'), 0, 0, tiled=True)]
  transfers between devices with their start and end apart: 31 -> 31, of which waited for: 12 -> 13; matrix products, arithmetic and copies ran while one was open for 1% -> 1% of each run, Pallas kernels for 7% -> 10%
where the time goes in v4:
time: 106 us; the launch traced here: 105 us
  starting transfers between devices  56.9 us (54%)
  waiting for transfers between devices  24.7 us (23%)
  Pallas kernels  16.7 us (16%)
  local copies, waits for them, and re-layouts  5.9 us (6%)
    ppermute x13, starting transfers between devices, along_z(): return lax.ppermute(x, 'z', [(i, i ^ by) for i in range(8)]) if by else x  23.4 us
    ppermute x15, starting transfers between devices, along_head(): return lax.ppermute(x, HEAD, [(i, i ^ by) for i in range(4)]) if by else x  17.6 us
    pallas_call x13, Pallas kernels, call(): pl.pallas_call(kernel, out_shape=outs, in_specs=specs, out_specs=vmem if...  16.7 us
    ppermute x13, waiting for transfers between devices, along_z(): return lax.ppermute(x, 'z', [(i, i ^ by) for i in range(8)]) if by else x  15 us
    all_to_all x1, starting transfers between devices, body(): terms = lax.all_to_all(terms, ('y', 'xh'), 0, 0, tiled=True)  6.19 us
    all_to_all x1, starting transfers between devices, body(): lax.all_to_all(terms, 'z', 0, 0, tiled=True, axis_index_groups=[list(rang...  5.3 us
    unnamed x32, local copies, waits for them, and re-layouts  5.1 us
    ppermute x15, waiting for transfers between devices, along_head(): return lax.ppermute(x, HEAD, [(i, i ^ by) for i in range(4)]) if by else x  4.76 us
  transfers between devices with their start and end apart: 31, of which 13 were waited for; matrix products, arithmetic and copies ran while one was open for 1% of the time, Pallas kernels for 10%

profile of v4, /device:TPU:1, one launch (start us, length us, event | category | flops | bytes accessed | tf_op | source)
XLA Modules:
  0.0 105.2 jit_solution(8422267761671672148)
XLA Ops:
  0.6 2.2 %norm.1 = (bf16[1280,128]{1,0:T(8,128)(2,1)}, bf16[640,128]{1,0:T(8,128)(2,1)}, bf16[320,128]{1,0:T(8,128)(2,1)}, f32[320,128]{1,0:T(8,128)}, f32[8,128]{1,0:T(8,128)}) custom-call(s32[1]{0:T(128)} %bitcast.1.head, bf16[128,1280]{1,0:T(8,128)(2,1)} %patches_far.1, f32[10,128]{1,0:T(8,128)} %bitcast.36, bf16[320,128]{1,0:T(8,128)(2,1)} %bitcast.31), custom_call_target="tpu_custom_call" | custom-call | flops 1000 | bytes 1000 | tf_op jit(solution)/shard_map/norm/pallas_call | solution.py:32
  2.9 2.6 %collective-permute-start.3 = (bf16[640,128]{1,0:T(8,128)(2,1)}, bf16[640,128]{1,0:T(8,128)(2,1)S(1)}, u32[]{:S(2)}, u32[]{:S(2)}) collective-permute-start(bf16[640,128]{1,0:T(8,128)(2,1)} %get-tuple-element.45), channel_id=1, source_target_pairs={{0,4},{4,0},{8,12},{12,8},{16,20},{20,16},{24,28},{28,24},{1,5},{5... | collective-permute-start | bytes 491528 | tf_op jit(solution)/shard_map/ppermute | solution.py:305
  5.4 2.8 %collective-permute-start.4 = (bf16[640,128]{1,0:T(8,128)(2,1)}, bf16[640,128]{1,0:T(8,128)(2,1)S(1)}, u32[]{:S(2)}, u32[]{:S(2)}) collective-permute-start(bf16[640,128]{1,0:T(8,128)(2,1)} %get-tuple-element.45), channel_id=1, source_target_pairs={{0,12},{4,8},{8,4},{12,0},{16,28},{20,24},{24,20},{28,16},{1,13},{... | collective-permute-start | bytes 491528 | tf_op jit(solution)/shard_map/ppermute | solution.py:305
  10.8 3.4 %project.1.proj = bf16[960,128]{1,0:T(8,128)(2,1)} custom-call(bf16[1280,128]{1,0:T(8,128)(2,1)} %get-tuple-element.40.normed, bf16[960,1280]{1,0:T(8,128)(2,1)} %bitcast.28), custom_call_target="tpu_custom_call" | custom-call | flops 1000 | bytes 1000 | tf_op jit(solution)/shard_map/project/pallas_call | solution.py:32
  14.3 1.4 %collective-permute-done.2.c3 = bf16[320,128]{1,0:T(8,128)(2,1)S(1)} collective-permute-done((bf16[320,128]{1,0:T(8,128)(2,1)}, bf16[320,128]{1,0:T(8,128)(2,1)S(1)}, u32[]{:S(2)}, u32[]{:S(2)}) %collective-permute-start.2) | collective-permute-done | bytes 81952 | tf_op jit(solution)/shard_map/ppermute | solution.py:309
  18.4 5.1 %collective-permute-start.6 = (bf16[336,128]{1,0:T(8,128)(2,1)S(1)}, bf16[336,128]{1,0:T(8,128)(2,1)S(1)}, u32[]{:S(2)}, u32[]{:S(2)}) collective-permute-start(bf16[336,128]{1,0:T(8,128)(2,1)S(1)} %get-tuple-element.46.r0), channel_id=1, source_target_pairs={{0,16},{4,20},{8,24},{12,28},{16,0},{20,4},{24,8},{28,12},{1,17},{... | collective-permute-start | bytes 258056 | tf_op jit(solution)/shard_map/ppermute | solution.py:305
  23.5 4.0 %collective-permute-start.8 = (bf16[336,128]{1,0:T(8,128)(2,1)S(1)}, bf16[336,128]{1,0:T(8,128)(2,1)S(1)}, u32[]{:S(2)}, u32[]{:S(2)}) collective-permute-start(bf16[336,128]{1,0:T(8,128)(2,1)S(1)} %get-tuple-element.48), channel_id=1, source_target_pairs={{0,24},{4,28},{8,16},{12,20},{16,8},{20,12},{24,0},{28,4},{1,25},{... | collective-permute-start | bytes 258056 | tf_op jit(solution)/shard_map/ppermute | solution.py:305
  27.6 1.6 %collective-permute-start.10 = (bf16[336,128]{1,0:T(8,128)(2,1)S(1)}, bf16[336,128]{1,0:T(8,128)(2,1)S(1)}, u32[]{:S(2)}, u32[]{:S(2)}) collective-permute-start(bf16[336,128]{1,0:T(8,128)(2,1)S(1)} %get-tuple-element.48), channel_id=1, source_target_pairs={{0,8},{4,12},{8,0},{12,4},{16,24},{20,28},{24,16},{28,20},{1,9},{5... | collective-permute-start | bytes 258056 | tf_op jit(solution)/shard_map/ppermute | solution.py:305
  29.2 3.6 %collective-permute-done.7.r5 = bf16[336,128]{1,0:T(8,128)(2,1)S(1)} collective-permute-done((bf16[336,128]{1,0:T(8,128)(2,1)S(1)}, bf16[336,128]{1,0:T(8,128)(2,1)S(1)}, u32[]{:S(2)}, u32[]{:S(2)}) %collective-permute-start.7) | collective-permute-done | bytes 86048 | tf_op jit(solution)/shard_map/ppermute | solution.py:305
  32.8 1.4 %collective-permute-start.11 = (bf16[336,128]{1,0:T(8,128)(2,1)S(1)}, bf16[336,128]{1,0:T(8,128)(2,1)S(1)}, u32[]{:S(2)}, u32[]{:S(2)}) collective-permute-start(bf16[336,128]{1,0:T(8,128)(2,1)S(1)} %get-tuple-element.49), channel_id=1, source_target_pairs={{0,12},{4,8},{8,4},{12,0},{16,28},{20,24},{24,20},{28,16},{1,13},{... | collective-permute-start | bytes 258056 | tf_op jit(solution)/shard_map/ppermute | solution.py:305
  34.2 1.9 %collective-permute-done.8.r6 = bf16[336,128]{1,0:T(8,128)(2,1)S(1)} collective-permute-done((bf16[336,128]{1,0:T(8,128)(2,1)S(1)}, bf16[336,128]{1,0:T(8,128)(2,1)S(1)}, u32[]{:S(2)}, u32[]{:S(2)}) %collective-permute-start.8) | collective-permute-done | bytes 86048 | tf_op jit(solution)/shard_map/ppermute | solution.py:305
  38.1 2.3 %collective-permute-done.11.r3 = bf16[336,128]{1,0:T(8,128)(2,1)S(1)} collective-permute-done((bf16[336,128]{1,0:T(8,128)(2,1)S(1)}, bf16[336,128]{1,0:T(8,128)(2,1)S(1)}, u32[]{:S(2)}, u32[]{:S(2)}) %collective-permute-start.11) | collective-permute-done | bytes 86048 | tf_op jit(solution)/shard_map/ppermute | solution.py:305
  40.4 4.4 %collective-permute-start.12 = (bf16[3,336,128]{2,1,0:T(8,128)(2,1)S(1)}, bf16[3,336,128]{2,1,0:T(8,128)(2,1)S(1)}, u32[]{:S(2)}, u32[]{:S(2)}) collective-permute-start(bf16[3,336,128]{2,1,0:T(8,128)(2,1)S(1)} %near.1), channel_id=1, source_target_pairs={{0,32},{4,36},{8,40},{12,44},{32,64},{36,68},{40,72},{44,76},{48,1... | collective-permute-start | bytes 774152 | tf_op jit(solution)/shard_map/ppermute | solution.py:318
  44.7 1.5 %collective-permute-start.13 = (bf16[1920,128]{1,0:T(8,128)(2,1)S(1)}, bf16[1920,128]{1,0:T(8,128)(2,1)S(1)}, u32[]{:S(2)}, u32[]{:S(2)}) collective-permute-start(bf16[1920,128]{1,0:T(8,128)(2,1)S(1)} %constant_dynamic-update-slice_fusion.refs_0_), channel_id=1, source_target_pairs={{0,1},{1,0},{2,3},{3,2},{4,5},{5,4},{6,7},{7,6},{8,9},{9,8},{10,11... | collective-permute-start | bytes 1474568 | tf_op jit(solution)/shard_map/ppermute | solution.py:309
  47.7 2.1 %collective-permute-done.5.r1 = bf16[336,128]{1,0:T(8,128)(2,1)S(1)} collective-permute-done((bf16[336,128]{1,0:T(8,128)(2,1)S(1)}, bf16[336,128]{1,0:T(8,128)(2,1)S(1)}, u32[]{:S(2)}, u32[]{:S(2)}) %collective-permute-start.5) | collective-permute-done | bytes 86048 | tf_op jit(solution)/shard_map/ppermute | solution.py:305
  49.8 1.7 %collective-permute-start.17 = (bf16[640,128]{1,0:T(8,128)(2,1)S(1)}, bf16[640,128]{1,0:T(8,128)(2,1)S(1)}, u32[]{:S(2)}, u32[]{:S(2)}) collective-permute-start(bf16[640,128]{1,0:T(8,128)(2,1)S(1)} %collective-permute-done.16.refs_4_), channel_id=1, source_target_pairs={{0,1},{1,0},{2,3},{3,2},{4,5},{5,4},{6,7},{7,6},{8,9},{9,8},{10,11... | collective-permute-start | bytes 491528 | tf_op jit(solution)/shard_map/ppermute | solution.py:309
  51.5 1.7 %collective-permute-done.18.refs_6_ = bf16[640,128]{1,0:T(8,128)(2,1)S(1)} collective-permute-done((bf16[640,128]{1,0:T(8,128)(2,1)S(1)}, bf16[640,128]{1,0:T(8,128)(2,1)S(1)}, u32[]{:S(2)}, u32[]{:S(2)}) %collective-permute-start.18) | collective-permute-done | bytes 163872 | tf_op jit(solution)/shard_map/ppermute | solution.py:309
  53.2 2.1 %collective-permute-start.19 = (bf16[640,128]{1,0:T(8,128)(2,1)S(1)}, bf16[640,128]{1,0:T(8,128)(2,1)S(1)}, u32[]{:S(2)}, u32[]{:S(2)}) collective-permute-start(bf16[640,128]{1,0:T(8,128)(2,1)S(1)} %collective-permute-done.18.refs_6_), channel_id=1, source_target_pairs={{0,1},{1,0},{2,3},{3,2},{4,5},{5,4},{6,7},{7,6},{8,9},{9,8},{10,11... | collective-permute-start | bytes 491528 | tf_op jit(solution)/shard_map/ppermute | solution.py:309
  55.3 4.1 %attention.1.grads = bf16[4,320,128]{2,1,0:T(8,128)(2,1)S(1)} custom-call(s32[1]{0:T(128)} %bitcast.zz, bf16[336,128]{1,0:T(8,128)(2,1)S(1)} %get-tuple-element.46.r0, bf16[336,128]{1,0:T(8,128)(2,1)S(1)} %collective-permute-done.5.r1, bf16[336,128]{1,0:T(8,128)(2,1)S(1)} %collective-permute-done.10.r2, bf16[336,128]{1,0:T(8,128)(2,1)S(1)} %collective-permute-done.11.r3, ...), custom_call_target="tpu_custom_call" | custom-call | flops 1000 | bytes 1000 | tf_op jit(solution)/shard_map/attention/pallas_call | solution.py:32
  61.9 2.2 %weights.1 = bf16[8,416,128]{2,1,0:T(8,128)(2,1)} custom-call(s32[1]{0:T(128)} %bitcast.zz, bf16[1280,512]{1,0:T(8,128)(2,1)S(1)} %get-tuple-element.55.n, bf16[1280,512]{1,0:T(8,128)(2,1)S(1)} %get-tuple-element.56.c, bf16[4,320,128]{2,1,0:T(8,128)(2,1)S(1)} %attention.1.grads, bf16[960,1280]{1,0:T(8,128)(2,1)S(1)} %bitcast.29), custom_call_target="tpu_custom_call" | custom-call | flops 1000 | bytes 1000 | tf_op jit(solution)/shard_map/weights/pallas_call | solution.py:32
  64.1 6.2 %all-to-all-start = ((bf16[8,416,128]{2,1,0:T(8,128)(2,1)}), bf16[8,416,128]{2,1,0:T(8,128)(2,1)S(1)}, u32[]{:S(2)}, u32[]{:S(2)}) async-start(bf16[8,416,128]{2,1,0:T(8,128)(2,1)} %weights.1), calls=%async_computation | async-start | bytes 1703936 | tf_op jit(solution)/shard_map/all_to_all | solution.py:396
  70.3 1.9 %collective-permute-start.21 = (bf16[320,128]{1,0:T(8,128)(2,1)}, bf16[320,128]{1,0:T(8,128)(2,1)S(1)}, u32[]{:S(2)}, u32[]{:S(2)}) collective-permute-start(bf16[320,128]{1,0:T(8,128)(2,1)} %get-tuple-element.60), channel_id=1, source_target_pairs={{0,8},{4,12},{8,0},{12,4},{16,24},{20,28},{24,16},{28,20},{1,9},{5... | collective-permute-start | bytes 245768 | tf_op jit(solution)/shard_map/ppermute | solution.py:305
  72.2 1.6 %collective-permute-start.22 = (bf16[320,128]{1,0:T(8,128)(2,1)}, bf16[320,128]{1,0:T(8,128)(2,1)S(1)}, u32[]{:S(2)}, u32[]{:S(2)}) collective-permute-start(bf16[320,128]{1,0:T(8,128)(2,1)} %get-tuple-element.61), channel_id=1, source_target_pairs={{0,12},{4,8},{8,4},{12,0},{16,28},{20,24},{24,20},{28,16},{1,13},{... | collective-permute-start | bytes 245768 | tf_op jit(solution)/shard_map/ppermute | solution.py:305
  74.9 3.2 %collective-permute-done.22.b3 = bf16[320,128]{1,0:T(8,128)(2,1)S(1)} collective-permute-done((bf16[320,128]{1,0:T(8,128)(2,1)}, bf16[320,128]{1,0:T(8,128)(2,1)S(1)}, u32[]{:S(2)}, u32[]{:S(2)}) %collective-permute-start.22) | collective-permute-done | bytes 81952 | tf_op jit(solution)/shard_map/ppermute | solution.py:305
  81.9 3.4 %all-to-all-done.got = bf16[8,416,128]{2,1,0:T(8,128)(2,1)S(1)} async-done(((bf16[8,416,128]{2,1,0:T(8,128)(2,1)}), bf16[8,416,128]{2,1,0:T(8,128)(2,1)S(1)}, u32[]{:S(2)}, u32[]{:S(2)}) %all-to-all-start) | async-done | bytes 852000 | tf_op jit(solution)/shard_map/all_to_all | solution.py:396
  86.0 5.3 %all-to-all-start.1 = ((bf16[8,80,128]{2,1,0:T(8,128)(2,1)}), bf16[8,80,128]{2,1,0:T(8,128)(2,1)S(1)}, u32[]{:S(2)}, u32[]{:S(2)}) async-start(bf16[8,80,128]{2,1,0:T(8,128)(2,1)} %middle.1), calls=%async_computation.1 | async-start | bytes 327680 | tf_op jit(solution)/shard_map/all_to_all | solution.py:412
  91.4 1.7 %collective-permute-start.23 = (bf16[656,128]{1,0:T(8,128)(2,1)S(1)}, bf16[656,128]{1,0:T(8,128)(2,1)S(1)}, u32[]{:S(2)}, u32[]{:S(2)}) collective-permute-start(bf16[656,128]{1,0:T(8,128)(2,1)S(1)} %get-tuple-element.73), channel_id=1, source_target_pairs={{0,1},{1,0},{2,3},{3,2},{4,5},{5,4},{6,7},{7,6},{8,9},{9,8},{10,11... | collective-permute-start | bytes 503816 | tf_op jit(solution)/shard_map/ppermute | solution.py:309
  93.3 1.6 %collective-permute-start.25 = (bf16[656,128]{1,0:T(8,128)(2,1)S(1)}, bf16[656,128]{1,0:T(8,128)(2,1)S(1)}, u32[]{:S(2)}, u32[]{:S(2)}) collective-permute-start(bf16[656,128]{1,0:T(8,128)(2,1)S(1)} %get-tuple-element.71), channel_id=1, source_target_pairs={{0,3},{1,2},{2,1},{3,0},{4,7},{5,6},{6,5},{7,4},{8,11},{9,10},{10,... | collective-permute-start | bytes 503816 | tf_op jit(solution)/shard_map/ppermute | solution.py:309
  94.9 1.6 %all-to-all-done.1.got = bf16[8,80,128]{2,1,0:T(8,128)(2,1)S(1)} async-done(((bf16[8,80,128]{2,1,0:T(8,128)(2,1)}), bf16[8,80,128]{2,1,0:T(8,128)(2,1)S(1)}, u32[]{:S(2)}, u32[]{:S(2)}) %all-to-all-start.1) | async-done | bytes 163872 | tf_op jit(solution)/shard_map/all_to_all | solution.py:412
  96.5 3.1 %collective-permute-start.26 = (f32[16,128]{1,0:T(8,128)S(1)}, f32[16,128]{1,0:T(8,128)S(1)}, u32[]{:S(2)}, u32[]{:S(2)}) collective-permute-start(f32[16,128]{1,0:T(8,128)S(1)} %tails.1.t0), channel_id=1, source_target_pairs={{0,1},{1,0},{2,3},{3,2},{4,5},{5,4},{6,7},{7,6},{8,9},{9,8},{10,11... | collective-permute-start | bytes 24584 | tf_op jit(solution)/shard_map/ppermute | solution.py:309
  99.8 1.5 %collective-permute-start.28 = (f32[16,128]{1,0:T(8,128)S(1)}, f32[16,128]{1,0:T(8,128)S(1)}, u32[]{:S(2)}, u32[]{:S(2)}) collective-permute-start(f32[16,128]{1,0:T(8,128)S(1)} %tails.1.t0), channel_id=1, source_target_pairs={{0,3},{1,2},{2,1},{3,0},{4,7},{5,6},{6,5},{7,4},{8,11},{9,10},{10,... | collective-permute-start | bytes 24584 | tf_op jit(solution)/shard_map/ppermute | solution.py:309
  101.3 1.6 %collective-permute-done.25.g3 = bf16[656,128]{1,0:T(8,128)(2,1)S(1)} collective-permute-done((bf16[656,128]{1,0:T(8,128)(2,1)S(1)}, bf16[656,128]{1,0:T(8,128)(2,1)S(1)}, u32[]{:S(2)}, u32[]{:S(2)}) %collective-permute-start.25) | collective-permute-done | bytes 167968 | tf_op jit(solution)/shard_map/ppermute | solution.py:309
  (78 shorter events, 19.5 us)
Async XLA Ops:
  2.9 14.2 %collective-permute-start.3 = (bf16[640,128]{1,0:T(8,128)(2,1)}, bf16[640,128]{1,0:T(8,128)(2,1)S(1)}, u32[]{:S(2)}, u32[]{:S(2)}) collective-permute-start(bf16[640,128]{1,0:T(8,128)(2,1)} %get-tuple-element.45), channel_id=1, source_target_pairs={{0,4},{4,0},{8,12},{12,8},{16,20},{20,16},{24,28},{28,24},{1,5},{5... | collective-permute-start | bytes 491528 | tf_op jit(solution)/shard_map/ppermute | solution.py:305
  5.4 11.6 %collective-permute-start.4 = (bf16[640,128]{1,0:T(8,128)(2,1)}, bf16[640,128]{1,0:T(8,128)(2,1)S(1)}, u32[]{:S(2)}, u32[]{:S(2)}) collective-permute-start(bf16[640,128]{1,0:T(8,128)(2,1)} %get-tuple-element.45), channel_id=1, source_target_pairs={{0,12},{4,8},{8,4},{12,0},{16,28},{20,24},{24,20},{28,16},{1,13},{... | collective-permute-start | bytes 491528 | tf_op jit(solution)/shard_map/ppermute | solution.py:305
  8.2 6.0 %collective-permute-start = (bf16[320,128]{1,0:T(8,128)(2,1)}, bf16[320,128]{1,0:T(8,128)(2,1)S(1)}, u32[]{:S(2)}, u32[]{:S(2)}) collective-permute-start(bf16[320,128]{1,0:T(8,128)(2,1)} %bitcast.32), channel_id=1, source_target_pairs={{0,1},{1,0},{2,3},{3,2},{4,5},{5,4},{6,7},{7,6},{8,9},{9,8},{10,11... | collective-permute-start | bytes 245768 | tf_op jit(solution)/shard_map/ppermute | solution.py:309
  9.2 5.1 %collective-permute-start.1 = (bf16[320,128]{1,0:T(8,128)(2,1)}, bf16[320,128]{1,0:T(8,128)(2,1)S(1)}, u32[]{:S(2)}, u32[]{:S(2)}) collective-permute-start(bf16[320,128]{1,0:T(8,128)(2,1)} %bitcast.33), channel_id=1, source_target_pairs={{0,2},{1,3},{2,0},{3,1},{4,6},{5,7},{6,4},{7,5},{8,10},{9,11},{10,... | collective-permute-start | bytes 245768 | tf_op jit(solution)/shard_map/ppermute | solution.py:309
  10.4 5.2 %collective-permute-start.2 = (bf16[320,128]{1,0:T(8,128)(2,1)}, bf16[320,128]{1,0:T(8,128)(2,1)S(1)}, u32[]{:S(2)}, u32[]{:S(2)}) collective-permute-start(bf16[320,128]{1,0:T(8,128)(2,1)} %bitcast.34), channel_id=1, source_target_pairs={{0,3},{1,2},{2,1},{3,0},{4,7},{5,6},{6,5},{7,4},{8,11},{9,10},{10,... | collective-permute-start | bytes 245768 | tf_op jit(solution)/shard_map/ppermute | solution.py:309
  17.1 29.2 %collective-permute-start.14 = (bf16[1920,128]{1,0:T(8,128)(2,1)S(1)}, bf16[1920,128]{1,0:T(8,128)(2,1)S(1)}, u32[]{:S(2)}, u32[]{:S(2)}) collective-permute-start(bf16[1920,128]{1,0:T(8,128)(2,1)S(1)} %constant_dynamic-update-slice_fusion.refs_0_), channel_id=1, source_target_pairs={{0,2},{1,3},{2,0},{3,1},{4,6},{5,7},{6,4},{7,5},{8,10},{9,11},{10,... | collective-permute-start | bytes 1474568 | tf_op jit(solution)/shard_map/ppermute | solution.py:309
  18.4 9.2 %collective-permute-start.6 = (bf16[336,128]{1,0:T(8,128)(2,1)S(1)}, bf16[336,128]{1,0:T(8,128)(2,1)S(1)}, u32[]{:S(2)}, u32[]{:S(2)}) collective-permute-start(bf16[336,128]{1,0:T(8,128)(2,1)S(1)} %get-tuple-element.46.r0), channel_id=1, source_target_pairs={{0,16},{4,20},{8,24},{12,28},{16,0},{20,4},{24,8},{28,12},{1,17},{... | collective-permute-start | bytes 258056 | tf_op jit(solution)/shard_map/ppermute | solution.py:305
  23.5 9.3 %collective-permute-start.7 = (bf16[336,128]{1,0:T(8,128)(2,1)S(1)}, bf16[336,128]{1,0:T(8,128)(2,1)S(1)}, u32[]{:S(2)}, u32[]{:S(2)}) collective-permute-start(bf16[336,128]{1,0:T(8,128)(2,1)S(1)} %get-tuple-element.47), channel_id=1, source_target_pairs={{0,20},{4,16},{8,28},{12,24},{16,4},{20,0},{24,12},{28,8},{1,21},{... | collective-permute-start | bytes 258056 | tf_op jit(solution)/shard_map/ppermute | solution.py:305
  23.5 12.5 %collective-permute-start.8 = (bf16[336,128]{1,0:T(8,128)(2,1)S(1)}, bf16[336,128]{1,0:T(8,128)(2,1)S(1)}, u32[]{:S(2)}, u32[]{:S(2)}) collective-permute-start(bf16[336,128]{1,0:T(8,128)(2,1)S(1)} %get-tuple-element.48), channel_id=1, source_target_pairs={{0,24},{4,28},{8,16},{12,20},{16,8},{20,12},{24,0},{28,4},{1,25},{... | collective-permute-start | bytes 258056 | tf_op jit(solution)/shard_map/ppermute | solution.py:305
  27.5 10.5 %collective-permute-start.9 = (bf16[336,128]{1,0:T(8,128)(2,1)S(1)}, bf16[336,128]{1,0:T(8,128)(2,1)S(1)}, u32[]{:S(2)}, u32[]{:S(2)}) collective-permute-start(bf16[336,128]{1,0:T(8,128)(2,1)S(1)} %get-tuple-element.49), channel_id=1, source_target_pairs={{0,28},{4,24},{8,20},{12,16},{16,12},{20,8},{24,4},{28,0},{1,29},{... | collective-permute-start | bytes 258056 | tf_op jit(solution)/shard_map/ppermute | solution.py:305
  27.6 10.5 %collective-permute-start.10 = (bf16[336,128]{1,0:T(8,128)(2,1)S(1)}, bf16[336,128]{1,0:T(8,128)(2,1)S(1)}, u32[]{:S(2)}, u32[]{:S(2)}) collective-permute-start(bf16[336,128]{1,0:T(8,128)(2,1)S(1)} %get-tuple-element.48), channel_id=1, source_target_pairs={{0,8},{4,12},{8,0},{12,4},{16,24},{20,28},{24,16},{28,20},{1,9},{5... | collective-permute-start | bytes 258056 | tf_op jit(solution)/shard_map/ppermute | solution.py:305
  32.8 7.6 %collective-permute-start.11 = (bf16[336,128]{1,0:T(8,128)(2,1)S(1)}, bf16[336,128]{1,0:T(8,128)(2,1)S(1)}, u32[]{:S(2)}, u32[]{:S(2)}) collective-permute-start(bf16[336,128]{1,0:T(8,128)(2,1)S(1)} %get-tuple-element.49), channel_id=1, source_target_pairs={{0,12},{4,8},{8,4},{12,0},{16,28},{20,24},{24,20},{28,16},{1,13},{... | collective-permute-start | bytes 258056 | tf_op jit(solution)/shard_map/ppermute | solution.py:305
  36.0 10.3 %collective-permute-start.16 = (bf16[640,128]{1,0:T(8,128)(2,1)S(1)}, bf16[640,128]{1,0:T(8,128)(2,1)S(1)}, u32[]{:S(2)}, u32[]{:S(2)}) collective-permute-start(bf16[640,128]{1,0:T(8,128)(2,1)S(1)} %collective-permute-done.4), channel_id=1, source_target_pairs={{0,4},{4,0},{8,12},{12,8},{16,20},{20,16},{24,28},{28,24},{1,5},{5... | collective-permute-start | bytes 491528 | tf_op jit(solution)/shard_map/ppermute | solution.py:305
  40.4 15.0 %collective-permute-start.12 = (bf16[3,336,128]{2,1,0:T(8,128)(2,1)S(1)}, bf16[3,336,128]{2,1,0:T(8,128)(2,1)S(1)}, u32[]{:S(2)}, u32[]{:S(2)}) collective-permute-start(bf16[3,336,128]{2,1,0:T(8,128)(2,1)S(1)} %near.1), channel_id=1, source_target_pairs={{0,32},{4,36},{8,40},{12,44},{32,64},{36,68},{40,72},{44,76},{48,1... | collective-permute-start | bytes 774152 | tf_op jit(solution)/shard_map/ppermute | solution.py:318
  44.7 15.5 %collective-permute-start.13 = (bf16[1920,128]{1,0:T(8,128)(2,1)S(1)}, bf16[1920,128]{1,0:T(8,128)(2,1)S(1)}, u32[]{:S(2)}, u32[]{:S(2)}) collective-permute-start(bf16[1920,128]{1,0:T(8,128)(2,1)S(1)} %constant_dynamic-update-slice_fusion.refs_0_), channel_id=1, source_target_pairs={{0,1},{1,0},{2,3},{3,2},{4,5},{5,4},{6,7},{7,6},{8,9},{9,8},{10,11... | collective-permute-start | bytes 1474568 | tf_op jit(solution)/shard_map/ppermute | solution.py:309
  46.3 13.9 %collective-permute-start.15 = (bf16[1920,128]{1,0:T(8,128)(2,1)S(1)}, bf16[1920,128]{1,0:T(8,128)(2,1)S(1)}, u32[]{:S(2)}, u32[]{:S(2)}) collective-permute-start(bf16[1920,128]{1,0:T(8,128)(2,1)S(1)} %collective-permute-done.14.refs_2_), channel_id=1, source_target_pairs={{0,1},{1,0},{2,3},{3,2},{4,5},{5,4},{6,7},{7,6},{8,9},{9,8},{10,11... | collective-permute-start | bytes 1474568 | tf_op jit(solution)/shard_map/ppermute | solution.py:309
  46.4 6.9 %collective-permute-start.18 = (bf16[640,128]{1,0:T(8,128)(2,1)S(1)}, bf16[640,128]{1,0:T(8,128)(2,1)S(1)}, u32[]{:S(2)}, u32[]{:S(2)}) collective-permute-start(bf16[640,128]{1,0:T(8,128)(2,1)S(1)} %collective-permute-done.16.refs_4_), channel_id=1, source_target_pairs={{0,2},{1,3},{2,0},{3,1},{4,6},{5,7},{6,4},{7,5},{8,10},{9,11},{10,... | collective-permute-start | bytes 491528 | tf_op jit(solution)/shard_map/ppermute | solution.py:309
  46.4 3.4 %collective-permute-start.5 = (bf16[336,128]{1,0:T(8,128)(2,1)S(1)}, bf16[336,128]{1,0:T(8,128)(2,1)S(1)}, u32[]{:S(2)}, u32[]{:S(2)}) collective-permute-start(bf16[336,128]{1,0:T(8,128)(2,1)S(1)} %get-tuple-element.47), channel_id=1, source_target_pairs={{0,4},{4,0},{8,12},{12,8},{16,20},{20,16},{24,28},{28,24},{1,5},{5... | collective-permute-start | bytes 258056 | tf_op jit(solution)/shard_map/ppermute | solution.py:305
  49.8 10.4 %collective-permute-start.17 = (bf16[640,128]{1,0:T(8,128)(2,1)S(1)}, bf16[640,128]{1,0:T(8,128)(2,1)S(1)}, u32[]{:S(2)}, u32[]{:S(2)}) collective-permute-start(bf16[640,128]{1,0:T(8,128)(2,1)S(1)} %collective-permute-done.16.refs_4_), channel_id=1, source_target_pairs={{0,1},{1,0},{2,3},{3,2},{4,5},{5,4},{6,7},{7,6},{8,9},{9,8},{10,11... | collective-permute-start | bytes 491528 | tf_op jit(solution)/shard_map/ppermute | solution.py:309
  53.2 7.0 %collective-permute-start.19 = (bf16[640,128]{1,0:T(8,128)(2,1)S(1)}, bf16[640,128]{1,0:T(8,128)(2,1)S(1)}, u32[]{:S(2)}, u32[]{:S(2)}) collective-permute-start(bf16[640,128]{1,0:T(8,128)(2,1)S(1)} %collective-permute-done.18.refs_6_), channel_id=1, source_target_pairs={{0,1},{1,0},{2,3},{3,2},{4,5},{5,4},{6,7},{7,6},{8,9},{9,8},{10,11... | collective-permute-start | bytes 491528 | tf_op jit(solution)/shard_map/ppermute | solution.py:309
  64.1 21.1 %all-to-all-start = ((bf16[8,416,128]{2,1,0:T(8,128)(2,1)}), bf16[8,416,128]{2,1,0:T(8,128)(2,1)S(1)}, u32[]{:S(2)}, u32[]{:S(2)}) async-start(bf16[8,416,128]{2,1,0:T(8,128)(2,1)} %weights.1), calls=%async_computation | async-start | bytes 1703936 | tf_op jit(solution)/shard_map/all_to_all | solution.py:396
  70.3 4.0 %collective-permute-start.20 = (bf16[320,128]{1,0:T(8,128)(2,1)}, bf16[320,128]{1,0:T(8,128)(2,1)S(1)}, u32[]{:S(2)}, u32[]{:S(2)}) collective-permute-start(bf16[320,128]{1,0:T(8,128)(2,1)} %get-tuple-element.59), channel_id=1, source_target_pairs={{0,4},{4,0},{8,12},{12,8},{16,20},{20,16},{24,28},{28,24},{1,5},{5... | collective-permute-start | bytes 245768 | tf_op jit(solution)/shard_map/ppermute | solution.py:305
  70.3 4.6 %collective-permute-start.21 = (bf16[320,128]{1,0:T(8,128)(2,1)}, bf16[320,128]{1,0:T(8,128)(2,1)S(1)}, u32[]{:S(2)}, u32[]{:S(2)}) collective-permute-start(bf16[320,128]{1,0:T(8,128)(2,1)} %get-tuple-element.60), channel_id=1, source_target_pairs={{0,8},{4,12},{8,0},{12,4},{16,24},{20,28},{24,16},{28,20},{1,9},{5... | collective-permute-start | bytes 245768 | tf_op jit(solution)/shard_map/ppermute | solution.py:305
  72.2 5.9 %collective-permute-start.22 = (bf16[320,128]{1,0:T(8,128)(2,1)}, bf16[320,128]{1,0:T(8,128)(2,1)S(1)}, u32[]{:S(2)}, u32[]{:S(2)}) collective-permute-start(bf16[320,128]{1,0:T(8,128)(2,1)} %get-tuple-element.61), channel_id=1, source_target_pairs={{0,12},{4,8},{8,4},{12,0},{16,28},{20,24},{24,20},{28,16},{1,13},{... | collective-permute-start | bytes 245768 | tf_op jit(solution)/shard_map/ppermute | solution.py:305
  81.9 21.1 %copy-start.12 = (f32[8,128]{1,0:T(8,128)S(1)}, f32[8,128]{1,0:T(8,128)}, u32[]{:S(2)}) copy-start(f32[8,128]{1,0:T(8,128)} %get-tuple-element.65.inv) | copy-start | bytes 12292
  86.0 10.4 %all-to-all-start.1 = ((bf16[8,80,128]{2,1,0:T(8,128)(2,1)}), bf16[8,80,128]{2,1,0:T(8,128)(2,1)S(1)}, u32[]{:S(2)}, u32[]{:S(2)}) async-start(bf16[8,80,128]{2,1,0:T(8,128)(2,1)} %middle.1), calls=%async_computation.1 | async-start | bytes 327680 | tf_op jit(solution)/shard_map/all_to_all | solution.py:412
  91.4 8.4 %collective-permute-start.23 = (bf16[656,128]{1,0:T(8,128)(2,1)S(1)}, bf16[656,128]{1,0:T(8,128)(2,1)S(1)}, u32[]{:S(2)}, u32[]{:S(2)}) collective-permute-start(bf16[656,128]{1,0:T(8,128)(2,1)S(1)} %get-tuple-element.73), channel_id=1, source_target_pairs={{0,1},{1,0},{2,3},{3,2},{4,5},{5,4},{6,7},{7,6},{8,9},{9,8},{10,11... | collective-permute-start | bytes 503816 | tf_op jit(solution)/shard_map/ppermute | solution.py:309
  93.1 8.2 %collective-permute-start.24 = (bf16[656,128]{1,0:T(8,128)(2,1)S(1)}, bf16[656,128]{1,0:T(8,128)(2,1)S(1)}, u32[]{:S(2)}, u32[]{:S(2)}) collective-permute-start(bf16[656,128]{1,0:T(8,128)(2,1)S(1)} %get-tuple-element.72), channel_id=1, source_target_pairs={{0,2},{1,3},{2,0},{3,1},{4,6},{5,7},{6,4},{7,5},{8,10},{9,11},{10,... | collective-permute-start | bytes 503816 | tf_op jit(solution)/shard_map/ppermute | solution.py:309
  93.3 9.6 %collective-permute-start.25 = (bf16[656,128]{1,0:T(8,128)(2,1)S(1)}, bf16[656,128]{1,0:T(8,128)(2,1)S(1)}, u32[]{:S(2)}, u32[]{:S(2)}) collective-permute-start(bf16[656,128]{1,0:T(8,128)(2,1)S(1)} %get-tuple-element.71), channel_id=1, source_target_pairs={{0,3},{1,2},{2,1},{3,0},{4,7},{5,6},{6,5},{7,4},{8,11},{9,10},{10,... | collective-permute-start | bytes 503816 | tf_op jit(solution)/shard_map/ppermute | solution.py:309
  96.5 8.0 %collective-permute-start.26 = (f32[16,128]{1,0:T(8,128)S(1)}, f32[16,128]{1,0:T(8,128)S(1)}, u32[]{:S(2)}, u32[]{:S(2)}) collective-permute-start(f32[16,128]{1,0:T(8,128)S(1)} %tails.1.t0), channel_id=1, source_target_pairs={{0,1},{1,0},{2,3},{3,2},{4,5},{5,4},{6,7},{7,6},{8,9},{9,8},{10,11... | collective-permute-start | bytes 24584 | tf_op jit(solution)/shard_map/ppermute | solution.py:309
  99.6 4.9 %collective-permute-start.27 = (f32[16,128]{1,0:T(8,128)S(1)}, f32[16,128]{1,0:T(8,128)S(1)}, u32[]{:S(2)}, u32[]{:S(2)}) collective-permute-start(f32[16,128]{1,0:T(8,128)S(1)} %tails.1.t0), channel_id=1, source_target_pairs={{0,2},{1,3},{2,0},{3,1},{4,6},{5,7},{6,4},{7,5},{8,10},{9,11},{10,... | collective-permute-start | bytes 24584 | tf_op jit(solution)/shard_map/ppermute | solution.py:309
  99.8 4.7 %collective-permute-start.28 = (f32[16,128]{1,0:T(8,128)S(1)}, f32[16,128]{1,0:T(8,128)S(1)}, u32[]{:S(2)}, u32[]{:S(2)}) collective-permute-start(f32[16,128]{1,0:T(8,128)S(1)} %tails.1.t0), channel_id=1, source_target_pairs={{0,3},{1,2},{2,1},{3,0},{4,7},{5,6},{6,5},{7,4},{8,11},{9,10},{10,... | collective-permute-start | bytes 24584 | tf_op jit(solution)/shard_map/ppermute | solution.py:309
  (14 other events, 98.8 us)

commit v5 on v4

--- a/solution.py
+++ b/solution.py
@@ -391,6 +391,7 @@
         c,
         grads,
         w,
+        limit=44,
     )
     backs, terms = lax.optimization_barrier((backs, terms))
     terms = lax.all_to_all(terms, ("y", "xh"), 0, 0, tiled=True)

time: 106 us -> 106 us (level)
  no operation moved by 1% of the time
where the time goes in v5:
time: 106 us; the launch traced here: 105 us
  starting transfers between devices  56.9 us (54%)
  waiting for transfers between devices  24.7 us (23%)
  Pallas kernels  16.7 us (16%)
  local copies, waits for them, and re-layouts  5.9 us (6%)
    ppermute x13, starting transfers between devices, along_z(): return lax.ppermute(x, 'z', [(i, i ^ by) for i in range(8)]) if by else x  23.4 us
    ppermute x15, starting transfers between devices, along_head(): return lax.ppermute(x, HEAD, [(i, i ^ by) for i in range(4)]) if by else x  17.6 us
    pallas_call x13, Pallas kernels, call(): pl.pallas_call(kernel, out_shape=outs, in_specs=specs, out_specs=vmem if...  16.7 us
    ppermute x13, waiting for transfers between devices, along_z(): return lax.ppermute(x, 'z', [(i, i ^ by) for i in range(8)]) if by else x  15 us
    all_to_all x1, starting transfers between devices, body(): terms = lax.all_to_all(terms, ('y', 'xh'), 0, 0, tiled=True)  6.19 us
    all_to_all x1, starting transfers between devices, body(): lax.all_to_all(terms, 'z', 0, 0, tiled=True, axis_index_groups=[list(rang...  5.3 us
    unnamed x32, local copies, waits for them, and re-layouts  5.1 us
    ppermute x15, waiting for transfers between devices, along_head(): return lax.ppermute(x, HEAD, [(i, i ^ by) for i in range(4)]) if by else x  4.76 us
  transfers between devices with their start and end apart: 31, of which 13 were waited for; matrix products, arithmetic and copies ran while one was open for 1% of the time, Pallas kernels for 10%

profile of v5, /device:TPU:1, one launch (start us, length us, event | category | flops | bytes accessed | tf_op | source)
XLA Modules:
  0.0 105.2 jit_solution(7734453539903313621)
XLA Ops:
  0.6 2.2 %norm.1 = (bf16[1280,128]{1,0:T(8,128)(2,1)}, bf16[640,128]{1,0:T(8,128)(2,1)}, bf16[320,128]{1,0:T(8,128)(2,1)}, f32[320,128]{1,0:T(8,128)}, f32[8,128]{1,0:T(8,128)}) custom-call(s32[1]{0:T(128)} %bitcast.1.head, bf16[128,1280]{1,0:T(8,128)(2,1)} %patches_far.1, f32[10,128]{1,0:T(8,128)} %bitcast.36, bf16[320,128]{1,0:T(8,128)(2,1)} %bitcast.31), custom_call_target="tpu_custom_call" | custom-call | flops 1000 | bytes 1000 | tf_op jit(solution)/shard_map/norm/pallas_call | solution.py:32
  2.9 2.6 %collective-permute-start.3 = (bf16[640,128]{1,0:T(8,128)(2,1)}, bf16[640,128]{1,0:T(8,128)(2,1)S(1)}, u32[]{:S(2)}, u32[]{:S(2)}) collective-permute-start(bf16[640,128]{1,0:T(8,128)(2,1)} %get-tuple-element.45), channel_id=1, source_target_pairs={{0,4},{4,0},{8,12},{12,8},{16,20},{20,16},{24,28},{28,24},{1,5},{5... | collective-permute-start | bytes 491528 | tf_op jit(solution)/shard_map/ppermute | solution.py:305
  5.4 2.8 %collective-permute-start.4 = (bf16[640,128]{1,0:T(8,128)(2,1)}, bf16[640,128]{1,0:T(8,128)(2,1)S(1)}, u32[]{:S(2)}, u32[]{:S(2)}) collective-permute-start(bf16[640,128]{1,0:T(8,128)(2,1)} %get-tuple-element.45), channel_id=1, source_target_pairs={{0,12},{4,8},{8,4},{12,0},{16,28},{20,24},{24,20},{28,16},{1,13},{... | collective-permute-start | bytes 491528 | tf_op jit(solution)/shard_map/ppermute | solution.py:305
  10.8 3.4 %project.1.proj = bf16[960,128]{1,0:T(8,128)(2,1)} custom-call(bf16[1280,128]{1,0:T(8,128)(2,1)} %get-tuple-element.40.normed, bf16[960,1280]{1,0:T(8,128)(2,1)} %bitcast.28), custom_call_target="tpu_custom_call" | custom-call | flops 1000 | bytes 1000 | tf_op jit(solution)/shard_map/project/pallas_call | solution.py:32
  14.3 1.4 %collective-permute-done.2.c3 = bf16[320,128]{1,0:T(8,128)(2,1)S(1)} collective-permute-done((bf16[320,128]{1,0:T(8,128)(2,1)}, bf16[320,128]{1,0:T(8,128)(2,1)S(1)}, u32[]{:S(2)}, u32[]{:S(2)}) %collective-permute-start.2) | collective-permute-done | bytes 81952 | tf_op jit(solution)/shard_map/ppermute | solution.py:309
  18.4 5.1 %collective-permute-start.6 = (bf16[336,128]{1,0:T(8,128)(2,1)S(1)}, bf16[336,128]{1,0:T(8,128)(2,1)S(1)}, u32[]{:S(2)}, u32[]{:S(2)}) collective-permute-start(bf16[336,128]{1,0:T(8,128)(2,1)S(1)} %get-tuple-element.46.r0), channel_id=1, source_target_pairs={{0,16},{4,20},{8,24},{12,28},{16,0},{20,4},{24,8},{28,12},{1,17},{... | collective-permute-start | bytes 258056 | tf_op jit(solution)/shard_map/ppermute | solution.py:305
  23.5 4.0 %collective-permute-start.8 = (bf16[336,128]{1,0:T(8,128)(2,1)S(1)}, bf16[336,128]{1,0:T(8,128)(2,1)S(1)}, u32[]{:S(2)}, u32[]{:S(2)}) collective-permute-start(bf16[336,128]{1,0:T(8,128)(2,1)S(1)} %get-tuple-element.48), channel_id=1, source_target_pairs={{0,24},{4,28},{8,16},{12,20},{16,8},{20,12},{24,0},{28,4},{1,25},{... | collective-permute-start | bytes 258056 | tf_op jit(solution)/shard_map/ppermute | solution.py:305
  27.6 1.6 %collective-permute-start.10 = (bf16[336,128]{1,0:T(8,128)(2,1)S(1)}, bf16[336,128]{1,0:T(8,128)(2,1)S(1)}, u32[]{:S(2)}, u32[]{:S(2)}) collective-permute-start(bf16[336,128]{1,0:T(8,128)(2,1)S(1)} %get-tuple-element.48), channel_id=1, source_target_pairs={{0,8},{4,12},{8,0},{12,4},{16,24},{20,28},{24,16},{28,20},{1,9},{5... | collective-permute-start | bytes 258056 | tf_op jit(solution)/shard_map/ppermute | solution.py:305
  29.2 3.6 %collective-permute-done.7.r5 = bf16[336,128]{1,0:T(8,128)(2,1)S(1)} collective-permute-done((bf16[336,128]{1,0:T(8,128)(2,1)S(1)}, bf16[336,128]{1,0:T(8,128)(2,1)S(1)}, u32[]{:S(2)}, u32[]{:S(2)}) %collective-permute-start.7) | collective-permute-done | bytes 86048 | tf_op jit(solution)/shard_map/ppermute | solution.py:305
  32.8 1.4 %collective-permute-start.11 = (bf16[336,128]{1,0:T(8,128)(2,1)S(1)}, bf16[336,128]{1,0:T(8,128)(2,1)S(1)}, u32[]{:S(2)}, u32[]{:S(2)}) collective-permute-start(bf16[336,128]{1,0:T(8,128)(2,1)S(1)} %get-tuple-element.49), channel_id=1, source_target_pairs={{0,12},{4,8},{8,4},{12,0},{16,28},{20,24},{24,20},{28,16},{1,13},{... | collective-permute-start | bytes 258056 | tf_op jit(solution)/shard_map/ppermute | solution.py:305
  34.2 1.9 %collective-permute-done.8.r6 = bf16[336,128]{1,0:T(8,128)(2,1)S(1)} collective-permute-done((bf16[336,128]{1,0:T(8,128)(2,1)S(1)}, bf16[336,128]{1,0:T(8,128)(2,1)S(1)}, u32[]{:S(2)}, u32[]{:S(2)}) %collective-permute-start.8) | collective-permute-done | bytes 86048 | tf_op jit(solution)/shard_map/ppermute | solution.py:305
  38.1 2.3 %collective-permute-done.11.r3 = bf16[336,128]{1,0:T(8,128)(2,1)S(1)} collective-permute-done((bf16[336,128]{1,0:T(8,128)(2,1)S(1)}, bf16[336,128]{1,0:T(8,128)(2,1)S(1)}, u32[]{:S(2)}, u32[]{:S(2)}) %collective-permute-start.11) | collective-permute-done | bytes 86048 | tf_op jit(solution)/shard_map/ppermute | solution.py:305
  40.4 4.4 %collective-permute-start.12 = (bf16[3,336,128]{2,1,0:T(8,128)(2,1)S(1)}, bf16[3,336,128]{2,1,0:T(8,128)(2,1)S(1)}, u32[]{:S(2)}, u32[]{:S(2)}) collective-permute-start(bf16[3,336,128]{2,1,0:T(8,128)(2,1)S(1)} %near.1), channel_id=1, source_target_pairs={{0,32},{4,36},{8,40},{12,44},{32,64},{36,68},{40,72},{44,76},{48,1... | collective-permute-start | bytes 774152 | tf_op jit(solution)/shard_map/ppermute | solution.py:318
  44.7 1.5 %collective-permute-start.13 = (bf16[1920,128]{1,0:T(8,128)(2,1)S(1)}, bf16[1920,128]{1,0:T(8,128)(2,1)S(1)}, u32[]{:S(2)}, u32[]{:S(2)}) collective-permute-start(bf16[1920,128]{1,0:T(8,128)(2,1)S(1)} %constant_dynamic-update-slice_fusion.refs_0_), channel_id=1, source_target_pairs={{0,1},{1,0},{2,3},{3,2},{4,5},{5,4},{6,7},{7,6},{8,9},{9,8},{10,11... | collective-permute-start | bytes 1474568 | tf_op jit(solution)/shard_map/ppermute | solution.py:309
  47.7 2.1 %collective-permute-done.5.r1 = bf16[336,128]{1,0:T(8,128)(2,1)S(1)} collective-permute-done((bf16[336,128]{1,0:T(8,128)(2,1)S(1)}, bf16[336,128]{1,0:T(8,128)(2,1)S(1)}, u32[]{:S(2)}, u32[]{:S(2)}) %collective-permute-start.5) | collective-permute-done | bytes 86048 | tf_op jit(solution)/shard_map/ppermute | solution.py:305
  49.8 1.7 %collective-permute-start.17 = (bf16[640,128]{1,0:T(8,128)(2,1)S(1)}, bf16[640,128]{1,0:T(8,128)(2,1)S(1)}, u32[]{:S(2)}, u32[]{:S(2)}) collective-permute-start(bf16[640,128]{1,0:T(8,128)(2,1)S(1)} %collective-permute-done.16.refs_4_), channel_id=1, source_target_pairs={{0,1},{1,0},{2,3},{3,2},{4,5},{5,4},{6,7},{7,6},{8,9},{9,8},{10,11... | collective-permute-start | bytes 491528 | tf_op jit(solution)/shard_map/ppermute | solution.py:309
  51.5 1.7 %collective-permute-done.18.refs_6_ = bf16[640,128]{1,0:T(8,128)(2,1)S(1)} collective-permute-done((bf16[640,128]{1,0:T(8,128)(2,1)S(1)}, bf16[640,128]{1,0:T(8,128)(2,1)S(1)}, u32[]{:S(2)}, u32[]{:S(2)}) %collective-permute-start.18) | collective-permute-done | bytes 163872 | tf_op jit(solution)/shard_map/ppermute | solution.py:309
  53.2 2.1 %collective-permute-start.19 = (bf16[640,128]{1,0:T(8,128)(2,1)S(1)}, bf16[640,128]{1,0:T(8,128)(2,1)S(1)}, u32[]{:S(2)}, u32[]{:S(2)}) collective-permute-start(bf16[640,128]{1,0:T(8,128)(2,1)S(1)} %collective-permute-done.18.refs_6_), channel_id=1, source_target_pairs={{0,1},{1,0},{2,3},{3,2},{4,5},{5,4},{6,7},{7,6},{8,9},{9,8},{10,11... | collective-permute-start | bytes 491528 | tf_op jit(solution)/shard_map/ppermute | solution.py:309
  55.3 4.1 %attention.1.grads = bf16[4,320,128]{2,1,0:T(8,128)(2,1)S(1)} custom-call(s32[1]{0:T(128)} %bitcast.zz, bf16[336,128]{1,0:T(8,128)(2,1)S(1)} %get-tuple-element.46.r0, bf16[336,128]{1,0:T(8,128)(2,1)S(1)} %collective-permute-done.5.r1, bf16[336,128]{1,0:T(8,128)(2,1)S(1)} %collective-permute-done.10.r2, bf16[336,128]{1,0:T(8,128)(2,1)S(1)} %collective-permute-done.11.r3, ...), custom_call_target="tpu_custom_call" | custom-call | flops 1000 | bytes 1000 | tf_op jit(solution)/shard_map/attention/pallas_call | solution.py:32
  61.9 2.2 %weights.1 = bf16[8,416,128]{2,1,0:T(8,128)(2,1)} custom-call(s32[1]{0:T(128)} %bitcast.zz, bf16[1280,512]{1,0:T(8,128)(2,1)S(1)} %get-tuple-element.55.n, bf16[1280,512]{1,0:T(8,128)(2,1)S(1)} %get-tuple-element.56.c, bf16[4,320,128]{2,1,0:T(8,128)(2,1)S(1)} %attention.1.grads, bf16[960,1280]{1,0:T(8,128)(2,1)S(1)} %bitcast.29), custom_call_target="tpu_custom_call" | custom-call | flops 1000 | bytes 1000 | tf_op jit(solution)/shard_map/weights/pallas_call | solution.py:32
  64.1 6.2 %all-to-all-start = ((bf16[8,416,128]{2,1,0:T(8,128)(2,1)}), bf16[8,416,128]{2,1,0:T(8,128)(2,1)S(1)}, u32[]{:S(2)}, u32[]{:S(2)}) async-start(bf16[8,416,128]{2,1,0:T(8,128)(2,1)} %weights.1), calls=%async_computation | async-start | bytes 1703936 | tf_op jit(solution)/shard_map/all_to_all | solution.py:397
  70.3 1.9 %collective-permute-start.21 = (bf16[320,128]{1,0:T(8,128)(2,1)}, bf16[320,128]{1,0:T(8,128)(2,1)S(1)}, u32[]{:S(2)}, u32[]{:S(2)}) collective-permute-start(bf16[320,128]{1,0:T(8,128)(2,1)} %get-tuple-element.60), channel_id=1, source_target_pairs={{0,8},{4,12},{8,0},{12,4},{16,24},{20,28},{24,16},{28,20},{1,9},{5... | collective-permute-start | bytes 245768 | tf_op jit(solution)/shard_map/ppermute | solution.py:305
  72.2 1.6 %collective-permute-start.22 = (bf16[320,128]{1,0:T(8,128)(2,1)}, bf16[320,128]{1,0:T(8,128)(2,1)S(1)}, u32[]{:S(2)}, u32[]{:S(2)}) collective-permute-start(bf16[320,128]{1,0:T(8,128)(2,1)} %get-tuple-element.61), channel_id=1, source_target_pairs={{0,12},{4,8},{8,4},{12,0},{16,28},{20,24},{24,20},{28,16},{1,13},{... | collective-permute-start | bytes 245768 | tf_op jit(solution)/shard_map/ppermute | solution.py:305
  74.9 3.2 %collective-permute-done.22.b3 = bf16[320,128]{1,0:T(8,128)(2,1)S(1)} collective-permute-done((bf16[320,128]{1,0:T(8,128)(2,1)}, bf16[320,128]{1,0:T(8,128)(2,1)S(1)}, u32[]{:S(2)}, u32[]{:S(2)}) %collective-permute-start.22) | collective-permute-done | bytes 81952 | tf_op jit(solution)/shard_map/ppermute | solution.py:305
  81.9 3.4 %all-to-all-done.got = bf16[8,416,128]{2,1,0:T(8,128)(2,1)S(1)} async-done(((bf16[8,416,128]{2,1,0:T(8,128)(2,1)}), bf16[8,416,128]{2,1,0:T(8,128)(2,1)S(1)}, u32[]{:S(2)}, u32[]{:S(2)}) %all-to-all-start) | async-done | bytes 852000 | tf_op jit(solution)/shard_map/all_to_all | solution.py:397
  86.0 5.3 %all-to-all-start.1 = ((bf16[8,80,128]{2,1,0:T(8,128)(2,1)}), bf16[8,80,128]{2,1,0:T(8,128)(2,1)S(1)}, u32[]{:S(2)}, u32[]{:S(2)}) async-start(bf16[8,80,128]{2,1,0:T(8,128)(2,1)} %middle.1), calls=%async_computation.1 | async-start | bytes 327680 | tf_op jit(solution)/shard_map/all_to_all | solution.py:413
  91.4 1.7 %collective-permute-start.23 = (bf16[656,128]{1,0:T(8,128)(2,1)S(1)}, bf16[656,128]{1,0:T(8,128)(2,1)S(1)}, u32[]{:S(2)}, u32[]{:S(2)}) collective-permute-start(bf16[656,128]{1,0:T(8,128)(2,1)S(1)} %get-tuple-element.73), channel_id=1, source_target_pairs={{0,1},{1,0},{2,3},{3,2},{4,5},{5,4},{6,7},{7,6},{8,9},{9,8},{10,11... | collective-permute-start | bytes 503816 | tf_op jit(solution)/shard_map/ppermute | solution.py:309
  93.3 1.6 %collective-permute-start.25 = (bf16[656,128]{1,0:T(8,128)(2,1)S(1)}, bf16[656,128]{1,0:T(8,128)(2,1)S(1)}, u32[]{:S(2)}, u32[]{:S(2)}) collective-permute-start(bf16[656,128]{1,0:T(8,128)(2,1)S(1)} %get-tuple-element.71), channel_id=1, source_target_pairs={{0,3},{1,2},{2,1},{3,0},{4,7},{5,6},{6,5},{7,4},{8,11},{9,10},{10,... | collective-permute-start | bytes 503816 | tf_op jit(solution)/shard_map/ppermute | solution.py:309
  94.9 1.6 %all-to-all-done.1.got = bf16[8,80,128]{2,1,0:T(8,128)(2,1)S(1)} async-done(((bf16[8,80,128]{2,1,0:T(8,128)(2,1)}), bf16[8,80,128]{2,1,0:T(8,128)(2,1)S(1)}, u32[]{:S(2)}, u32[]{:S(2)}) %all-to-all-start.1) | async-done | bytes 163872 | tf_op jit(solution)/shard_map/all_to_all | solution.py:413
  96.5 3.1 %collective-permute-start.26 = (f32[16,128]{1,0:T(8,128)S(1)}, f32[16,128]{1,0:T(8,128)S(1)}, u32[]{:S(2)}, u32[]{:S(2)}) collective-permute-start(f32[16,128]{1,0:T(8,128)S(1)} %tails.1.t0), channel_id=1, source_target_pairs={{0,1},{1,0},{2,3},{3,2},{4,5},{5,4},{6,7},{7,6},{8,9},{9,8},{10,11... | collective-permute-start | bytes 24584 | tf_op jit(solution)/shard_map/ppermute | solution.py:309
  99.8 1.5 %collective-permute-start.28 = (f32[16,128]{1,0:T(8,128)S(1)}, f32[16,128]{1,0:T(8,128)S(1)}, u32[]{:S(2)}, u32[]{:S(2)}) collective-permute-start(f32[16,128]{1,0:T(8,128)S(1)} %tails.1.t0), channel_id=1, source_target_pairs={{0,3},{1,2},{2,1},{3,0},{4,7},{5,6},{6,5},{7,4},{8,11},{9,10},{10,... | collective-permute-start | bytes 24584 | tf_op jit(solution)/shard_map/ppermute | solution.py:309
  101.3 1.6 %collective-permute-done.25.g3 = bf16[656,128]{1,0:T(8,128)(2,1)S(1)} collective-permute-done((bf16[656,128]{1,0:T(8,128)(2,1)S(1)}, bf16[656,128]{1,0:T(8,128)(2,1)S(1)}, u32[]{:S(2)}, u32[]{:S(2)}) %collective-permute-start.25) | collective-permute-done | bytes 167968 | tf_op jit(solution)/shard_map/ppermute | solution.py:309
  (78 shorter events, 19.5 us)
Async XLA Ops:
  2.9 14.2 %collective-permute-start.3 = (bf16[640,128]{1,0:T(8,128)(2,1)}, bf16[640,128]{1,0:T(8,128)(2,1)S(1)}, u32[]{:S(2)}, u32[]{:S(2)}) collective-permute-start(bf16[640,128]{1,0:T(8,128)(2,1)} %get-tuple-element.45), channel_id=1, source_target_pairs={{0,4},{4,0},{8,12},{12,8},{16,20},{20,16},{24,28},{28,24},{1,5},{5... | collective-permute-start | bytes 491528 | tf_op jit(solution)/shard_map/ppermute | solution.py:305
  5.4 11.6 %collective-permute-start.4 = (bf16[640,128]{1,0:T(8,128)(2,1)}, bf16[640,128]{1,0:T(8,128)(2,1)S(1)}, u32[]{:S(2)}, u32[]{:S(2)}) collective-permute-start(bf16[640,128]{1,0:T(8,128)(2,1)} %get-tuple-element.45), channel_id=1, source_target_pairs={{0,12},{4,8},{8,4},{12,0},{16,28},{20,24},{24,20},{28,16},{1,13},{... | collective-permute-start | bytes 491528 | tf_op jit(solution)/shard_map/ppermute | solution.py:305
  8.2 6.0 %collective-permute-start = (bf16[320,128]{1,0:T(8,128)(2,1)}, bf16[320,128]{1,0:T(8,128)(2,1)S(1)}, u32[]{:S(2)}, u32[]{:S(2)}) collective-permute-start(bf16[320,128]{1,0:T(8,128)(2,1)} %bitcast.32), channel_id=1, source_target_pairs={{0,1},{1,0},{2,3},{3,2},{4,5},{5,4},{6,7},{7,6},{8,9},{9,8},{10,11... | collective-permute-start | bytes 245768 | tf_op jit(solution)/shard_map/ppermute | solution.py:309
  9.2 5.1 %collective-permute-start.1 = (bf16[320,128]{1,0:T(8,128)(2,1)}, bf16[320,128]{1,0:T(8,128)(2,1)S(1)}, u32[]{:S(2)}, u32[]{:S(2)}) collective-permute-start(bf16[320,128]{1,0:T(8,128)(2,1)} %bitcast.33), channel_id=1, source_target_pairs={{0,2},{1,3},{2,0},{3,1},{4,6},{5,7},{6,4},{7,5},{8,10},{9,11},{10,... | collective-permute-start | bytes 245768 | tf_op jit(solution)/shard_map/ppermute | solution.py:309
  10.4 5.2 %collective-permute-start.2 = (bf16[320,128]{1,0:T(8,128)(2,1)}, bf16[320,128]{1,0:T(8,128)(2,1)S(1)}, u32[]{:S(2)}, u32[]{:S(2)}) collective-permute-start(bf16[320,128]{1,0:T(8,128)(2,1)} %bitcast.34), channel_id=1, source_target_pairs={{0,3},{1,2},{2,1},{3,0},{4,7},{5,6},{6,5},{7,4},{8,11},{9,10},{10,... | collective-permute-start | bytes 245768 | tf_op jit(solution)/shard_map/ppermute | solution.py:309
  17.1 29.2 %collective-permute-start.14 = (bf16[1920,128]{1,0:T(8,128)(2,1)S(1)}, bf16[1920,128]{1,0:T(8,128)(2,1)S(1)}, u32[]{:S(2)}, u32[]{:S(2)}) collective-permute-start(bf16[1920,128]{1,0:T(8,128)(2,1)S(1)} %constant_dynamic-update-slice_fusion.refs_0_), channel_id=1, source_target_pairs={{0,2},{1,3},{2,0},{3,1},{4,6},{5,7},{6,4},{7,5},{8,10},{9,11},{10,... | collective-permute-start | bytes 1474568 | tf_op jit(solution)/shard_map/ppermute | solution.py:309
  18.4 9.2 %collective-permute-start.6 = (bf16[336,128]{1,0:T(8,128)(2,1)S(1)}, bf16[336,128]{1,0:T(8,128)(2,1)S(1)}, u32[]{:S(2)}, u32[]{:S(2)}) collective-permute-start(bf16[336,128]{1,0:T(8,128)(2,1)S(1)} %get-tuple-element.46.r0), channel_id=1, source_target_pairs={{0,16},{4,20},{8,24},{12,28},{16,0},{20,4},{24,8},{28,12},{1,17},{... | collective-permute-start | bytes 258056 | tf_op jit(solution)/shard_map/ppermute | solution.py:305
  23.5 9.3 %collective-permute-start.7 = (bf16[336,128]{1,0:T(8,128)(2,1)S(1)}, bf16[336,128]{1,0:T(8,128)(2,1)S(1)}, u32[]{:S(2)}, u32[]{:S(2)}) collective-permute-start(bf16[336,128]{1,0:T(8,128)(2,1)S(1)} %get-tuple-element.47), channel_id=1, source_target_pairs={{0,20},{4,16},{8,28},{12,24},{16,4},{20,0},{24,12},{28,8},{1,21},{... | collective-permute-start | bytes 258056 | tf_op jit(solution)/shard_map/ppermute | solution.py:305
  23.5 12.5 %collective-permute-start.8 = (bf16[336,128]{1,0:T(8,128)(2,1)S(1)}, bf16[336,128]{1,0:T(8,128)(2,1)S(1)}, u32[]{:S(2)}, u32[]{:S(2)}) collective-permute-start(bf16[336,128]{1,0:T(8,128)(2,1)S(1)} %get-tuple-element.48), channel_id=1, source_target_pairs={{0,24},{4,28},{8,16},{12,20},{16,8},{20,12},{24,0},{28,4},{1,25},{... | collective-permute-start | bytes 258056 | tf_op jit(solution)/shard_map/ppermute | solution.py:305
  27.5 10.5 %collective-permute-start.9 = (bf16[336,128]{1,0:T(8,128)(2,1)S(1)}, bf16[336,128]{1,0:T(8,128)(2,1)S(1)}, u32[]{:S(2)}, u32[]{:S(2)}) collective-permute-start(bf16[336,128]{1,0:T(8,128)(2,1)S(1)} %get-tuple-element.49), channel_id=1, source_target_pairs={{0,28},{4,24},{8,20},{12,16},{16,12},{20,8},{24,4},{28,0},{1,29},{... | collective-permute-start | bytes 258056 | tf_op jit(solution)/shard_map/ppermute | solution.py:305
  27.6 10.5 %collective-permute-start.10 = (bf16[336,128]{1,0:T(8,128)(2,1)S(1)}, bf16[336,128]{1,0:T(8,128)(2,1)S(1)}, u32[]{:S(2)}, u32[]{:S(2)}) collective-permute-start(bf16[336,128]{1,0:T(8,128)(2,1)S(1)} %get-tuple-element.48), channel_id=1, source_target_pairs={{0,8},{4,12},{8,0},{12,4},{16,24},{20,28},{24,16},{28,20},{1,9},{5... | collective-permute-start | bytes 258056 | tf_op jit(solution)/shard_map/ppermute | solution.py:305
  32.8 7.6 %collective-permute-start.11 = (bf16[336,128]{1,0:T(8,128)(2,1)S(1)}, bf16[336,128]{1,0:T(8,128)(2,1)S(1)}, u32[]{:S(2)}, u32[]{:S(2)}) collective-permute-start(bf16[336,128]{1,0:T(8,128)(2,1)S(1)} %get-tuple-element.49), channel_id=1, source_target_pairs={{0,12},{4,8},{8,4},{12,0},{16,28},{20,24},{24,20},{28,16},{1,13},{... | collective-permute-start | bytes 258056 | tf_op jit(solution)/shard_map/ppermute | solution.py:305
  36.0 10.3 %collective-permute-start.16 = (bf16[640,128]{1,0:T(8,128)(2,1)S(1)}, bf16[640,128]{1,0:T(8,128)(2,1)S(1)}, u32[]{:S(2)}, u32[]{:S(2)}) collective-permute-start(bf16[640,128]{1,0:T(8,128)(2,1)S(1)} %collective-permute-done.4), channel_id=1, source_target_pairs={{0,4},{4,0},{8,12},{12,8},{16,20},{20,16},{24,28},{28,24},{1,5},{5... | collective-permute-start | bytes 491528 | tf_op jit(solution)/shard_map/ppermute | solution.py:305
  40.4 15.0 %collective-permute-start.12 = (bf16[3,336,128]{2,1,0:T(8,128)(2,1)S(1)}, bf16[3,336,128]{2,1,0:T(8,128)(2,1)S(1)}, u32[]{:S(2)}, u32[]{:S(2)}) collective-permute-start(bf16[3,336,128]{2,1,0:T(8,128)(2,1)S(1)} %near.1), channel_id=1, source_target_pairs={{0,32},{4,36},{8,40},{12,44},{32,64},{36,68},{40,72},{44,76},{48,1... | collective-permute-start | bytes 774152 | tf_op jit(solution)/shard_map/ppermute | solution.py:318
  44.7 15.5 %collective-permute-start.13 = (bf16[1920,128]{1,0:T(8,128)(2,1)S(1)}, bf16[1920,128]{1,0:T(8,128)(2,1)S(1)}, u32[]{:S(2)}, u32[]{:S(2)}) collective-permute-start(bf16[1920,128]{1,0:T(8,128)(2,1)S(1)} %constant_dynamic-update-slice_fusion.refs_0_), channel_id=1, source_target_pairs={{0,1},{1,0},{2,3},{3,2},{4,5},{5,4},{6,7},{7,6},{8,9},{9,8},{10,11... | collective-permute-start | bytes 1474568 | tf_op jit(solution)/shard_map/ppermute | solution.py:309
  46.3 13.9 %collective-permute-start.15 = (bf16[1920,128]{1,0:T(8,128)(2,1)S(1)}, bf16[1920,128]{1,0:T(8,128)(2,1)S(1)}, u32[]{:S(2)}, u32[]{:S(2)}) collective-permute-start(bf16[1920,128]{1,0:T(8,128)(2,1)S(1)} %collective-permute-done.14.refs_2_), channel_id=1, source_target_pairs={{0,1},{1,0},{2,3},{3,2},{4,5},{5,4},{6,7},{7,6},{8,9},{9,8},{10,11... | collective-permute-start | bytes 1474568 | tf_op jit(solution)/shard_map/ppermute | solution.py:309
  46.4 6.9 %collective-permute-start.18 = (bf16[640,128]{1,0:T(8,128)(2,1)S(1)}, bf16[640,128]{1,0:T(8,128)(2,1)S(1)}, u32[]{:S(2)}, u32[]{:S(2)}) collective-permute-start(bf16[640,128]{1,0:T(8,128)(2,1)S(1)} %collective-permute-done.16.refs_4_), channel_id=1, source_target_pairs={{0,2},{1,3},{2,0},{3,1},{4,6},{5,7},{6,4},{7,5},{8,10},{9,11},{10,... | collective-permute-start | bytes 491528 | tf_op jit(solution)/shard_map/ppermute | solution.py:309
  46.4 3.4 %collective-permute-start.5 = (bf16[336,128]{1,0:T(8,128)(2,1)S(1)}, bf16[336,128]{1,0:T(8,128)(2,1)S(1)}, u32[]{:S(2)}, u32[]{:S(2)}) collective-permute-start(bf16[336,128]{1,0:T(8,128)(2,1)S(1)} %get-tuple-element.47), channel_id=1, source_target_pairs={{0,4},{4,0},{8,12},{12,8},{16,20},{20,16},{24,28},{28,24},{1,5},{5... | collective-permute-start | bytes 258056 | tf_op jit(solution)/shard_map/ppermute | solution.py:305
  49.8 10.4 %collective-permute-start.17 = (bf16[640,128]{1,0:T(8,128)(2,1)S(1)}, bf16[640,128]{1,0:T(8,128)(2,1)S(1)}, u32[]{:S(2)}, u32[]{:S(2)}) collective-permute-start(bf16[640,128]{1,0:T(8,128)(2,1)S(1)} %collective-permute-done.16.refs_4_), channel_id=1, source_target_pairs={{0,1},{1,0},{2,3},{3,2},{4,5},{5,4},{6,7},{7,6},{8,9},{9,8},{10,11... | collective-permute-start | bytes 491528 | tf_op jit(solution)/shard_map/ppermute | solution.py:309
  53.2 7.0 %collective-permute-start.19 = (bf16[640,128]{1,0:T(8,128)(2,1)S(1)}, bf16[640,128]{1,0:T(8,128)(2,1)S(1)}, u32[]{:S(2)}, u32[]{:S(2)}) collective-permute-start(bf16[640,128]{1,0:T(8,128)(2,1)S(1)} %collective-permute-done.18.refs_6_), channel_id=1, source_target_pairs={{0,1},{1,0},{2,3},{3,2},{4,5},{5,4},{6,7},{7,6},{8,9},{9,8},{10,11... | collective-permute-start | bytes 491528 | tf_op jit(solution)/shard_map/ppermute | solution.py:309
  64.1 21.1 %all-to-all-start = ((bf16[8,416,128]{2,1,0:T(8,128)(2,1)}), bf16[8,416,128]{2,1,0:T(8,128)(2,1)S(1)}, u32[]{:S(2)}, u32[]{:S(2)}) async-start(bf16[8,416,128]{2,1,0:T(8,128)(2,1)} %weights.1), calls=%async_computation | async-start | bytes 1703936 | tf_op jit(solution)/shard_map/all_to_all | solution.py:397
  70.3 4.0 %collective-permute-start.20 = (bf16[320,128]{1,0:T(8,128)(2,1)}, bf16[320,128]{1,0:T(8,128)(2,1)S(1)}, u32[]{:S(2)}, u32[]{:S(2)}) collective-permute-start(bf16[320,128]{1,0:T(8,128)(2,1)} %get-tuple-element.59), channel_id=1, source_target_pairs={{0,4},{4,0},{8,12},{12,8},{16,20},{20,16},{24,28},{28,24},{1,5},{5... | collective-permute-start | bytes 245768 | tf_op jit(solution)/shard_map/ppermute | solution.py:305
  70.3 4.6 %collective-permute-start.21 = (bf16[320,128]{1,0:T(8,128)(2,1)}, bf16[320,128]{1,0:T(8,128)(2,1)S(1)}, u32[]{:S(2)}, u32[]{:S(2)}) collective-permute-start(bf16[320,128]{1,0:T(8,128)(2,1)} %get-tuple-element.60), channel_id=1, source_target_pairs={{0,8},{4,12},{8,0},{12,4},{16,24},{20,28},{24,16},{28,20},{1,9},{5... | collective-permute-start | bytes 245768 | tf_op jit(solution)/shard_map/ppermute | solution.py:305
  72.2 5.9 %collective-permute-start.22 = (bf16[320,128]{1,0:T(8,128)(2,1)}, bf16[320,128]{1,0:T(8,128)(2,1)S(1)}, u32[]{:S(2)}, u32[]{:S(2)}) collective-permute-start(bf16[320,128]{1,0:T(8,128)(2,1)} %get-tuple-element.61), channel_id=1, source_target_pairs={{0,12},{4,8},{8,4},{12,0},{16,28},{20,24},{24,20},{28,16},{1,13},{... | collective-permute-start | bytes 245768 | tf_op jit(solution)/shard_map/ppermute | solution.py:305
  81.9 21.1 %copy-start.12 = (f32[8,128]{1,0:T(8,128)S(1)}, f32[8,128]{1,0:T(8,128)}, u32[]{:S(2)}) copy-start(f32[8,128]{1,0:T(8,128)} %get-tuple-element.65.inv) | copy-start | bytes 12292
  86.0 10.4 %all-to-all-start.1 = ((bf16[8,80,128]{2,1,0:T(8,128)(2,1)}), bf16[8,80,128]{2,1,0:T(8,128)(2,1)S(1)}, u32[]{:S(2)}, u32[]{:S(2)}) async-start(bf16[8,80,128]{2,1,0:T(8,128)(2,1)} %middle.1), calls=%async_computation.1 | async-start | bytes 327680 | tf_op jit(solution)/shard_map/all_to_all | solution.py:413
  91.4 8.4 %collective-permute-start.23 = (bf16[656,128]{1,0:T(8,128)(2,1)S(1)}, bf16[656,128]{1,0:T(8,128)(2,1)S(1)}, u32[]{:S(2)}, u32[]{:S(2)}) collective-permute-start(bf16[656,128]{1,0:T(8,128)(2,1)S(1)} %get-tuple-element.73), channel_id=1, source_target_pairs={{0,1},{1,0},{2,3},{3,2},{4,5},{5,4},{6,7},{7,6},{8,9},{9,8},{10,11... | collective-permute-start | bytes 503816 | tf_op jit(solution)/shard_map/ppermute | solution.py:309
  93.1 8.2 %collective-permute-start.24 = (bf16[656,128]{1,0:T(8,128)(2,1)S(1)}, bf16[656,128]{1,0:T(8,128)(2,1)S(1)}, u32[]{:S(2)}, u32[]{:S(2)}) collective-permute-start(bf16[656,128]{1,0:T(8,128)(2,1)S(1)} %get-tuple-element.72), channel_id=1, source_target_pairs={{0,2},{1,3},{2,0},{3,1},{4,6},{5,7},{6,4},{7,5},{8,10},{9,11},{10,... | collective-permute-start | bytes 503816 | tf_op jit(solution)/shard_map/ppermute | solution.py:309
  93.3 9.6 %collective-permute-start.25 = (bf16[656,128]{1,0:T(8,128)(2,1)S(1)}, bf16[656,128]{1,0:T(8,128)(2,1)S(1)}, u32[]{:S(2)}, u32[]{:S(2)}) collective-permute-start(bf16[656,128]{1,0:T(8,128)(2,1)S(1)} %get-tuple-element.71), channel_id=1, source_target_pairs={{0,3},{1,2},{2,1},{3,0},{4,7},{5,6},{6,5},{7,4},{8,11},{9,10},{10,... | collective-permute-start | bytes 503816 | tf_op jit(solution)/shard_map/ppermute | solution.py:309
  96.5 8.0 %collective-permute-start.26 = (f32[16,128]{1,0:T(8,128)S(1)}, f32[16,128]{1,0:T(8,128)S(1)}, u32[]{:S(2)}, u32[]{:S(2)}) collective-permute-start(f32[16,128]{1,0:T(8,128)S(1)} %tails.1.t0), channel_id=1, source_target_pairs={{0,1},{1,0},{2,3},{3,2},{4,5},{5,4},{6,7},{7,6},{8,9},{9,8},{10,11... | collective-permute-start | bytes 24584 | tf_op jit(solution)/shard_map/ppermute | solution.py:309
  99.6 4.9 %collective-permute-start.27 = (f32[16,128]{1,0:T(8,128)S(1)}, f32[16,128]{1,0:T(8,128)S(1)}, u32[]{:S(2)}, u32[]{:S(2)}) collective-permute-start(f32[16,128]{1,0:T(8,128)S(1)} %tails.1.t0), channel_id=1, source_target_pairs={{0,2},{1,3},{2,0},{3,1},{4,6},{5,7},{6,4},{7,5},{8,10},{9,11},{10,... | collective-permute-start | bytes 24584 | tf_op jit(solution)/shard_map/ppermute | solution.py:309
  99.8 4.7 %collective-permute-start.28 = (f32[16,128]{1,0:T(8,128)S(1)}, f32[16,128]{1,0:T(8,128)S(1)}, u32[]{:S(2)}, u32[]{:S(2)}) collective-permute-start(f32[16,128]{1,0:T(8,128)S(1)} %tails.1.t0), channel_id=1, source_target_pairs={{0,3},{1,2},{2,1},{3,0},{4,7},{5,6},{6,5},{7,4},{8,11},{9,10},{10,... | collective-permute-start | bytes 24584 | tf_op jit(solution)/shard_map/ppermute | solution.py:309
  (14 other events, 98.8 us)
